TPU v7x, 256 devices: a whole 4x4x8 slice. The times are simulated.
256 devices in a mesh: cp: 64 (over z_hi, x, y), blk: 4 (over z_lo, core).
Axes of the slice: x: 4, y: 4, z: 8 (z_hi: 4, z_lo: 2; z = z_hi * 2 + z_lo), core: 2. Of those that a mesh axis runs over, the one named last changes fastest.
Arguments:
- queries: bfloat16 [16384, 3072], P(('cp', 'blk')), may hold values from -8 to 8
- key_vectors: bfloat16 [16384, 512], P(('cp', 'blk')), may hold values from -8 to 8
- value_vectors: bfloat16 [16384, 512], P(('cp', 'blk')), may hold values from -6 to 6
- segment_lengths: int32 [16], replicated, may hold values from 1 to 2048, 16384 in all
- segment_allowed: int32 [16, 16], replicated, may hold values from 0 to 1, as said below
- noise_level: int32 [16], replicated, may hold values from 0 to 15
- gate_table: bfloat16 [16, 3072], P(None, 'blk'), may hold values from 0.099609375 to 1.8984375
Outputs:
- attended: bfloat16 [16384, 3072], P(('cp', 'blk'))
Inputs may be any that keep to these rules, and one draw needn't show every extreme that they name: `segment_lengths`: the longest segment has exactly 2048 tokens. segment_allowed[a, b] is 0 for b > a, 1 for b = a and for b = 0, either value otherwise.
All inputs are finite; a program needn't handle non-finite values.
Results may differ from a plain program's by a relative error of at most 0.0055.
Values may be sent and summed in bfloat16 or wider, within the bound.
No kernel may reach another device: no remote copies, remote signals or barrier semaphores. Data moves between devices by JAX's collectives and lax.ppermute only.
A program may use at most 64 MiB of HBM per device.

v0:
```python
import math

import jax
import jax.numpy as jnp
from jax import lax
from jax.sharding import PartitionSpec as P

HEADS = 24
KV_HEADS = 4
HEAD_DIM = 128


NEGATIVE = -1e30


def segment_table(positions, segment_ends):
    counts = jnp.sum((segment_ends[None, :] <= positions[:, None]).astype(jnp.int32), axis=1)
    labels = jnp.arange(segment_ends.shape[0], dtype=jnp.int32)
    return (counts[:, None] == labels[None, :]).astype(jnp.float32)


def attend_block(current, query_heads, query_reach, key_block, value_block, key_table):
    running, totals, mixed_sum = current
    visible = jnp.dot(query_reach, key_table.T, precision=lax.Precision.HIGHEST) > 0.5
    kv_count = query_heads.shape[1]
    block_width = key_block.shape[0]
    key_heads = key_block.reshape(block_width, kv_count, HEAD_DIM)
    value_heads = value_block.reshape(block_width, kv_count, HEAD_DIM)
    scores = jnp.einsum(
        "rgqd,kgd->gqrk", query_heads, key_heads, preferred_element_type=jnp.float32
    ) * (1.0 / math.sqrt(HEAD_DIM))
    scores = jnp.where(visible, scores, NEGATIVE)
    updated = jnp.maximum(running, jnp.max(scores, axis=-1))
    factor = jnp.exp(running - updated)
    weights = jnp.where(visible, jnp.exp(scores - updated[..., None]), 0.0)
    totals = totals * factor + jnp.sum(weights, axis=-1)
    mixed_sum = mixed_sum * factor[..., None] + jnp.einsum(
        "gqrk,kgd->gqrd",
        weights.astype(jnp.bfloat16),
        value_heads,
        preferred_element_type=jnp.float32,
    )
    return (updated, totals, mixed_sum)


def fold_keys(
    current, pieces, query_heads, query_reach, query_present, allowed, segment_ends, key_place
):
    key_piece, value_piece = pieces
    length = key_piece.shape[0]
    block_width = math.gcd(length, 512)
    key_table = segment_table(key_place(jnp.arange(length, dtype=jnp.int32)), segment_ends)
    present = jnp.max(key_table, axis=0)
    reach_any = (
        jnp.dot(
            jnp.dot(query_present, allowed, precision=lax.Precision.HIGHEST),
            present,
            precision=lax.Precision.HIGHEST,
        )
        > 0.5
    )

    def run_blocks(outer_state):

        def one_step(step_index, inner_state):
            offset = step_index * block_width
            return attend_block(
                inner_state,
                query_heads,
                query_reach,
                lax.dynamic_slice_in_dim(key_piece, offset, block_width, 0),
                lax.dynamic_slice_in_dim(value_piece, offset, block_width, 0),
                lax.dynamic_slice_in_dim(key_table, offset, block_width, 0),
            )

        return lax.fori_loop(0, length // block_width, one_step, outer_state)

    return lax.cond(reach_any, run_blocks, lambda outer_state: outer_state, current)


def per_device(
    queries, key_vectors, value_vectors, segment_lengths, segment_allowed, noise_level, gate_table
):
    cp_count = lax.axis_size("cp")
    cp_index = lax.axis_index("cp")
    segment_ends = jnp.cumsum(segment_lengths)
    allowed = segment_allowed.astype(jnp.float32)
    level_table = (
        noise_level[:, None] == jnp.arange(gate_table.shape[0], dtype=jnp.int32)[None, :]
    ).astype(jnp.float32)
    queries, key_vectors, value_vectors = (
        lax.all_to_all(queries, "blk", split_axis=1, concat_axis=0, tiled=True),
        lax.all_to_all(key_vectors, "blk", split_axis=1, concat_axis=0, tiled=True),
        lax.all_to_all(value_vectors, "blk", split_axis=1, concat_axis=0, tiled=True),
    )
    row_count = queries.shape[0]

    def key_place(position_index):
        return position_index

    local_rows = jnp.arange(row_count, dtype=jnp.int32)
    queries = lax.all_to_all(queries, "cp", split_axis=0, concat_axis=0, tiled=True)
    piece_rows = row_count // cp_count
    query_place = (
        local_rows // piece_rows * row_count + cp_index * piece_rows + local_rows % piece_rows
    )
    head_count = queries.shape[1] // HEAD_DIM
    group_size = HEADS // KV_HEADS
    kv_count = head_count // group_size
    query_heads = queries.reshape(row_count, kv_count, group_size, HEAD_DIM)
    query_table = segment_table(query_place, segment_ends)
    query_reach = jnp.dot(query_table, allowed, precision=lax.Precision.HIGHEST)
    query_present = jnp.max(query_table, axis=0)
    start_state = (
        jnp.full((kv_count, group_size, row_count), NEGATIVE, jnp.float32),
        jnp.zeros((kv_count, group_size, row_count), jnp.float32),
        jnp.zeros((kv_count, group_size, row_count, HEAD_DIM), jnp.float32),
    )
    final_state = fold_keys(
        start_state,
        (
            lax.all_gather(key_vectors, "cp", axis=0, tiled=True),
            lax.all_gather(value_vectors, "cp", axis=0, tiled=True),
        ),
        query_heads,
        query_reach,
        query_present,
        allowed,
        segment_ends,
        key_place,
    )
    running, totals, mixed_sum = final_state
    normalized = mixed_sum / totals[..., None]
    normalized = jnp.transpose(normalized, (2, 0, 1, 3)).reshape(row_count, head_count * HEAD_DIM)
    row_levels = jnp.dot(query_table, level_table, precision=lax.Precision.HIGHEST).astype(
        jnp.bfloat16
    )
    row_gate = jnp.dot(row_levels, gate_table, preferred_element_type=jnp.float32)
    attended = (normalized * row_gate).astype(jnp.bfloat16)
    attended = lax.all_to_all(attended, "cp", split_axis=0, concat_axis=0, tiled=True)
    return lax.all_to_all(attended, "blk", split_axis=0, concat_axis=1, tiled=True)


def solution(mesh):
    in_specs = (
        P(("cp", "blk"), None),
        P(("cp", "blk"), None),
        P(("cp", "blk"), None),
        P(),
        P(),
        P(),
        P(None, "blk"),
    )
    out_specs = P(("cp", "blk"), None)
    return jax.shard_map(
        per_device, mesh=mesh, in_specs=in_specs, out_specs=out_specs, check_vma=False
    )
```

profile of v0, /device:TPU:6, one launch (start us, length us, event | category | flops | bytes accessed | tf_op | source)
XLA Modules:
  0.0 516.9 jit_solution(2957245746683546686)
XLA Ops:
  7.4 7.2 %all_to_all.91 = bf16[64,4,128]{2,0,1:T(8,128)(2,1)} all-to-all(bf16[64,4,128]{2,0,1:T(8,128)(2,1)S(1)} %copy_bitcast_fusion.2), channel_id=1, replica_groups=mesh['cp'=64,'blk'=4] {'blk'}, dimensions={1} | all-to-all | bytes 131072 | tf_op jit(solution)/shard_map/all_to_all | solution.py:93
  15.5 7.2 %all_to_all.92 = bf16[64,4,128]{2,0,1:T(8,128)(2,1)} all-to-all(bf16[64,4,128]{2,0,1:T(8,128)(2,1)S(1)} %copy_bitcast_fusion.1), channel_id=1, replica_groups=mesh['cp'=64,'blk'=4] {'blk'}, dimensions={1} | all-to-all | bytes 131072 | tf_op jit(solution)/shard_map/all_to_all | solution.py:94
  22.7 1.8 copy.62
  24.5 3.5 all-to-all-start
  30.4 5.4 %all-to-all-done = bf16[64,4,768]{2,0,1:T(8,128)(2,1)S(1)} async-done(((bf16[64,4,768]{2,0,1:T(8,128)(2,1)}), bf16[64,4,768]{2,0,1:T(8,128)(2,1)S(1)}, u32[]{:S(2)}, u32[]{:S(2)}) %all-to-all-start) | async-done | bytes 393248 | tf_op jit(solution)/shard_map/all_to_all | solution.py:92
  36.7 14.9 %all-to-all-start.1 = ((bf16[64,4,768]{2,1,0:T(4,128)(2,1)}), bf16[64,4,768]{2,1,0:T(4,128)(2,1)S(1)}, u32[]{:S(2)}, u32[]{:S(2)}) async-start(bf16[64,4,768]{2,1,0:T(4,128)(2,1)} %all_to_all.69), calls=%async_computation.1 | async-start | bytes 786432 | tf_op jit(solution)/shard_map/all_to_all | solution.py:102
  54.0 14.5 %all-to-all-done.1 = bf16[64,4,768]{2,1,0:T(4,128)(2,1)S(1)} async-done(((bf16[64,4,768]{2,1,0:T(4,128)(2,1)}), bf16[64,4,768]{2,1,0:T(4,128)(2,1)S(1)}, u32[]{:S(2)}, u32[]{:S(2)}) %all-to-all-start.1) | async-done | bytes 393248 | tf_op jit(solution)/shard_map/all_to_all | solution.py:102
  68.5 41.8 %all-gather.3.cloned.1.call-done = bf16[16384,128]{1,0:T(8,128)(2,1)} async-done(((bf16[256,128]{1,0:T(8,128)(2,1)}), bf16[16384,128]{1,0:T(8,128)(2,1)}) %all-gather.3.cloned.1.call-update) | async-done | bytes 4194320 | tf_op jit(solution)/shard_map/all_gather | solution.py:122
  110.3 90.9 %all-gather.5.cloned.1.call-done = bf16[16384,128]{1,0:T(8,128)(2,1)} async-done(((bf16[256,128]{1,0:T(8,128)(2,1)}), bf16[16384,128]{1,0:T(8,128)(2,1)}) %all-gather.5.cloned.1.call-update) | async-done | bytes 4194320 | tf_op jit(solution)/shard_map/all_gather | solution.py:123
  201.2 271.5 %conditional.1 = (f32[1,6,256]{2,1,0:T(8,128)}, f32[1,6,256,128]{2,3,1,0:T(8,128)}) conditional(s32[]{:T(128)} %convert_element_type.37, () %tuple.27, (bf16[64,4,768]{2,1,0:T(4,128)(2,1)S(1)}, f32[16384,16]{0,1:T(8,128)}, f32[256,16]{0,1:T(8,128)S(1)}, bf16[16384,128]{1,0:T(8,128)(2,1)}, bf16[16384,128]{1,0:T(8,128)(2,1)}) %tuple.28), branch_computations={%region_5.6_spmd, %region_6.11_spmd} | conditional | flops 438772736 | bytes 15483203 | solution.py:78
  202.2 268.2 %while.17 = (s32[]{:T(128)}, f32[1,6,256]{2,1,0:T(8,128)S(1)}, f32[1,6,256]{2,1,0:T(8,128)}, f32[1,6,256,128]{3,2,1,0:T(8,128)}, f32[16384,16]{0,1:T(8,128)}, /*...) while((s32[]{:T(128)}, f32[1,6,256]{2,1,0:T(8,128)S(1)}, ...), condition=%wide.region_10.10_spmd.clone, body=%wide.region_7.9_spmd.clone.sunk | while | flops 438772736 | bytes 12337347 | solution.py:76
  203.6 1.7 fusion.64
  205.3 2.9 fusion.67
  211.0 1.7 fusion.64
  212.7 3.2 fusion.67
  219.4 1.7 fusion.64
  221.1 3.2 fusion.67
  227.8 1.7 fusion.64
  229.5 3.2 fusion.67
  236.2 1.7 fusion.64
  238.0 3.2 fusion.67
  244.6 1.7 fusion.64
  246.4 3.2 fusion.67
  253.1 1.7 fusion.64
  254.8 3.2 fusion.67
  261.5 1.7 fusion.64
  263.2 3.2 fusion.67
  269.9 1.7 fusion.64
  271.6 3.2 fusion.67
  278.3 1.7 fusion.64
  280.0 3.2 fusion.67
  288.4 3.2 fusion.67
  296.9 3.2 fusion.67
  303.5 1.7 fusion.64
  305.3 3.2 fusion.67
  313.7 3.2 fusion.67
  320.4 1.7 fusion.64
  322.1 3.2 fusion.67
  330.5 3.2 fusion.67
  338.9 3.2 fusion.67
  347.3 3.2 fusion.67
  355.7 3.2 fusion.67
  362.4 1.7 fusion.64
  364.2 3.2 fusion.67
  372.6 3.2 fusion.67
  379.2 1.7 fusion.64
  381.0 3.2 fusion.67
  389.4 3.2 fusion.67
  397.8 3.2 fusion.67
  404.5 1.7 fusion.64
  406.2 3.2 fusion.67
  414.6 3.2 fusion.67
  421.3 1.7 fusion.64
  423.0 3.2 fusion.67
  431.5 3.2 fusion.67
  438.1 1.7 fusion.64
  439.9 3.2 fusion.67
  448.3 3.2 fusion.67
  456.7 3.2 fusion.67
  463.4 1.7 fusion.64
  465.1 3.2 fusion.67
  470.4 2.3 copy.54
  474.6 24.3 %all_to_all.93 = bf16[64,4,768]{2,1,0:T(4,128)(2,1)S(1)} all-to-all(bf16[64,4,768]{2,1,0:T(4,128)(2,1)S(1)} %all_to_all.79), channel_id=1, replica_groups=mesh['cp'=64,'blk'=4] {'cp'}, dimensions={0} | all-to-all | bytes 786432 | tf_op jit(solution)/shard_map/all_to_all | solution.py:140
  499.0 10.3 %all_to_all.94 = bf16[4,64,768]{2,1,0:T(8,128)(2,1)S(1)} all-to-all(bf16[4,64,768]{2,1,0:T(8,128)(2,1)S(1)} %all_to_all.81), channel_id=1, replica_groups=mesh['cp'=64,'blk'=4] {'blk'}, dimensions={0} | all-to-all | bytes 786432 | tf_op jit(solution)/shard_map/all_to_all | solution.py:141
  (212 shorter events, 144.8 us)
Async XLA Ops:
  6.5 0.8 copy-start
  6.5 45.4 %copy-start.2 = (s32[16,16]{1,0:T(8,128)S(1)}, s32[16,16]{1,0:T(8,128)}, u32[]{:S(2)}) copy-start(s32[16,16]{1,0:T(8,128)} %param.15) | copy-start | bytes 3076
  6.5 47.0 %copy-start.3 = (s32[16]{0:T(128)S(1)}, s32[16]{0:T(128)}, u32[]{:S(2)}) copy-start(s32[16]{0:T(128)} %param.16) | copy-start | bytes 196
  6.5 103.8 %all-gather.3.cloned.1.call-start = ((), (), s32[]{:S(2)}) async-start(), calls=%async_computation.6 | async-start | bytes 4259840 | tf_op jit(solution)/shard_map/all_gather | solution.py:122
  14.6 186.6 %all-gather.5.cloned.1.call-start = ((), (), s32[]{:S(2)}) async-start(), calls=%async_computation.7 | async-start | bytes 4259840 | tf_op jit(solution)/shard_map/all_gather | solution.py:123
  24.5 11.3 %all-to-all-start = ((bf16[64,4,768]{2,0,1:T(8,128)(2,1)}), bf16[64,4,768]{2,0,1:T(8,128)(2,1)S(1)}, u32[]{:S(2)}, u32[]{:S(2)}) async-start(bf16[64,4,768]{2,0,1:T(8,128)(2,1)} %bitcast.93), calls=%async_computation | async-start | bytes 786432 | tf_op jit(solution)/shard_map/all_to_all | solution.py:92
  36.7 31.8 %all-to-all-start.1 = ((bf16[64,4,768]{2,1,0:T(4,128)(2,1)}), bf16[64,4,768]{2,1,0:T(4,128)(2,1)S(1)}, u32[]{:S(2)}, u32[]{:S(2)}) async-start(bf16[64,4,768]{2,1,0:T(4,128)(2,1)} %all_to_all.69), calls=%async_computation.1 | async-start | bytes 786432 | tf_op jit(solution)/shard_map/all_to_all | solution.py:102
  472.7 1.5 copy-start.1
Sparse Core Ops, SparseCore 0:
  14.8 95.5 all-gather.2
  113.6 87.5 all-gather.4
where the time goes:
time: 526 us; the launch traced here: 517 us
  matrix products  202 us (38%)
  waiting for transfers between devices  153 us (29%)
  other arithmetic  69.8 us (13%)
  blocking collectives  48.9 us (9%)
  starting transfers between devices  18.4 us (3%)
  between operations  14.2 us (3%)
  local copies, waits for them, and re-layouts  9.61 us (2%)
    dot_general x32, matrix products, attend_block(): jnp.einsum('gqrk,kgd->gqrd', weights.astype(jnp.bfloat16), value_heads, p...  102 us
    all_gather x1, waiting for transfers between devices, per_device(): lax.all_gather(value_vectors, 'cp', axis=0, tiled=True)  90.9 us
    dot_general x32, matrix products, attend_block(): jnp.einsum('rgqd,kgd->gqrk', query_heads, key_heads, preferred_element_ty...  54.4 us
    dot_general x32, matrix products, attend_block(): jnp.dot(query_reach, key_table.T, precision=lax.Precision.HIGHEST) > 0.5  44 us
    all_gather x1, waiting for transfers between devices, per_device(): lax.all_gather(key_vectors, 'cp', axis=0, tiled=True)  41.8 us
    add x32, other arithmetic, attend_block(): totals = totals * factor + jnp.sum(weights, axis=-1)  41.4 us
    reduce_sum x32, other arithmetic, attend_block(): totals = totals * factor + jnp.sum(weights, axis=-1)  24.8 us
    all_to_all x1, blocking collectives, per_device(): lax.all_to_all(attended, 'cp', split_axis=0, concat_axis=0, tiled=True)  24.3 us
  transfers between devices with their start and end apart: 4, of which 4 were waited for; matrix products, arithmetic and copies ran while one was open for 1% of the time, Pallas kernels for 0%

commit v1 on v0

v1 whole, which is shorter than its diff:
```python
import functools
import math

import jax
import jax.numpy as jnp
from jax import lax
from jax.experimental import pallas as pl
from jax.experimental.pallas import tpu as pltpu
from jax.sharding import Mesh, PartitionSpec as P

HEAD_DIM = 128
GROUP = 6
SEGMENTS = 16
AXES = ("zh", "x", "y", "zl", "core")
UNIT = math.log2(math.e) / math.sqrt(HEAD_DIM)
HIDDEN = -1e30
TILE = 256
TILES = 32
STEP = 4
LEAST = 2.0**-60
MOST_SUM = 2.0**100


def shift(x, axis, by):
    return lax.ppermute(x, axis, [(i, (i + by) % 4) for i in range(4)])


def swap(x, axis):
    return lax.ppermute(x, axis, [(0, 1), (1, 0)])


def one_hot_rows(position, bounds_ref):
    inside = (position >= bounds_ref[0:1, :]) & (position < bounds_ref[1:2, :])
    return inside.astype(jnp.float32).astype(jnp.bfloat16)


def attend(
    counts,
    tiles,
    place,
    bounds_ref,
    hidden_ref,
    own_ref,
    other_ref,
    a_refs,
    b_refs,
    kept_ref,
    kept_sums_ref,
    sent_ref,
    sent_sums_ref,
    keys,
    values,
    rows,
    total,
    peak,
    faults,
    arrived,
):
    x, y, zl, core = place[0], place[1], place[2], place[3]
    copies = []

    def bring(source, first_zh, from_x, from_y):
        where = ((from_x % 4) * 4 + from_y % 4) * 2
        for begin, target in ((0, keys), (64, values)):
            copies.append(
                pltpu.make_async_copy(
                    source.at[:, :, pl.ds(begin, 64), :],
                    target.at[pl.ds(first_zh, 2), pl.ds(where, 2), :, pl.ds(0, 128)],
                    arrived,
                )
            )

    away = (0, 3, 1, 2)
    for refs, first_zh, along_x in ((a_refs, 0, True), (b_refs, 2, False)):
        here, minus, plus, far_low, far_high = refs
        for ref, first, step in (
            (here, 0, 0),
            (minus, 0, 3),
            (plus, 0, 1),
            (far_low, 0, 2),
            (far_high, 2, 2),
        ):
            for i in range(ref.shape[0]):
                inner = away[first + i]
                if along_x:
                    bring(ref.at[i], first_zh, x + inner, y + step)
                else:
                    bring(ref.at[i], first_zh, x + step, y + inner)
    for copy in copies:
        copy.start()

    lanes = lax.broadcasted_iota(jnp.int32, (64, 128), 1)
    ones = jnp.ones((32, 64, 128), jnp.bfloat16)
    row = lax.broadcasted_iota(jnp.int32, (32, 64, 128), 1)
    block = lax.broadcasted_iota(jnp.int32, (32, 64, 128), 0)
    for zh in range(4):
        position = zh * 4096 + block * 128 + core * 64 + row
        inside = (position >= bounds_ref[0:1, :][None]) & (position < bounds_ref[1:2, :][None])
        keys[zh, :, :, 128:] = inside.astype(jnp.float32).astype(jnp.bfloat16)
        values[zh, :, :, 128:] = ones
    blank = (lax.broadcasted_iota(jnp.int32, (4, 64, 256), 2) == 255).astype(jnp.float32)
    keys[4, 0:4] = blank.astype(jnp.bfloat16)
    values[4, 0:4] = jnp.zeros((4, 64, 256), jnp.bfloat16)
    faults[...] = jnp.zeros_like(faults)

    for copy in copies:
        copy.wait()

    def prepare(t):
        row = lax.broadcasted_iota(jnp.int32, (64, 128), 0)
        for half, (ref, side) in enumerate(((own_ref, core), (other_ref, 1 - core))):
            position = t * 4096 + (x * 4 + y) * 256 + zl * 128 + side * 64 + row
            mark = jnp.dot(
                one_hot_rows(position, bounds_ref),
                hidden_ref[...],
                preferred_element_type=jnp.float32,
            ).astype(jnp.bfloat16)
            for g in range(GROUP):
                at = pl.ds(half * 384 + g * 64, 64)
                rows[at, 0:128] = ref[t, :, g * 128 : (g + 1) * 128]
                rows[at, 128:256] = mark
        total[...] = jnp.zeros_like(total)

    def load(ref, t, i):
        parts = []
        for j in range(STEP):
            n = tiles[t * TILES + i * STEP + j]
            parts.append(ref[n // 8, pl.ds((n % 8) * 4, 4)].reshape(TILE, 256))
        return jnp.concatenate(parts, axis=0)

    def score(t, i):
        return lax.dot_general(
            rows[...],
            load(keys, t, i),
            (((1,), (1,)), ((), ())),
            preferred_element_type=jnp.float32,
        )

    def finish(t, tops):
        def packed(first, second):
            result = jnp.zeros((64, 128), jnp.float32)
            for g in range(GROUP):
                result = jnp.where(lanes == g, first(g), result)
                if second is not None:
                    result = jnp.where(lanes == 64 + g, second(g), result)
            return result

        for half in range(2):

            def sums(g, half=half):
                return total[half * 384 + g * 64 : half * 384 + (g + 1) * 64, 128:256]

            def top(g, half=half):
                return peak[half * 384 + g * 64 : half * 384 + (g + 1) * 64, :]

            both = packed(sums, top if tops else None)
            if half == 0:
                kept_ref[t] = total[0:384, 0:128]
                kept_sums_ref[t] = both
            else:
                sent_ref[t] = total[384:768, 0:128].astype(jnp.bfloat16)
                sent_sums_ref[t] = both

    def quick(t, _):
        prepare(t)

        def step(i, _):
            weights = jnp.exp2(score(t, i) * UNIT).astype(jnp.bfloat16)
            total[...] += jnp.dot(
                weights, load(values, t, i), preferred_element_type=jnp.float32
            )
            return 0

        lax.fori_loop(0, counts[t], step, 0)
        sums = total[:, 128:256]
        good = (sums >= LEAST) & (sums <= MOST_SUM)
        bad = jnp.where(good, 0.0, 1.0)
        faults[...] = jnp.maximum(faults[...], jnp.max(bad.reshape(96, 8, 128), axis=0))
        finish(t, False)
        return 0

    lax.fori_loop(0, 4, quick, 0)

    @pl.when(jnp.max(faults[...]) > 0.0)
    def _():
        def careful(t, _):
            prepare(t)
            peak[...] = jnp.full_like(peak, -3e38)

            def step(i, _):
                scores = score(t, i) * UNIT
                before = peak[...]
                top = jnp.maximum(before, jnp.max(scores, axis=1, keepdims=True))
                weights = jnp.exp2(scores - top[:, 0:1]).astype(jnp.bfloat16)
                factor = jnp.exp2(before - top)
                added = jnp.dot(
                    weights, load(values, t, i), preferred_element_type=jnp.float32
                )
                total[:, 0:128] = total[:, 0:128] * factor + added[:, 0:128]
                total[:, 128:256] = total[:, 128:256] * factor + added[:, 128:256]
                peak[...] = top
                return 0

            lax.fori_loop(0, counts[t], step, 0)
            finish(t, True)
            return 0

        lax.fori_loop(0, 4, careful, 0)


def attend_call(counts, tiles, place, bounds, hidden, own, other, a_parts, b_parts):
    def body(*refs):
        attend(*refs[:7], refs[7:12], refs[12:17], *refs[17:])

    smem = pl.BlockSpec(memory_space=pltpu.SMEM)
    vmem = pl.BlockSpec(memory_space=pltpu.VMEM)
    anywhere = pl.BlockSpec(memory_space=pl.ANY)
    return pl.pallas_call(
        body,
        out_shape=(
            jax.ShapeDtypeStruct((4, 384, 128), jnp.float32),
            jax.ShapeDtypeStruct((4, 64, 128), jnp.float32),
            jax.ShapeDtypeStruct((4, 384, 128), jnp.bfloat16),
            jax.ShapeDtypeStruct((4, 64, 128), jnp.float32),
        ),
        in_specs=[smem] * 3 + [vmem] * 4 + [anywhere] * 10,
        out_specs=(vmem,) * 4,
        scratch_shapes=[
            pltpu.VMEM((5, 32, 64, 256), jnp.bfloat16),
            pltpu.VMEM((5, 32, 64, 256), jnp.bfloat16),
            pltpu.VMEM((768, 256), jnp.bfloat16),
            pltpu.VMEM((768, 256), jnp.float32),
            pltpu.VMEM((768, 128), jnp.float32),
            pltpu.VMEM((8, 128), jnp.float32),
            pltpu.SemaphoreType.DMA,
        ],
        compiler_params=pltpu.CompilerParams(vmem_limit_bytes=48 * 1024 * 1024),
        name="attend",
    )(counts, tiles, place, bounds, hidden, own, other, *a_parts, *b_parts)


def merge(place, bounds_ref, gate_ref, kept, kept_sums, got, got_sums, out_ref):
    x, y, zl, core = place[0], place[1], place[2], place[3]
    row = lax.broadcasted_iota(jnp.int32, (64, 128), 0)
    for t in range(4):
        position = t * 4096 + (x * 4 + y) * 256 + zl * 128 + core * 64 + row
        gates = jnp.dot(
            one_hot_rows(position, bounds_ref), gate_ref[...], preferred_element_type=jnp.float32
        )
        for g in range(GROUP):
            at = slice(g * 64, (g + 1) * 64)
            first_top = kept_sums[t, :, 64 + g : 65 + g]
            second_top = got_sums[t, :, 64 + g : 65 + g]
            top = jnp.maximum(first_top, second_top)
            first = jnp.exp2(first_top - top)
            second = jnp.exp2(second_top - top)
            sums = first * kept_sums[t, :, g : g + 1] + second * got_sums[t, :, g : g + 1]
            mixed = first * kept[t, at, :] + second * got[t, at, :].astype(jnp.float32)
            result = mixed / sums * gates[:, g * 128 : (g + 1) * 128]
            out_ref[t, :, g * 128 : (g + 1) * 128] = result.astype(jnp.bfloat16)


def merge_call(place, bounds, gate, kept, kept_sums, got, got_sums):
    vmem = pl.BlockSpec(memory_space=pltpu.VMEM)
    return pl.pallas_call(
        merge,
        out_shape=jax.ShapeDtypeStruct((4, 64, 768), jnp.bfloat16),
        in_specs=[pl.BlockSpec(memory_space=pltpu.SMEM)] + [vmem] * 6,
        out_specs=vmem,
        name="merge",
    )(place, bounds, gate, kept, kept_sums, got, got_sums)


def gather_both_ways(own, axis):
    minus = shift(own, axis, 1)
    plus = shift(own, axis, -1)
    half = own.shape[0] // 2
    return minus, plus, shift(minus[:half], axis, 1), shift(plus[half:], axis, -1)


def per_device(
    queries, key_vectors, value_vectors, segment_lengths, segment_allowed, noise_level, gate_table
):
    zh, x, y, zl, core = (lax.axis_index(name) for name in AXES)
    place = jnp.stack([x, y, zl, core, zh]).astype(jnp.int32)

    pairs = jnp.concatenate(
        [
            jnp.transpose(key_vectors.reshape(64, 4, 128), (1, 0, 2)),
            jnp.transpose(value_vectors.reshape(64, 4, 128), (1, 0, 2)),
        ],
        axis=1,
    )
    pairs = jnp.broadcast_to(pairs[:, None], (4, 2, 128, 128)).reshape(8, 128, 128)
    column = lax.all_to_all(pairs, ("zh", "zl"), split_axis=0, concat_axis=0, tiled=True)

    a, b = column[:4], column[4:]
    a_minus, a_plus, a_low, a_high = gather_both_ways(a, "x")
    b_minus, b_plus, b_low, b_high = gather_both_ways(b, "y")
    a_line = jnp.stack([a, a_minus, a_plus, jnp.concatenate([a_low, a_high])])
    b_line = jnp.stack([b, b_minus, b_plus, jnp.concatenate([b_low, b_high])])
    a_parts = (a_line,) + gather_both_ways(a_line, "y")
    b_parts = (b_line,) + gather_both_ways(b_line, "x")
    a_parts = [part.reshape(-1, 2, 2, 128, 128) for part in a_parts]
    b_parts = [part.reshape(-1, 2, 2, 128, 128) for part in b_parts]

    asked = jnp.transpose(queries.reshape(64, 4, 768), (1, 0, 2))
    own = lax.all_to_all(asked, "zh", split_axis=0, concat_axis=0, tiled=True)
    other = swap(own, "core")

    gate_pair = jnp.stack([gate_table, swap(gate_table, "core")])
    gate_all = jnp.concatenate([gate_pair, swap(gate_pair, "zl")])
    gate = lax.dynamic_index_in_dim(gate_all, zh ^ (zl * 2 + core), 0, keepdims=False)
    levels = noise_level[:, None] == jnp.arange(gate.shape[0], dtype=jnp.int32)[None, :]
    levels = jnp.pad(levels.astype(jnp.bfloat16), ((0, 128 - SEGMENTS), (0, 0)))
    gate = jnp.dot(levels, gate, preferred_element_type=jnp.float32).astype(jnp.bfloat16)

    ends = jnp.cumsum(segment_lengths).astype(jnp.int32)
    starts = ends - segment_lengths
    bounds = jnp.pad(jnp.stack([starts, ends]), ((0, 6), (0, 128 - SEGMENTS)))
    hidden = jnp.where(segment_allowed == 1, 0.0, HIDDEN)
    hidden = jnp.pad(hidden, ((0, 128 - SEGMENTS), (0, 128 - SEGMENTS)))
    hidden = jnp.where(jnp.arange(128)[None, :] == 127, HIDDEN, hidden).astype(jnp.bfloat16)
    query_from = jnp.arange(4) * 4096 + (x * 4 + y) * 256 + zl * 128
    key_from = jnp.arange(TILES) * (TILE * 2)
    asks = (starts[None] < query_from[:, None] + 128) & (ends[None] > query_from[:, None])
    holds = (starts[None] < key_from[:, None] + TILE * 2) & (ends[None] > key_from[:, None])
    reach = jnp.any(asks[:, :, None] & (segment_allowed == 1)[None], axis=1)
    seen = jnp.any(reach[:, None, :] & holds[None], axis=2).astype(jnp.int32)
    slot = jnp.cumsum(seen, axis=1) - 1
    wanted = jnp.arange(TILES)
    chosen = (seen[:, :, None] == 1) & (slot[:, :, None] == wanted[None, None])
    tiles = jnp.min(jnp.where(chosen, wanted[None, :, None], TILES), axis=1)
    counts = (jnp.sum(seen, axis=1) + STEP - 1) // STEP
    tiles = tiles.reshape(-1).astype(jnp.int32)
    counts = counts.astype(jnp.int32)

    kept, kept_sums, sent, sent_sums = attend_call(
        counts, tiles, place, bounds, hidden, own, other, a_parts, b_parts
    )
    got, got_sums = swap(sent, "core"), swap(sent_sums, "core")
    merged = merge_call(place, bounds, gate, kept, kept_sums, got, got_sums)
    returned = lax.all_to_all(merged, "zh", split_axis=0, concat_axis=0, tiled=True)
    return jnp.transpose(returned, (1, 0, 2)).reshape(64, 3072)


def solution(mesh):
    finer = Mesh(mesh.devices.reshape(4, 4, 4, 2, 2), AXES)
    by_token = P(AXES, None)
    in_specs = (by_token, by_token, by_token, P(), P(), P(), P(None, ("zl", "core")))
    return jax.shard_map(
        per_device, mesh=finer, in_specs=in_specs, out_specs=by_token, check_vma=False
    )
```

time: 526 us -> 170 us (0.32); the launches traced: 517 us -> 174 us
  matrix products: 202 us -> 0.88 us
  waiting for transfers between devices: 153 us -> 20.1 us
  Pallas kernels: 0 us -> 82.4 us
  other arithmetic: 69.8 us -> 4.19 us
  blocking collectives: 48.9 us -> 20.3 us
  starting transfers between devices: 18.4 us -> 35.8 us
  between operations: 14.2 us -> 0.41 us
    dot_general x100 -> x1, matrix products: 202 us -> 0.88 us  [per_device(): jnp.dot(levels, gate, preferred_element_type=jnp.float32)]
    all_gather x2 -> x0, waiting for transfers between devices: 133 us -> none  [the longest x1 90.9 us: per_device(): lax.all_gather(value_vectors, 'cp', axis=0, tiled=True)]
    pallas_call x0 -> x2, Pallas kernels: none -> 82.4 us  [the longest x1 78.3 us: attend_call(): pl.pallas_call(body, out_shape=(jax.ShapeDtypeStruct((4, 384, 128), jnp.f...]
    add x33 -> x1, other arithmetic: 41.4 us -> 0.01 us  [per_device(): query_from[:, None] + 128]
    all_to_all x4 -> x1, blocking collectives: 48.9 us -> 20.3 us  [per_device(): lax.all_to_all(merged, 'zh', split_axis=0, concat_axis=0, tiled=True)]
    reduce_sum x34 -> x1, other arithmetic: 25.2 us -> 0.11 us  [per_device(): counts = (jnp.sum(seen, axis=1) + STEP - 1) // STEP]
    ppermute x0 -> x21, starting transfers between devices: none -> 23.8 us  [the longest x16 23 us: shift(): return lax.ppermute(x, axis, [(i, (i + by) % 4) for i in range(4)])]
    ppermute x0 -> x21, waiting for transfers between devices: none -> 10.8 us  [the longest x16 7.36 us: shift(): return lax.ppermute(x, axis, [(i, (i + by) % 4) for i in range(4)])]
  transfers between devices with their start and end apart: 4 -> 23, of which waited for: 4 -> 8; matrix products, arithmetic and copies ran while one was open for 1% -> 5% of each run, Pallas kernels for 0% -> 45%
where the time goes in v1:
time: 170 us; the launch traced here: 174 us
  Pallas kernels  82.4 us (48%)
  starting transfers between devices  35.8 us (21%)
  blocking collectives  20.3 us (12%)
  waiting for transfers between devices  20.1 us (12%)
  local copies, waits for them, and re-layouts  9.83 us (6%)
  other arithmetic  4.19 us (2%)
    pallas_call x1, Pallas kernels, attend_call(): pl.pallas_call(body, out_shape=(jax.ShapeDtypeStruct((4, 384, 128), jnp.f...  78.3 us
    ppermute x16, starting transfers between devices, shift(): return lax.ppermute(x, axis, [(i, (i + by) % 4) for i in range(4)])  23 us
    all_to_all x1, blocking collectives, per_device(): lax.all_to_all(merged, 'zh', split_axis=0, concat_axis=0, tiled=True)  20.3 us
    all_to_all x1, waiting for transfers between devices, per_device(): lax.all_to_all(pairs, ('zh', 'zl'), split_axis=0, concat_axis=0, tiled=True)  9.22 us
    all_to_all x1, starting transfers between devices, per_device(): lax.all_to_all(pairs, ('zh', 'zl'), split_axis=0, concat_axis=0, tiled=True)  8.6 us
    ppermute x16, waiting for transfers between devices, shift(): return lax.ppermute(x, axis, [(i, (i + by) % 4) for i in range(4)])  7.36 us
    pallas_call x1, Pallas kernels, merge_call(): pl.pallas_call(merge, out_shape=jax.ShapeDtypeStruct((4, 64, 768), jnp.bf...  4.03 us
    ppermute x5, waiting for transfers between devices, swap(): return lax.ppermute(x, axis, [(0, 1), (1, 0)])  3.48 us
  transfers between devices with their start and end apart: 23, of which 8 were waited for; matrix products, arithmetic and copies ran while one was open for 5% of the time, Pallas kernels for 45%

profile of v1, /device:TPU:6, one launch (start us, length us, event | category | flops | bytes accessed | tf_op | source)
XLA Modules:
  0.0 173.8 jit_solution(13937593458223353479)
XLA Ops:
  0.0 0.9 reshape.224
  0.9 0.1 pad_maximum_fusion.4
  1.1 0.7 broadcast_in_dim.36
  1.8 8.6 %all-to-all-start.1 = ((bf16[8,128,128]{2,1,0:T(8,128)(2,1)}), bf16[8,128,128]{2,1,0:T(8,128)(2,1)S(1)}, u32[]{:S(2)}, u32[]{:S(2)}) async-start(bf16[8,128,128]{2,1,0:T(8,128)(2,1)} %bitcast.13), calls=%async_computation.1 | async-start | bytes 524288 | tf_op jit(solution)/shard_map/all_to_all | solution.py:295
  10.4 0.0 copy-start.21
  10.4 0.6 copy-done.21
  11.1 0.1 copy.14
  11.2 0.1 reduce
  11.3 0.6 copy-done.20
  11.9 0.1 compare_and_fusion.1
  12.0 0.1 compare_and_fusion
  12.1 0.8 copy.21
  12.8 0.1 and_reduce_fusion.1
  12.9 0.1 and_reduce_fusion
  13.0 9.2 %all-to-all-done.1 = bf16[8,128,128]{2,1,0:T(8,128)(2,1)S(1)} async-done(((bf16[8,128,128]{2,1,0:T(8,128)(2,1)}), bf16[8,128,128]{2,1,0:T(8,128)(2,1)S(1)}, u32[]{:S(2)}, u32[]{:S(2)}) %all-to-all-start.1) | async-done | bytes 262176 | tf_op jit(solution)/shard_map/all_to_all | solution.py:295
  22.3 3.5 %all-to-all-start = ((bf16[4,64,768]{2,1,0:T(8,128)(2,1)}), bf16[4,64,768]{2,1,0:T(8,128)(2,1)S(1)}, u32[]{:S(2)}, u32[]{:S(2)}) async-start(bf16[4,64,768]{2,1,0:T(8,128)(2,1)} %bitcast.51), calls=%async_computation | async-start | bytes 786432 | tf_op jit(solution)/shard_map/all_to_all | solution.py:308
  25.7 0.1 slice_bitcast_fusion
  25.8 1.7 collective-permute-start.11
  27.5 1.7 collective-permute-start.12
  29.2 0.5 collective-permute-start.3
  29.6 1.5 collective-permute-start.4
  31.2 0.2 reduce_window_sum.18
  31.4 0.7 collective-permute-done.11
  32.1 0.9 collective-permute-start.13
  33.0 0.1 convert_reduce_fusion
  33.1 2.5 %collective-permute-start.14 = (bf16[2,128,128]{2,1,0:T(8,128)(2,1)S(1)}, bf16[2,128,128]{2,1,0:T(8,128)(2,1)S(1)}, u32[]{:S(2)}, u32[]{:S(2)}) collective-permute-start(bf16[2,128,128]{2,1,0:T(8,128)(2,1)S(1)} %slice.47), channel_id=1, source_target_pairs={{0,12},{4,0},{8,4},{12,8},{1,13},{5,1},{9,5},{13,9},{2,14},{6,2},{... | collective-permute-start | bytes 196616 | tf_op jit(solution)/shard_map/ppermute | solution.py:25
  35.7 1.1 collective-permute-start.5
  36.8 1.1 collective-permute-start.6
  38.0 0.6 copy-done.9
  38.6 0.9 pad_maximum_fusion.3
  39.4 2.2 %collective-permute-start.15 = (bf16[4,4,128,128]{3,2,1,0:T(8,128)(2,1)}, bf16[4,4,128,128]{3,2,1,0:T(8,128)(2,1)S(1)}, u32[]{:S(2)}, u32[]{:S(2)}) collective-permute-start(bf16[4,4,128,128]{3,2,1,0:T(8,128)(2,1)} %pad_maximum_fusion.3), channel_id=1, source_target_pairs={{0,16},{16,32},{32,48},{48,0},{1,17},{17,33},{33,49},{49,1},{2,18}... | collective-permute-start | bytes 1572872 | tf_op jit(solution)/shard_map/ppermute | solution.py:25
  41.7 1.4 collective-permute-done.6
  43.1 0.9 pad_maximum_fusion.1
  43.9 3.2 %collective-permute-start.8 = (bf16[4,4,128,128]{3,2,1,0:T(8,128)(2,1)}, bf16[4,4,128,128]{3,2,1,0:T(8,128)(2,1)S(1)}, u32[]{:S(2)}, u32[]{:S(2)}) collective-permute-start(bf16[4,4,128,128]{3,2,1,0:T(8,128)(2,1)} %pad_maximum_fusion.1), channel_id=1, source_target_pairs={{0,12},{4,0},{8,4},{12,8},{1,13},{5,1},{9,5},{13,9},{2,14},{6,2},{... | collective-permute-start | bytes 1572872 | tf_op jit(solution)/shard_map/ppermute | solution.py:25
  47.2 0.1 select_reduce_fusion
  47.3 2.8 %collective-permute-done.15 = bf16[4,4,128,128]{3,2,1,0:T(8,128)(2,1)S(1)} collective-permute-done((bf16[4,4,128,128]{3,2,1,0:T(8,128)(2,1)}, bf16[4,4,128,128]{3,2,1,0:T(8,128)(2,1)S(1)}, u32[]{:S(2)}, u32[]{:S(2)}) %collective-permute-start.15) | collective-permute-done | bytes 524320 | tf_op jit(solution)/shard_map/ppermute | solution.py:25
  50.1 0.7 slice.48
  50.8 3.4 %collective-permute-start.17 = (bf16[2,4,128,128]{3,2,1,0:T(8,128)(2,1)}, bf16[2,4,128,128]{3,2,1,0:T(8,128)(2,1)S(1)}, u32[]{:S(2)}, u32[]{:S(2)}) collective-permute-start(bf16[2,4,128,128]{3,2,1,0:T(8,128)(2,1)} %slice.48), channel_id=1, source_target_pairs={{0,16},{16,32},{32,48},{48,0},{1,17},{17,33},{33,49},{49,1},{2,18}... | collective-permute-start | bytes 786440 | tf_op jit(solution)/shard_map/ppermute | solution.py:25
  54.2 0.7 slice.49
  54.9 0.7 slice.43
  55.7 0.0 collective-permute-start.9
  55.7 0.7 slice.44
  56.4 3.2 %collective-permute-start.10 = (bf16[2,4,128,128]{3,2,1,0:T(8,128)(2,1)}, bf16[2,4,128,128]{3,2,1,0:T(8,128)(2,1)}, u32[]{:S(2)}, u32[]{:S(2)}) collective-permute-start(bf16[2,4,128,128]{3,2,1,0:T(8,128)(2,1)} %slice.44), channel_id=1, source_target_pairs={{0,12},{4,0},{8,4},{12,8},{1,13},{5,1},{9,5},{13,9},{2,14},{6,2},{... | collective-permute-start | bytes 786440 | tf_op jit(solution)/shard_map/ppermute | solution.py:25
  59.6 0.1 reshape.222.refs_1_
  59.7 0.1 stack.91.refs_2_.place
  59.8 1.2 pad_maximum_fusion.2.refs_12_
  61.1 0.1 collective-permute-start
  61.2 0.1 pad_maximum_fusion.refs_7_
  61.3 1.4 collective-permute-done.18
  62.7 0.8 collective-permute-done.9
  63.6 0.3 collective-permute-done.10
  63.8 78.3 %attend.1 = (f32[4,384,128]{2,1,0:T(8,128)}, f32[4,64,128]{2,1,0:T(8,128)S(1)}, bf16[4,384,128]{2,1,0:T(8,128)(2,1)}, f32[4,64,128]{2,1,0:T(8,128)}) custom-call(s32[4]{0:T(128)S(1)} %and_select_fusion.refs_0_, s32[128]{0:T(128)S(1)} %reshape.222.refs_1_, s32[5]{0:T(128)S(1)} %stack.91.refs_2_.place, s32[8,128]{1,0:T(8,128)S(1)} %pad.15.refs_3_.bounds_ref, ...), custom_call_target="tpu_custom_call" | custom-call | tf_op jit(solution)/shard_map/attend/pallas_call | solution.py:218
  142.2 0.6 copy-done
  142.8 0.0 copy-start.22
  142.8 0.1 collective-permute-start.1
  142.9 0.6 collective-permute-start.20
  143.5 0.1 iota_compare_fusion.1
  143.6 3.5 %collective-permute-done.1 = bf16[2,16,768]{2,1,0:T(8,128)(2,1)S(1)} collective-permute-done((bf16[2,16,768]{2,1,0:T(8,128)(2,1)S(1)}, bf16[2,16,768]{2,1,0:T(8,128)(2,1)S(1)}, u32[]{:S(2)}, u32[]{:S(2)}) %collective-permute-start.1) | collective-permute-done | bytes 49184 | tf_op jit(solution)/shard_map/ppermute | solution.py:29
  147.1 0.9 convolution_convert_fusion.gate_ref
  148.0 0.6 copy-done.17
  148.6 0.1 copy-done.15
  148.8 4.0 %merge.1 = bf16[4,64,768]{2,1,0:T(8,128)(2,1)} custom-call(s32[5]{0:T(128)} %copy-done.2, s32[8,128]{1,0:T(8,128)} %copy-done.1, bf16[128,768]{1,0:T(8,128)(2,1)} %convolution_convert_fusion.gate_ref, f32[4,384,128]{2,1,0:T(8,128)} %get-tuple-element.9.kept, f32[4,64,128]{2,1,0:T(8,128)} %copy-done, bf16[4,384,128]{2,1,0:T(8,128)(2,1)} %copy-done.15, ...), custom_call_target="tpu_custom_call" | custom-call | tf_op jit(solution)/shard_map/merge/pallas_call | solution.py:265
  152.8 20.3 %all_to_all.15 = bf16[4,64,768]{2,1,0:T(8,128)(2,1)S(1)} all-to-all(bf16[4,64,768]{2,1,0:T(8,128)(2,1)} %merge.1), channel_id=1, replica_groups=mesh['zh'=4,'x'=4,'y'=4,'zl'=2,'core'=2] {'zh'}, dimensions={0} | all-to-all | bytes 786432 | tf_op jit(solution)/shard_map/all_to_all | solution.py:343
  173.0 0.8 copy.19
  (81 shorter events, 0.3 us)
Async XLA Ops:
  0.0 0.9 copy-start.19
  1.8 10.3 %copy-start.16 = (bf16[64,3072]{1,0:T(8,128)(2,1)S(1)}, bf16[64,3072]{1,0:T(8,128)(2,1)}, u32[]{:S(2)}) copy-start(bf16[64,3072]{1,0:T(8,128)(2,1)} %param.7) | copy-start | bytes 1179652
  1.8 20.5 %all-to-all-start.1 = ((bf16[8,128,128]{2,1,0:T(8,128)(2,1)}), bf16[8,128,128]{2,1,0:T(8,128)(2,1)S(1)}, u32[]{:S(2)}, u32[]{:S(2)}) async-start(bf16[8,128,128]{2,1,0:T(8,128)(2,1)} %bitcast.13), calls=%async_computation.1 | async-start | bytes 524288 | tf_op jit(solution)/shard_map/all_to_all | solution.py:295
  10.4 0.7 copy-start.21
  11.2 0.7 copy-start.20
  22.3 24.9 %all-to-all-start = ((bf16[4,64,768]{2,1,0:T(8,128)(2,1)}), bf16[4,64,768]{2,1,0:T(8,128)(2,1)S(1)}, u32[]{:S(2)}, u32[]{:S(2)}) async-start(bf16[4,64,768]{2,1,0:T(8,128)(2,1)} %bitcast.51), calls=%async_computation | async-start | bytes 786432 | tf_op jit(solution)/shard_map/all_to_all | solution.py:308
  25.8 7.3 %copy-start.12 = (bf16[4,128,128]{2,1,0:T(8,128)(2,1)}, bf16[4,128,128]{2,1,0:T(8,128)(2,1)S(1)}, u32[]{:S(2)}) copy-start(bf16[4,128,128]{2,1,0:T(8,128)(2,1)S(1)} %get-tuple-element.20) | copy-start | bytes 393220
  25.8 7.3 %copy-start.14 = (bf16[4,128,128]{2,1,0:T(8,128)(2,1)}, bf16[4,128,128]{2,1,0:T(8,128)(2,1)S(1)}, u32[]{:S(2)}) copy-start(bf16[4,128,128]{2,1,0:T(8,128)(2,1)S(1)} %get-tuple-element.19) | copy-start | bytes 393220
  25.8 6.3 %collective-permute-start.11 = (bf16[4,128,128]{2,1,0:T(8,128)(2,1)S(1)}, bf16[4,128,128]{2,1,0:T(8,128)(2,1)S(1)}, u32[]{:S(2)}, u32[]{:S(2)}) collective-permute-start(bf16[4,128,128]{2,1,0:T(8,128)(2,1)S(1)} %get-tuple-element.19), channel_id=1, source_target_pairs={{0,4},{4,8},{8,12},{12,0},{1,5},{5,9},{9,13},{13,1},{2,6},{6,10},{... | collective-permute-start | bytes 393224 | tf_op jit(solution)/shard_map/ppermute | solution.py:25
  27.5 5.6 %collective-permute-start.12 = (bf16[4,128,128]{2,1,0:T(8,128)(2,1)S(1)}, bf16[4,128,128]{2,1,0:T(8,128)(2,1)S(1)}, u32[]{:S(2)}, u32[]{:S(2)}) collective-permute-start(bf16[4,128,128]{2,1,0:T(8,128)(2,1)S(1)} %get-tuple-element.19), channel_id=1, source_target_pairs={{0,12},{4,0},{8,4},{12,8},{1,13},{5,1},{9,5},{13,9},{2,14},{6,2},{... | collective-permute-start | bytes 393224 | tf_op jit(solution)/shard_map/ppermute | solution.py:25
  29.2 6.5 %collective-permute-start.3 = (bf16[4,128,128]{2,1,0:T(8,128)(2,1)S(1)}, bf16[4,128,128]{2,1,0:T(8,128)(2,1)S(1)}, u32[]{:S(2)}, u32[]{:S(2)}) collective-permute-start(bf16[4,128,128]{2,1,0:T(8,128)(2,1)S(1)} %get-tuple-element.20), channel_id=1, source_target_pairs={{0,16},{16,32},{32,48},{48,0},{1,17},{17,33},{33,49},{49,1},{2,18}... | collective-permute-start | bytes 393224 | tf_op jit(solution)/shard_map/ppermute | solution.py:25
  29.6 7.1 %collective-permute-start.4 = (bf16[4,128,128]{2,1,0:T(8,128)(2,1)S(1)}, bf16[4,128,128]{2,1,0:T(8,128)(2,1)S(1)}, u32[]{:S(2)}, u32[]{:S(2)}) collective-permute-start(bf16[4,128,128]{2,1,0:T(8,128)(2,1)S(1)} %get-tuple-element.20), channel_id=1, source_target_pairs={{0,48},{16,0},{32,16},{48,32},{1,49},{17,1},{33,17},{49,33},{2,50}... | collective-permute-start | bytes 393224 | tf_op jit(solution)/shard_map/ppermute | solution.py:25
  32.1 5.8 %copy-start.7 = (bf16[4,128,128]{2,1,0:T(8,128)(2,1)}, bf16[4,128,128]{2,1,0:T(8,128)(2,1)S(1)}, u32[]{:S(2)}) copy-start(bf16[4,128,128]{2,1,0:T(8,128)(2,1)S(1)} %collective-permute-done.11) | copy-start | bytes 393220
  32.1 5.8 %collective-permute-start.13 = (bf16[2,128,128]{2,1,0:T(8,128)(2,1)S(1)}, bf16[2,128,128]{2,1,0:T(8,128)(2,1)S(1)}, u32[]{:S(2)}, u32[]{:S(2)}) collective-permute-start(bf16[2,128,128]{2,1,0:T(8,128)(2,1)S(1)} %slice.46), channel_id=1, source_target_pairs={{0,4},{4,8},{8,12},{12,0},{1,5},{5,9},{9,13},{13,1},{2,6},{6,10},{... | collective-permute-start | bytes 196616 | tf_op jit(solution)/shard_map/ppermute | solution.py:25
  33.1 4.8 %copy-start.8 = (bf16[4,128,128]{2,1,0:T(8,128)(2,1)}, bf16[4,128,128]{2,1,0:T(8,128)(2,1)S(1)}, u32[]{:S(2)}) copy-start(bf16[4,128,128]{2,1,0:T(8,128)(2,1)S(1)} %collective-permute-done.12) | copy-start | bytes 393220
  33.1 4.8 %collective-permute-start.14 = (bf16[2,128,128]{2,1,0:T(8,128)(2,1)S(1)}, bf16[2,128,128]{2,1,0:T(8,128)(2,1)S(1)}, u32[]{:S(2)}, u32[]{:S(2)}) collective-permute-start(bf16[2,128,128]{2,1,0:T(8,128)(2,1)S(1)} %slice.47), channel_id=1, source_target_pairs={{0,12},{4,0},{8,4},{12,8},{1,13},{5,1},{9,5},{13,9},{2,14},{6,2},{... | collective-permute-start | bytes 196616 | tf_op jit(solution)/shard_map/ppermute | solution.py:25
  35.7 7.4 %copy-start.3 = (bf16[4,128,128]{2,1,0:T(8,128)(2,1)}, bf16[4,128,128]{2,1,0:T(8,128)(2,1)S(1)}, u32[]{:S(2)}) copy-start(bf16[4,128,128]{2,1,0:T(8,128)(2,1)S(1)} %collective-permute-done.3) | copy-start | bytes 393220
  35.7 6.0 %collective-permute-start.5 = (bf16[2,128,128]{2,1,0:T(8,128)(2,1)S(1)}, bf16[2,128,128]{2,1,0:T(8,128)(2,1)S(1)}, u32[]{:S(2)}, u32[]{:S(2)}) collective-permute-start(bf16[2,128,128]{2,1,0:T(8,128)(2,1)S(1)} %slice.41), channel_id=1, source_target_pairs={{0,16},{16,32},{32,48},{48,0},{1,17},{17,33},{33,49},{49,1},{2,18}... | collective-permute-start | bytes 196616 | tf_op jit(solution)/shard_map/ppermute | solution.py:25
  36.8 6.3 %copy-start.5 = (bf16[4,128,128]{2,1,0:T(8,128)(2,1)}, bf16[4,128,128]{2,1,0:T(8,128)(2,1)S(1)}, u32[]{:S(2)}) copy-start(bf16[4,128,128]{2,1,0:T(8,128)(2,1)S(1)} %collective-permute-done.4) | copy-start | bytes 393220
  36.8 6.3 %collective-permute-start.6 = (bf16[2,128,128]{2,1,0:T(8,128)(2,1)S(1)}, bf16[2,128,128]{2,1,0:T(8,128)(2,1)S(1)}, u32[]{:S(2)}, u32[]{:S(2)}) collective-permute-start(bf16[2,128,128]{2,1,0:T(8,128)(2,1)S(1)} %slice.42), channel_id=1, source_target_pairs={{0,48},{16,0},{32,16},{48,32},{1,49},{17,1},{33,17},{49,33},{2,50}... | collective-permute-start | bytes 196616 | tf_op jit(solution)/shard_map/ppermute | solution.py:25
  37.9 0.7 copy-start.9
  39.4 10.6 %collective-permute-start.15 = (bf16[4,4,128,128]{3,2,1,0:T(8,128)(2,1)}, bf16[4,4,128,128]{3,2,1,0:T(8,128)(2,1)S(1)}, u32[]{:S(2)}, u32[]{:S(2)}) collective-permute-start(bf16[4,4,128,128]{3,2,1,0:T(8,128)(2,1)} %pad_maximum_fusion.3), channel_id=1, source_target_pairs={{0,16},{16,32},{32,48},{48,0},{1,17},{17,33},{33,49},{49,1},{2,18}... | collective-permute-start | bytes 1572872 | tf_op jit(solution)/shard_map/ppermute | solution.py:25
  41.7 12.5 %collective-permute-start.16 = (bf16[4,4,128,128]{3,2,1,0:T(8,128)(2,1)}, bf16[4,4,128,128]{3,2,1,0:T(8,128)(2,1)S(1)}, u32[]{:S(2)}, u32[]{:S(2)}) collective-permute-start(bf16[4,4,128,128]{3,2,1,0:T(8,128)(2,1)} %pad_maximum_fusion.3), channel_id=1, source_target_pairs={{0,48},{16,0},{32,16},{48,32},{1,49},{17,1},{33,17},{49,33},{2,50}... | collective-permute-start | bytes 1572872 | tf_op jit(solution)/shard_map/ppermute | solution.py:25
  43.0 0.9 copy-start.10
  43.9 11.0 %collective-permute-start.7 = (bf16[4,4,128,128]{3,2,1,0:T(8,128)(2,1)}, bf16[4,4,128,128]{3,2,1,0:T(8,128)(2,1)S(1)}, u32[]{:S(2)}, u32[]{:S(2)}) collective-permute-start(bf16[4,4,128,128]{3,2,1,0:T(8,128)(2,1)} %pad_maximum_fusion.1), channel_id=1, source_target_pairs={{0,4},{4,8},{8,12},{12,0},{1,5},{5,9},{9,13},{13,1},{2,6},{6,10},{... | collective-permute-start | bytes 1572872 | tf_op jit(solution)/shard_map/ppermute | solution.py:25
  43.9 11.8 %collective-permute-start.8 = (bf16[4,4,128,128]{3,2,1,0:T(8,128)(2,1)}, bf16[4,4,128,128]{3,2,1,0:T(8,128)(2,1)S(1)}, u32[]{:S(2)}, u32[]{:S(2)}) collective-permute-start(bf16[4,4,128,128]{3,2,1,0:T(8,128)(2,1)} %pad_maximum_fusion.1), channel_id=1, source_target_pairs={{0,12},{4,0},{8,4},{12,8},{1,13},{5,1},{9,5},{13,9},{2,14},{6,2},{... | collective-permute-start | bytes 1572872 | tf_op jit(solution)/shard_map/ppermute | solution.py:25
  47.2 13.9 %collective-permute-start.2 = (bf16[4,64,768]{2,1,0:T(8,128)(2,1)S(1)}, bf16[4,64,768]{2,1,0:T(8,128)(2,1)S(1)}, u32[]{:S(2)}, u32[]{:S(2)}) collective-permute-start(bf16[4,64,768]{2,1,0:T(8,128)(2,1)S(1)} %all-to-all-done.refs_5_), channel_id=1, source_target_pairs={{0,1},{1,0},{2,3},{3,2},{4,5},{5,4},{6,7},{7,6},{8,9},{9,8},{10,11... | collective-permute-start | bytes 1179656 | tf_op jit(solution)/shard_map/ppermute | solution.py:29
  50.8 10.5 %collective-permute-start.17 = (bf16[2,4,128,128]{3,2,1,0:T(8,128)(2,1)}, bf16[2,4,128,128]{3,2,1,0:T(8,128)(2,1)S(1)}, u32[]{:S(2)}, u32[]{:S(2)}) collective-permute-start(bf16[2,4,128,128]{3,2,1,0:T(8,128)(2,1)} %slice.48), channel_id=1, source_target_pairs={{0,16},{16,32},{32,48},{48,0},{1,17},{17,33},{33,49},{49,1},{2,18}... | collective-permute-start | bytes 786440 | tf_op jit(solution)/shard_map/ppermute | solution.py:25
  54.9 7.8 %collective-permute-start.18 = (bf16[2,4,128,128]{3,2,1,0:T(8,128)(2,1)}, bf16[2,4,128,128]{3,2,1,0:T(8,128)(2,1)S(1)}, u32[]{:S(2)}, u32[]{:S(2)}) collective-permute-start(bf16[2,4,128,128]{3,2,1,0:T(8,128)(2,1)} %slice.49), channel_id=1, source_target_pairs={{0,48},{16,0},{32,16},{48,32},{1,49},{17,1},{33,17},{49,33},{2,50}... | collective-permute-start | bytes 786440 | tf_op jit(solution)/shard_map/ppermute | solution.py:25
  55.7 7.9 %collective-permute-start.9 = (bf16[2,4,128,128]{3,2,1,0:T(8,128)(2,1)}, bf16[2,4,128,128]{3,2,1,0:T(8,128)(2,1)}, u32[]{:S(2)}, u32[]{:S(2)}) collective-permute-start(bf16[2,4,128,128]{3,2,1,0:T(8,128)(2,1)} %slice.43), channel_id=1, source_target_pairs={{0,4},{4,8},{8,12},{12,0},{1,5},{5,9},{9,13},{13,1},{2,6},{6,10},{... | collective-permute-start | bytes 786440 | tf_op jit(solution)/shard_map/ppermute | solution.py:25
  56.4 7.4 %collective-permute-start.10 = (bf16[2,4,128,128]{3,2,1,0:T(8,128)(2,1)}, bf16[2,4,128,128]{3,2,1,0:T(8,128)(2,1)}, u32[]{:S(2)}, u32[]{:S(2)}) collective-permute-start(bf16[2,4,128,128]{3,2,1,0:T(8,128)(2,1)} %slice.44), channel_id=1, source_target_pairs={{0,12},{4,0},{8,4},{12,8},{1,13},{5,1},{9,5},{13,9},{2,14},{6,2},{... | collective-permute-start | bytes 786440 | tf_op jit(solution)/shard_map/ppermute | solution.py:25
  59.7 4.1 %copy-start.1 = (s32[8,128]{1,0:T(8,128)}, s32[8,128]{1,0:T(8,128)S(1)}, u32[]{:S(2)}) copy-start(s32[8,128]{1,0:T(8,128)S(1)} %pad.15.refs_3_.bounds_ref) | copy-start | bytes 12292
  59.8 4.0 %copy-start.2 = (s32[5]{0:T(128)}, s32[5]{0:T(128)S(1)}, u32[]{:S(2)}) copy-start(s32[5]{0:T(128)S(1)} %stack.91.refs_2_.place) | copy-start | bytes 64
  59.8 1.3 copy-start.18
  59.8 1.4 copy-start.4
  59.8 1.4 copy-start.6
  59.8 1.4 copy-start.11
  59.8 1.4 copy-start.13
  61.1 81.7 %collective-permute-start = (bf16[16,768]{1,0:T(8,128)(2,1)S(1)}, bf16[16,768]{1,0:T(8,128)(2,1)S(1)}, u32[]{:S(2)}, u32[]{:S(2)}) collective-permute-start(bf16[16,768]{1,0:T(8,128)(2,1)S(1)} %copy-done.18), channel_id=1, source_target_pairs={{0,1},{1,0},{2,3},{3,2},{4,5},{5,4},{6,7},{7,6},{8,9},{9,8},{10,11... | collective-permute-start | bytes 73736 | tf_op jit(solution)/shard_map/ppermute | solution.py:29
  142.2 0.7 copy-start
  142.8 5.2 %collective-permute-start.19 = (bf16[4,384,128]{2,1,0:T(8,128)(2,1)}, bf16[4,384,128]{2,1,0:T(8,128)(2,1)S(1)}, u32[]{:S(2)}, u32[]{:S(2)}) collective-permute-start(bf16[4,384,128]{2,1,0:T(8,128)(2,1)} %get-tuple-element.11), channel_id=1, source_target_pairs={{0,1},{1,0},{2,3},{3,2},{4,5},{5,4},{6,7},{7,6},{8,9},{9,8},{10,11... | collective-permute-start | bytes 1179656 | tf_op jit(solution)/shard_map/ppermute | solution.py:29
  142.8 0.7 copy-start.22
  142.8 4.2 %collective-permute-start.1 = (bf16[2,16,768]{2,1,0:T(8,128)(2,1)S(1)}, bf16[2,16,768]{2,1,0:T(8,128)(2,1)S(1)}, u32[]{:S(2)}, u32[]{:S(2)}) collective-permute-start(bf16[2,16,768]{2,1,0:T(8,128)(2,1)S(1)} %pad_maximum_fusion.5), channel_id=1, source_target_pairs={{0,2},{2,0},{1,3},{3,1},{4,6},{6,4},{5,7},{7,5},{8,10},{10,8},{9,1... | collective-permute-start | bytes 147464 | tf_op jit(solution)/shard_map/ppermute | solution.py:29
  142.9 5.0 %collective-permute-start.20 = (f32[4,64,128]{2,1,0:T(8,128)}, f32[4,64,128]{2,1,0:T(8,128)S(1)}, u32[]{:S(2)}, u32[]{:S(2)}) collective-permute-start(f32[4,64,128]{2,1,0:T(8,128)} %get-tuple-element.12), channel_id=1, source_target_pairs={{0,1},{1,0},{2,3},{3,2},{4,5},{5,4},{6,7},{7,6},{8,9},{9,8},{10,11... | collective-permute-start | bytes 393224 | tf_op jit(solution)/shard_map/ppermute | solution.py:29
  148.0 0.7 copy-start.17
  148.0 0.8 copy-start.15

commit v2 on v0

v2 whole, which is shorter than its diff:
```python
import math

import jax
import jax.numpy as jnp
from jax import lax
from jax.experimental import pallas as pl
from jax.experimental.pallas import tpu as pltpu
from jax.sharding import Mesh, PartitionSpec as P

HEAD_DIM = 128
GROUP = 6
SEGMENTS = 16
AXES = ("zh", "x", "y", "zl", "core")
COLUMN = ("zh", "zl")
UNIT = math.log2(math.e) / math.sqrt(HEAD_DIM)
HIDDEN = -1e30
LEAST = 2.0**-60
MOST_SUM = 2.0**100
TILE = 128
TILES = 64
LONG, SHORT = 8, 4
STAGES = ((0, 16), (16, 32), (48, 16))
LAST = len(STAGES) - 1
AWAY = (0, 3, 1, 2)


def shift(x, axis, by):
    return lax.ppermute(x, axis, [(i, (i + by) % 4) for i in range(4)])


def swap(x, axis):
    return lax.ppermute(x, axis, [(0, 1), (1, 0)])


def shift_cross(x, first, by):
    pairs = []
    for i in range(4):
        for j in range(4):
            for core in range(2):
                along_x = (core == 0) == first
                to = ((i + by) % 4 * 4 + j) if along_x else (i * 4 + (j + by) % 4)
                pairs.append(((i * 4 + j) * 2 + core, to * 2 + core))
    return lax.ppermute(x, ("x", "y", "core"), pairs)


def shift_column(x, by, flip):
    pairs = [(i, (i // 2 + by) % 4 * 2 + (i % 2 ^ flip)) for i in range(8)]
    return lax.ppermute(x, COLUMN, pairs)


def one_hot_rows(position, bounds_ref):
    inside = (position >= bounds_ref[0:1, :]) & (position < bounds_ref[1:2, :])
    return inside.astype(jnp.float32).astype(jnp.bfloat16)


def attend(stage, *refs):
    last = stage == LAST
    base, count = STAGES[stage]
    parts_count = (1, 2, 4)[stage]
    fast_parts = (1, 2, 1)[stage]
    slots, tiles, place, bounds_ref, hidden_ref, own_ref, other_ref = refs[:7]
    refs = refs[7:]
    if stage > 0:
        state_ref, refs = refs[0], refs[1:]
    parts, refs = refs[:parts_count], refs[parts_count:]
    if last:
        kept_ref, kept_sums_ref, sent_ref, refs = *refs[:3], refs[3:]
    else:
        result_ref, refs = refs[0], refs[1:]
    keys, values, marks, ones, rows, total, arrived = refs[:7]
    if last:
        peak, faults = refs[7:]
    x, y, zl, core, zh = place[0], place[1], place[2], place[3], place[4]
    blank_tile = TILES if last else count

    def bring(some, at):
        copies = []
        for part in some:
            n = part.shape[0]
            for begin, target in ((0, keys), (64, values)):
                copies.append(
                    pltpu.make_async_copy(
                        part.at[:, :, pl.ds(begin, 64), :],
                        target.at[pl.ds(at, n)],
                        arrived,
                    )
                )
            at += n
        for copy in copies:
            copy.start()
        return copies

    def mark_keys(first, start, number):
        row = lax.broadcasted_iota(jnp.int32, (TILE, 128), 0)
        inner = ((row // 64) ^ zl) * 128 + core * 64 + row % 64

        def mark(n, _):
            position = tile_from(place, start + n) + inner
            at = first + n
            marks[at] = one_hot_rows(position, bounds_ref)
            return 0

        lax.fori_loop(0, number, mark, 0)

    copies = bring(parts[:fast_parts], 0)
    mark_keys(0, base, count)
    blank = (lax.broadcasted_iota(jnp.int32, (TILE, 128), 1) == 127).astype(jnp.float32)
    marks[blank_tile] = blank.astype(jnp.bfloat16)
    keys[blank_tile] = jnp.zeros((2, 64, 128), jnp.bfloat16)
    values[blank_tile] = jnp.zeros((2, 64, 128), jnp.bfloat16)
    ones[...] = jnp.ones_like(ones)
    if last:
        faults[...] = jnp.zeros_like(faults)
    for copy in copies:
        copy.wait()

    def prepare(t):
        row = lax.broadcasted_iota(jnp.int32, (64, 128), 0)
        for half, (ref, side) in enumerate(((own_ref, core), (other_ref, 1 - core))):
            position = rows_from(place, t) + side * 64 + row
            mark = jnp.dot(
                one_hot_rows(position, bounds_ref),
                hidden_ref[...],
                preferred_element_type=jnp.float32,
            ).astype(jnp.bfloat16)
            for g in range(GROUP):
                at = pl.ds(half * 384 + g * 64, 64)
                rows[at, 0:128] = ref[t, :, g * 128 : (g + 1) * 128]
                rows[at, 128:256] = mark

    def load(ref, beside, numbers):
        wide = [
            jnp.concatenate([ref[n].reshape(TILE, 128), beside(n)], axis=1) for n in numbers
        ]
        return jnp.concatenate(wide, axis=0)

    def load_keys(numbers):
        return load(keys, lambda n: marks[n], numbers)

    def load_values(numbers):
        return load(values, lambda n: ones[...], numbers)

    def score(numbers):
        return lax.dot_general(
            rows[...],
            load_keys(numbers),
            (((1,), (1,)), ((), ())),
            preferred_element_type=jnp.float32,
        )

    def finish(t, tops):
        lanes = lax.broadcasted_iota(jnp.int32, (64, 128), 1)
        for half in range(2):
            both = jnp.zeros((64, 128), jnp.float32)
            for g in range(GROUP):
                at = slice(half * 384 + g * 64, half * 384 + (g + 1) * 64)
                both = jnp.where(lanes == g, total[at, 128:256], both)
                if tops:
                    both = jnp.where(lanes == 64 + g, peak[at, :], both)
            if half == 0:
                kept_ref[t] = total[0:384, 0:128]
                kept_sums_ref[t] = both
            else:
                sent_ref[t, 0:384, :] = total[384:768, 0:128].astype(jnp.bfloat16)
                for i in range(3):
                    piece = both.astype(jnp.bfloat16)
                    sent_ref[t, 384 + 64 * i : 448 + 64 * i, :] = piece
                    both = both - piece.astype(jnp.float32)

    def quick(t, _):
        prepare(t)
        total[...] = jnp.zeros_like(total) if stage == 0 else state_ref[t]
        begin, end = slots[t, base], slots[t, base + count]
        seen = end - begin

        def numbers(first, width):
            picked = []
            for j in range(width):
                inside = first + j < end
                at = jnp.where(inside, first + j, 0)
                picked.append(jnp.where(inside, tiles[t, at] - base, blank_tile))
            return picked

        def add(first, width):
            picked = numbers(first, width)
            weights = jnp.exp2(score(picked) * UNIT).astype(jnp.bfloat16)
            total[...] += jnp.dot(
                weights, load_values(picked), preferred_element_type=jnp.float32
            )

        def step(i, _):
            add(begin + i * LONG, LONG)
            return 0

        whole = (seen + LONG - SHORT - 1) // LONG
        lax.fori_loop(0, whole, step, 0)

        @pl.when(seen > whole * LONG)
        def _():
            add(begin + whole * LONG, SHORT)

        if last:
            sums = total[:, 128:256]
            good = (sums >= LEAST) & (sums <= MOST_SUM)
            bad = jnp.where(good, 0.0, 1.0)
            faults[...] = jnp.maximum(faults[...], jnp.max(bad.reshape(96, 8, 128), axis=0))
            finish(t, False)
        else:
            result_ref[t] = total[...]
        return 0

    lax.fori_loop(0, 4, quick, 0)

    if last:

        @pl.when(jnp.max(faults[...]) > 0.0)
        def _():
            others = bring(parts[fast_parts:], count)
            mark_keys(count, 0, base)
            for copy in others:
                copy.wait()

            def careful(t, _):
                prepare(t)
                total[...] = jnp.zeros_like(total)
                peak[...] = jnp.full_like(peak, -3e38)

                def step(i, _):
                    picked = [i * LONG + j for j in range(LONG)]
                    scores = score(picked) * UNIT
                    before = peak[...]
                    top = jnp.maximum(before, jnp.max(scores, axis=1, keepdims=True))
                    weights = jnp.exp2(scores - top[:, 0:1]).astype(jnp.bfloat16)
                    factor = jnp.exp2(before - top)
                    added = jnp.dot(
                        weights, load_values(picked), preferred_element_type=jnp.float32
                    )
                    total[:, 0:128] = total[:, 0:128] * factor + added[:, 0:128]
                    total[:, 128:256] = total[:, 128:256] * factor + added[:, 128:256]
                    peak[...] = top
                    return 0

                lax.fori_loop(0, TILES // LONG, step, 0)
                finish(t, True)
                return 0

            lax.fori_loop(0, 4, careful, 0)


def attend_call(stage, scalars, tables, asked, state, parts):
    last = stage == LAST
    smem = pl.BlockSpec(memory_space=pltpu.SMEM)
    vmem = pl.BlockSpec(memory_space=pltpu.VMEM)
    anywhere = pl.BlockSpec(memory_space=pl.ANY)
    held = TILES + 1 if last else STAGES[stage][1] + 1
    scratch = [
        pltpu.VMEM((held, 2, 64, 128), jnp.bfloat16),
        pltpu.VMEM((held, 2, 64, 128), jnp.bfloat16),
        pltpu.VMEM((held, TILE, 128), jnp.bfloat16),
        pltpu.VMEM((TILE, 128), jnp.bfloat16),
        pltpu.VMEM((768, 256), jnp.bfloat16),
        pltpu.VMEM((768, 256), jnp.float32),
        pltpu.SemaphoreType.DMA,
    ]
    if last:
        scratch += [pltpu.VMEM((768, 128), jnp.float32), pltpu.VMEM((8, 128), jnp.float32)]
        out_shape = (
            jax.ShapeDtypeStruct((4, 384, 128), jnp.float32),
            jax.ShapeDtypeStruct((4, 64, 128), jnp.float32),
            jax.ShapeDtypeStruct((4, 576, 128), jnp.bfloat16),
        )
    else:
        out_shape = jax.ShapeDtypeStruct((4, 768, 256), jnp.float32)
    states = [] if state is None else [state]

    def body(*refs):
        attend(stage, *refs)

    share = STAGES[stage][1] / TILES
    return pl.pallas_call(
        body,
        out_shape=out_shape,
        in_specs=[smem] * 3 + [vmem] * (4 + len(states)) + [anywhere] * len(parts),
        out_specs=(vmem,) * 3 if last else vmem,
        scratch_shapes=scratch,
        compiler_params=pltpu.CompilerParams(vmem_limit_bytes=24 * 1024 * 1024),
        cost_estimate=pl.CostEstimate(
            flops=int(1.2e10 * share), bytes_accessed=8 << 20, transcendentals=0
        ),
        name=f"attend{stage}",
    )(*scalars, *tables, *asked, *states, *parts)


def ring_step(v):
    return jnp.where(v == 0, 0, jnp.where(v == 1, 3, v - 1))


def tile_from(place, n):
    x, y, core, zh = place[0], place[1], place[3], place[4]
    across, along, depth = ring_step(n // 16), ring_step(n // 4 % 4), n % 4
    first = (core == 0).astype(jnp.int32)
    by_x = along * first + across * (1 - first)
    by_y = across * first + along * (1 - first)
    return (zh + 4 - depth) % 4 * 4096 + ((x + by_x) % 4 * 4 + (y + by_y) % 4) * 256


def rows_from(place, t):
    x, y, zl = place[0], place[1], place[2]
    return t * 4096 + (x * 4 + y) * 256 + zl * 128


def plan(place, lengths, allowed, slots_ref, tiles_ref, bounds_ref, hidden_ref, pad):
    lane = lax.broadcasted_iota(jnp.int32, (8, 128), 1)
    line = lax.broadcasted_iota(jnp.int32, (8, 128), 0)
    bounds = jnp.zeros((8, 128), jnp.int32)
    start = 0
    for c in range(SEGMENTS):
        end = start + lengths[c]
        at = lane == c
        bounds = jnp.where(at & (line == 0), start, bounds)
        bounds = jnp.where(at & (line == 1), end, bounds)
        start = end
    bounds_ref[...] = bounds
    pad[...] = jnp.zeros_like(pad)
    pad[0:SEGMENTS, 0:SEGMENTS] = allowed[...].astype(jnp.float32)
    open_pairs = pad[...]
    row = lax.broadcasted_iota(jnp.int32, (128, 128), 0)
    column = lax.broadcasted_iota(jnp.int32, (128, 128), 1)
    inner = (row < SEGMENTS) & (column < SEGMENTS)
    hides = (inner & (open_pairs < 0.5)) | (column == 127)
    hidden_ref[...] = jnp.where(hides, HIDDEN, 0.0).astype(jnp.bfloat16)

    starts, ends = bounds[0:1, :], bounds[1:2, :]

    def flags(condition):
        return jnp.where(condition, 1.0, 0.0).astype(jnp.bfloat16)

    def dot(a, b, turned):
        return lax.dot_general(
            a, b, (((1,), (1 if turned else 0,)), ((), ())), preferred_element_type=jnp.float32
        )

    query_from = rows_from(place, line)
    asks = (starts < query_from + 128) & (ends > query_from) & (line < 4)
    reach = flags(dot(flags(asks), flags(open_pairs > 0.5), False) > 0.5)
    key_from = tile_from(place, row)
    holds = (starts < key_from + 256) & (ends > key_from) & (row < TILES)
    seen = dot(reach, flags(holds), True) > 0.5
    slots = dot(flags(seen), flags(row < column), False)
    slots_ref[...] = slots.astype(jnp.int32)
    number = lane.astype(jnp.float32).astype(jnp.bfloat16)
    result = jnp.zeros((8, 128), jnp.float32)
    for t in range(4):
        mine = jnp.where(seen[t : t + 1, :], slots[t : t + 1, :], -1.0)
        chosen = flags(mine == row.astype(jnp.float32))
        result = jnp.where(line == t, dot(number, chosen, True), result)
    tiles_ref[...] = result.astype(jnp.int32)


def plan_call(place, lengths, allowed):
    smem = pl.BlockSpec(memory_space=pltpu.SMEM)
    vmem = pl.BlockSpec(memory_space=pltpu.VMEM)
    return pl.pallas_call(
        plan,
        out_shape=(
            jax.ShapeDtypeStruct((8, 128), jnp.int32),
            jax.ShapeDtypeStruct((8, 128), jnp.int32),
            jax.ShapeDtypeStruct((8, 128), jnp.int32),
            jax.ShapeDtypeStruct((128, 128), jnp.bfloat16),
        ),
        in_specs=[smem, smem, vmem],
        out_specs=(vmem,) * 4,
        scratch_shapes=[pltpu.VMEM((128, 128), jnp.float32)],
        compiler_params=pltpu.CompilerParams(vmem_limit_bytes=4 * 1024 * 1024),
        name="plan",
    )(place, lengths, allowed)


def merge(place, bounds_ref, gate_ref, kept, kept_sums, got, *out_refs):
    core, zh = place[3], place[4]
    row = lax.broadcasted_iota(jnp.int32, (64, 128), 0)
    for d, out_ref in enumerate(out_refs):
        t = (zh + d) % 4
        position = rows_from(place, t) + core * 64 + row
        gates = jnp.dot(
            one_hot_rows(position, bounds_ref), gate_ref[...], preferred_element_type=jnp.float32
        )
        near = kept_sums[t]
        far = got[t, 384:448, :].astype(jnp.float32)
        far = far + got[t, 448:512, :].astype(jnp.float32)
        far = far + got[t, 512:576, :].astype(jnp.float32)
        near_top, far_top = pltpu.roll(near, 64, 1), pltpu.roll(far, 64, 1)
        top = jnp.maximum(near_top, far_top)
        near_scale, far_scale = jnp.exp2(near_top - top), jnp.exp2(far_top - top)
        sums = near_scale * near + far_scale * far
        near_scale, far_scale = near_scale / sums, far_scale / sums
        for g in range(GROUP):
            at = slice(g * 64, (g + 1) * 64)
            mixed = near_scale[:, g : g + 1] * kept[t, at, :]
            mixed = mixed + far_scale[:, g : g + 1] * got[t, at, :].astype(jnp.float32)
            result = mixed * gates[:, g * 128 : (g + 1) * 128]
            out_ref[:, g * 128 : (g + 1) * 128] = result.astype(jnp.bfloat16)


def merge_call(place, bounds, gate, kept, kept_sums, got):
    vmem = pl.BlockSpec(memory_space=pltpu.VMEM)
    return pl.pallas_call(
        merge,
        out_shape=(jax.ShapeDtypeStruct((64, 768), jnp.bfloat16),) * 4,
        in_specs=[pl.BlockSpec(memory_space=pltpu.SMEM)] + [vmem] * 5,
        out_specs=(vmem,) * 4,
        compiler_params=pltpu.CompilerParams(vmem_limit_bytes=8 * 1024 * 1024),
        name="merge",
    )(place, bounds, gate, kept, kept_sums, got)


def assemble(place, *refs):
    out_ref = refs[-1]
    for d, ref in enumerate(refs[:-1]):
        head = (place[4] + 4 - d) % 4
        out_ref[:, pl.ds(pl.multiple_of(head * 768, 768), 768)] = ref[...]


def assemble_call(place, pieces):
    vmem = pl.BlockSpec(memory_space=pltpu.VMEM)
    return pl.pallas_call(
        assemble,
        out_shape=jax.ShapeDtypeStruct((64, 3072), jnp.bfloat16),
        in_specs=[pl.BlockSpec(memory_space=pltpu.SMEM)] + [vmem] * 4,
        out_specs=vmem,
        compiler_params=pltpu.CompilerParams(vmem_limit_bytes=4 * 1024 * 1024),
        name="assemble",
    )(place, *pieces)


def per_device(
    queries, key_vectors, value_vectors, segment_lengths, segment_allowed, noise_level, gate_table
):
    zh, x, y, zl, core = (lax.axis_index(name) for name in AXES)
    place = jnp.stack([x, y, zl, core, zh]).astype(jnp.int32)

    asked = jnp.transpose(queries.reshape(64, 4, 768), (1, 0, 2))
    asked, key_vectors, value_vectors = lax.optimization_barrier(
        (asked, key_vectors, value_vectors)
    )
    own = lax.all_to_all(asked, "zh", split_axis=0, concat_axis=0, tiled=True)
    other = swap(own, "core")

    column = []
    for d in range(4):
        at = (zh + d) % 4 * HEAD_DIM
        pair = jnp.concatenate(
            [
                lax.dynamic_slice_in_dim(key_vectors, at, HEAD_DIM, 1),
                lax.dynamic_slice_in_dim(value_vectors, at, HEAD_DIM, 1),
            ],
            axis=0,
        )
        column.append(pair if d == 0 else shift_column(pair, d, 0))
        column.append(shift_column(pair, d, 1))

    own_column = jnp.stack(column)


    own_column, segment_lengths, segment_allowed = lax.optimization_barrier(
        (own_column, segment_lengths, segment_allowed)
    )
    line = jnp.stack([own_column] + [shift_cross(own_column, True, by) for by in (1, -1, 2)])
    line = line.reshape(16, 2, 128, 128)
    slots, tiles, bounds, hidden = plan_call(place, segment_lengths, segment_allowed)
    line, noise_level, gate_table = lax.optimization_barrier((line, noise_level, gate_table))
    near = [shift_cross(line, False, by) for by in (1, -1)]

    gate = lax.ppermute(
        gate_table, ("zh", "zl", "core"), [(b * 4 + h, h * 4 + b) for b in range(4) for h in range(4)]
    )
    levels = noise_level[:, None] == jnp.arange(gate.shape[0], dtype=jnp.int32)[None, :]
    levels = jnp.pad(levels.astype(jnp.bfloat16), ((0, 128 - SEGMENTS), (0, 0)))
    gate = jnp.dot(levels, gate, preferred_element_type=jnp.float32).astype(jnp.bfloat16)

    scalars, tables, asked = (slots, tiles, place), (bounds, hidden), (own, other)
    state = attend_call(0, scalars, tables, asked, None, [line])
    after, near, state, gate = lax.optimization_barrier((line, near, state, gate))
    far = shift_cross(after, False, 2)
    state = attend_call(1, scalars, tables, asked, state, near)
    kept, kept_sums, sent = attend_call(2, scalars, tables, asked, state, [far, line] + near)
    got = swap(sent, "core")
    merged = merge_call(place, bounds, gate, kept, kept_sums, got)
    pieces = [merged[0]] + [shift(merged[d], "zh", d) for d in (1, 2, 3)]
    return assemble_call(place, pieces)


def solution(mesh):
    finer = Mesh(mesh.devices.reshape(4, 4, 4, 2, 2), AXES)
    by_token = P(AXES, None)
    in_specs = (by_token, by_token, by_token, P(), P(), P(), P(None, ("zl", "core")))
    return jax.shard_map(
        per_device, mesh=finer, in_specs=in_specs, out_specs=by_token, check_vma=False
    )
```

time: 526 us -> 190 us (0.36); the launches traced: 517 us -> 190 us
  matrix products: 202 us -> 0.19 us
  waiting for transfers between devices: 153 us -> 17.1 us
  Pallas kernels: 0 us -> 123 us
  other arithmetic: 69.8 us -> 0.22 us
  blocking collectives: 48.9 us -> 0 us
  starting transfers between devices: 18.4 us -> 46.3 us
  between operations: 14.2 us -> 0.21 us
  local copies, waits for them, and re-layouts: 9.61 us -> 2.78 us
    dot_general x100 -> x1, matrix products: 202 us -> 0.19 us  [per_device(): jnp.dot(levels, gate, preferred_element_type=jnp.float32)]
    all_gather x2 -> x0, waiting for transfers between devices: 133 us -> none  [the longest x1 90.9 us: per_device(): lax.all_gather(value_vectors, 'cp', axis=0, tiled=True)]
    pallas_call x0 -> x6, Pallas kernels: none -> 123 us  [the longest x3 119 us: attend_call(): pl.pallas_call(body, out_shape=out_shape, in_specs=[smem] * 3 + [vmem] *...]
    all_to_all x4 -> x0, blocking collectives: 48.9 us -> none  [the longest x1 24.3 us: per_device(): lax.all_to_all(attended, 'cp', split_axis=0, concat_axis=0, tiled=True)]
    add x33 -> x0, other arithmetic: 41.4 us -> none  [the longest x32 41.4 us: attend_block(): totals = totals * factor + jnp.sum(weights, axis=-1)]
    ppermute x0 -> x19, starting transfers between devices: none -> 41 us  [the longest x7 16.9 us: shift_column(): return lax.ppermute(x, COLUMN, pairs)]
    reduce_sum x34 -> x0, other arithmetic: 25.2 us -> none  [the longest x32 24.8 us: attend_block(): totals = totals * factor + jnp.sum(weights, axis=-1)]
    all_to_all x2 -> x1, waiting for transfers between devices: 19.9 us -> 2.58 us  [per_device(): own = lax.all_to_all(asked, 'zh', split_axis=0, concat_axis=0, tiled=True)]
  transfers between devices with their start and end apart: 4 -> 20, of which waited for: 4 -> 8; matrix products, arithmetic and copies ran while one was open for 1% -> 0% of each run, Pallas kernels for 0% -> 12%
where the time goes in v2:
time: 190 us
  Pallas kernels  123 us (65%)
  starting transfers between devices  46.3 us (24%)
  waiting for transfers between devices  17.1 us (9%)
  local copies, waits for them, and re-layouts  2.78 us (1%)
    pallas_call x3, Pallas kernels, attend_call(): pl.pallas_call(body, out_shape=out_shape, in_specs=[smem] * 3 + [vmem] *...  119 us
    ppermute x7, starting transfers between devices, shift_column(): return lax.ppermute(x, COLUMN, pairs)  16.9 us
    ppermute x6, starting transfers between devices, shift_cross(): return lax.ppermute(x, ('x', 'y', 'core'), pairs)  12.3 us
    ppermute x3, starting transfers between devices, shift(): return lax.ppermute(x, axis, [(i, (i + by) % 4) for i in range(4)])  9.38 us
    ppermute x7, waiting for transfers between devices, shift_column(): return lax.ppermute(x, COLUMN, pairs)  6.95 us
    all_to_all x1, starting transfers between devices, per_device(): own = lax.all_to_all(asked, 'zh', split_axis=0, concat_axis=0, tiled=True)  5.24 us
  transfers between devices with their start and end apart: 20, of which 8 were waited for; matrix products, arithmetic and copies ran while one was open for 0% of the time, Pallas kernels for 12%

profile of v2, /device:TPU:6, one launch (start us, length us, event | category | flops | bytes accessed | tf_op | source)
XLA Modules:
  0.0 189.9 jit_solution(5482785709211720942)
XLA Ops:
  0.0 0.0 copy-start.1
  0.0 0.0 copy-start
  0.0 0.0 copy-start.2
  0.0 0.0 copy-start.3
  0.1 1.8 copy.11
  1.8 0.8 constant_dynamic-slice_fusion
  2.7 3.3 %collective-permute-start.1 = (bf16[128,128]{1,0:T(8,128)(2,1)S(1)}, bf16[128,128]{1,0:T(8,128)(2,1)S(1)}, u32[]{:S(2)}, u32[]{:S(2)}) collective-permute-start(bf16[128,128]{1,0:T(8,128)(2,1)S(1)} %pad_maximum_fusion.2), channel_id=1, source_target_pairs={{0,64},{2,66},{64,128},{66,130},{128,192},{130,194},{192,0},{194,2... | collective-permute-start | bytes 98312 | tf_op jit(solution)/shard_map/ppermute | solution.py:48
  6.1 4.9 %collective-permute-start.2 = (bf16[128,128]{1,0:T(8,128)(2,1)S(1)}, bf16[128,128]{1,0:T(8,128)(2,1)S(1)}, u32[]{:S(2)}, u32[]{:S(2)}) collective-permute-start(bf16[128,128]{1,0:T(8,128)(2,1)S(1)} %pad_maximum_fusion.2), channel_id=1, source_target_pairs={{0,66},{2,64},{64,130},{66,128},{128,194},{130,192},{192,2},{194,0... | collective-permute-start | bytes 98312 | tf_op jit(solution)/shard_map/ppermute | solution.py:48
  11.0 1.0 collective-permute-start.3
  12.0 3.6 %collective-permute-start.4 = (bf16[128,128]{1,0:T(8,128)(2,1)S(1)}, bf16[128,128]{1,0:T(8,128)(2,1)S(1)}, u32[]{:S(2)}, u32[]{:S(2)}) collective-permute-start(bf16[128,128]{1,0:T(8,128)(2,1)S(1)} %pad_maximum_fusion.3), channel_id=1, source_target_pairs={{0,130},{2,128},{64,194},{66,192},{128,2},{130,0},{192,66},{194,64... | collective-permute-start | bytes 98312 | tf_op jit(solution)/shard_map/ppermute | solution.py:48
  15.6 1.9 %collective-permute-start = (bf16[128,128]{1,0:T(8,128)(2,1)S(1)}, bf16[128,128]{1,0:T(8,128)(2,1)S(1)}, u32[]{:S(2)}, u32[]{:S(2)}) collective-permute-start(bf16[128,128]{1,0:T(8,128)(2,1)S(1)} %pad_maximum_fusion.1), channel_id=1, source_target_pairs={{0,2},{2,0},{64,66},{66,64},{128,130},{130,128},{192,194},{194,192... | collective-permute-start | bytes 98312 | tf_op jit(solution)/shard_map/ppermute | solution.py:48
  17.5 2.3 %collective-permute-done = bf16[128,128]{1,0:T(8,128)(2,1)S(1)} collective-permute-done((bf16[128,128]{1,0:T(8,128)(2,1)S(1)}, bf16[128,128]{1,0:T(8,128)(2,1)S(1)}, u32[]{:S(2)}, u32[]{:S(2)}) %collective-permute-start) | collective-permute-done | bytes 32800 | tf_op jit(solution)/shard_map/ppermute | solution.py:48
  19.8 0.2 collective-permute-start.5
  20.0 0.0 collective-permute-done.1
  20.0 2.0 %collective-permute-start.6 = (bf16[128,128]{1,0:T(8,128)(2,1)S(1)}, bf16[128,128]{1,0:T(8,128)(2,1)S(1)}, u32[]{:S(2)}, u32[]{:S(2)}) collective-permute-start(bf16[128,128]{1,0:T(8,128)(2,1)S(1)} %pad_maximum_fusion.4), channel_id=1, source_target_pairs={{0,194},{2,192},{64,2},{66,0},{128,66},{130,64},{192,130},{194,128... | collective-permute-start | bytes 98312 | tf_op jit(solution)/shard_map/ppermute | solution.py:48
  22.0 0.0 collective-permute-done.2
  22.0 0.0 collective-permute-done.3
  22.0 0.0 collective-permute-done.4
  22.0 2.6 %collective-permute-done.5 = bf16[128,128]{1,0:T(8,128)(2,1)S(1)} collective-permute-done((bf16[128,128]{1,0:T(8,128)(2,1)S(1)}, bf16[128,128]{1,0:T(8,128)(2,1)S(1)}, u32[]{:S(2)}, u32[]{:S(2)}) %collective-permute-start.5) | collective-permute-done | bytes 32800 | tf_op jit(solution)/shard_map/ppermute | solution.py:48
  24.6 2.1 %collective-permute-done.6 = bf16[128,128]{1,0:T(8,128)(2,1)S(1)} collective-permute-done((bf16[128,128]{1,0:T(8,128)(2,1)S(1)}, bf16[128,128]{1,0:T(8,128)(2,1)S(1)}, u32[]{:S(2)}, u32[]{:S(2)}) %collective-permute-start.6) | collective-permute-done | bytes 32800 | tf_op jit(solution)/shard_map/ppermute | solution.py:48
  26.7 0.5 collective-permute-start.7
  27.2 1.5 collective-permute-start.8
  28.8 1.4 collective-permute-start.9
  30.2 5.2 %all-to-all-start = ((bf16[4,64,768]{2,1,0:T(8,128)(2,1)}), bf16[4,64,768]{2,1,0:T(8,128)(2,1)S(1)}, u32[]{:S(2)}, u32[]{:S(2)}) async-start(bf16[4,64,768]{2,1,0:T(8,128)(2,1)} %bitcast.33), calls=%async_computation | async-start | bytes 786432 | tf_op jit(solution)/shard_map/all_to_all | solution.py:446
  35.4 0.0 collective-permute-done.7
  35.4 2.2 %collective-permute-done.8 = bf16[8,128,128]{2,1,0:T(8,128)(2,1)S(1)} collective-permute-done((bf16[8,128,128]{2,1,0:T(8,128)(2,1)S(1)}, bf16[8,128,128]{2,1,0:T(8,128)(2,1)S(1)}, u32[]{:S(2)}, u32[]{:S(2)}) %collective-permute-start.8) | collective-permute-done | bytes 262176 | tf_op jit(solution)/shard_map/ppermute | solution.py:43
  37.6 0.0 collective-permute-done.9
  37.6 0.1 pad_maximum_fusion
  37.7 1.7 collective-permute-start.10
  39.4 2.2 %collective-permute-start.11 = (bf16[16,2,128,128]{3,2,1,0:T(8,128)(2,1)S(1)}, bf16[16,2,128,128]{3,2,1,0:T(8,128)(2,1)}, u32[]{:S(2)}, u32[]{:S(2)}) collective-permute-start(bf16[16,2,128,128]{3,2,1,0:T(8,128)(2,1)S(1)} %bitcast.35), channel_id=1, source_target_pairs={{0,12},{1,49},{4,0},{5,53},{8,4},{9,57},{12,8},{13,61},{16,28},{17... | collective-permute-start | bytes 3145736 | tf_op jit(solution)/shard_map/ppermute | solution.py:43
  41.6 0.1 stack.65.place.refs_2_
  41.7 0.0 copy-done.1
  41.7 0.0 copy-done
  41.7 1.1 plan.1
  42.8 0.0 copy-done.3
  42.8 0.7 collective-permute-start.13
  43.4 2.6 %all-to-all-done.refs_5_ = bf16[4,64,768]{2,1,0:T(8,128)(2,1)S(1)} async-done(((bf16[4,64,768]{2,1,0:T(8,128)(2,1)}), bf16[4,64,768]{2,1,0:T(8,128)(2,1)S(1)}, u32[]{:S(2)}, u32[]{:S(2)}) %all-to-all-start) | async-done | bytes 393248 | tf_op jit(solution)/shard_map/all_to_all | solution.py:446
  46.0 1.6 collective-permute-start.12
  47.6 0.0 copy-done.2
  47.6 0.1 iota_compare_fusion
  47.7 0.0 collective-permute-done.13
  47.7 0.2 convolution_convert_fusion.gate_ref
  47.9 1.1 collective-permute-done.12.refs_6_
  49.0 8.1 %attend0.1.refs_7_ = f32[4,768,256]{2,1,0:T(8,128)S(1)} custom-call(s32[8,128]{1,0:T(8,128)S(1)} %get-tuple-element.37.refs_0_, s32[8,128]{1,0:T(8,128)S(1)} %get-tuple-element.38.refs_1_, s32[5]{0:T(128)S(1)} %stack.65.place.refs_2_, s32[8,128]{1,0:T(8,128)S(1)} %get-tuple-element.34.refs_3_.bounds_ref, bf16[128,128]{1,0:T(8,128)(2,1)S(1)} %get-tuple-element.39.refs_4_, ...), custom_call_target="tpu_custom_call" | custom-call | flops 3000000000 | bytes 8388608 | tf_op jit(solution)/shard_map/attend0/pallas_call | solution.py:280
  57.1 0.0 collective-permute-done.10.refs_8_.refs_10_
  57.2 0.0 collective-permute-done.11.refs_9_.refs_11_
  57.2 5.1 %collective-permute-start.14 = (bf16[16,2,128,128]{3,2,1,0:T(8,128)(2,1)S(1)}, bf16[16,2,128,128]{3,2,1,0:T(8,128)(2,1)S(1)}, u32[]{:S(2)}, u32[]{:S(2)}) collective-permute-start(bf16[16,2,128,128]{3,2,1,0:T(8,128)(2,1)S(1)} %bitcast.37), channel_id=1, source_target_pairs={{0,8},{1,33},{4,12},{5,37},{8,0},{9,41},{12,4},{13,45},{16,24},{17... | collective-permute-start | bytes 3145736 | tf_op jit(solution)/shard_map/ppermute | solution.py:43
  62.2 13.4 %attend1.1.refs_7_ = f32[4,768,256]{2,1,0:T(8,128)S(1)} custom-call(s32[8,128]{1,0:T(8,128)S(1)} %get-tuple-element.37.refs_0_, s32[8,128]{1,0:T(8,128)S(1)} %get-tuple-element.38.refs_1_, s32[5]{0:T(128)S(1)} %stack.65.place.refs_2_, s32[8,128]{1,0:T(8,128)S(1)} %get-tuple-element.34.refs_3_.bounds_ref, bf16[128,128]{1,0:T(8,128)(2,1)S(1)} %get-tuple-element.39.refs_4_, ...), custom_call_target="tpu_custom_call" | custom-call | flops 6000000000 | bytes 8388608 | tf_op jit(solution)/shard_map/attend1/pallas_call | solution.py:280
  75.6 0.0 collective-permute-done.14.refs_8_
  75.6 97.4 %attend2.1 = (f32[4,384,128]{2,1,0:T(8,128)S(1)}, f32[4,64,128]{2,1,0:T(8,128)S(1)}, bf16[4,576,128]{2,1,0:T(8,128)(2,1)S(1)}) custom-call(s32[8,128]{1,0:T(8,128)S(1)} %get-tuple-element.37.refs_0_, s32[8,128]{1,0:T(8,128)S(1)} %get-tuple-element.38.refs_1_, s32[5]{0:T(128)S(1)} %stack.65.place.refs_2_, s32[8,128]{1,0:T(8,128)S(1)} %get-tuple-element.34.refs_3_.bounds_ref, ...), custom_call_target="tpu_custom_call" | custom-call | flops 3000000000 | bytes 8388608 | tf_op jit(solution)/shard_map/attend2/pallas_call | solution.py:280
  173.0 0.1 collective-permute-start.15
  173.1 2.0 %collective-permute-done.15.got = bf16[4,576,128]{2,1,0:T(8,128)(2,1)S(1)} collective-permute-done((bf16[4,576,128]{2,1,0:T(8,128)(2,1)S(1)}, bf16[4,576,128]{2,1,0:T(8,128)(2,1)S(1)}, u32[]{:S(2)}, u32[]{:S(2)}) %collective-permute-start.15) | collective-permute-done | bytes 589856 | tf_op jit(solution)/shard_map/ppermute | solution.py:32
  175.1 1.7 merge.1
  176.8 2.8 %collective-permute-start.16 = (bf16[64,768]{1,0:T(8,128)(2,1)S(1)}, bf16[64,768]{1,0:T(8,128)(2,1)S(1)}, u32[]{:S(2)}, u32[]{:S(2)}) collective-permute-start(bf16[64,768]{1,0:T(8,128)(2,1)S(1)} %get-tuple-element.52), channel_id=1, source_target_pairs={{0,64},{64,128},{128,192},{192,0},{1,65},{65,129},{129,193},{193,1... | collective-permute-start | bytes 294920 | tf_op jit(solution)/shard_map/ppermute | solution.py:28
  179.7 2.5 %collective-permute-start.17 = (bf16[64,768]{1,0:T(8,128)(2,1)S(1)}, bf16[64,768]{1,0:T(8,128)(2,1)S(1)}, u32[]{:S(2)}, u32[]{:S(2)}) collective-permute-start(bf16[64,768]{1,0:T(8,128)(2,1)S(1)} %get-tuple-element.53), channel_id=1, source_target_pairs={{0,128},{64,192},{128,0},{192,64},{1,129},{65,193},{129,1},{193,65... | collective-permute-start | bytes 294920 | tf_op jit(solution)/shard_map/ppermute | solution.py:28
  182.2 4.0 %collective-permute-start.18 = (bf16[64,768]{1,0:T(8,128)(2,1)S(1)}, bf16[64,768]{1,0:T(8,128)(2,1)S(1)}, u32[]{:S(2)}, u32[]{:S(2)}) collective-permute-start(bf16[64,768]{1,0:T(8,128)(2,1)S(1)} %get-tuple-element.54), channel_id=1, source_target_pairs={{0,192},{64,0},{128,64},{192,128},{1,193},{65,1},{129,65},{193,129... | collective-permute-start | bytes 294920 | tf_op jit(solution)/shard_map/ppermute | solution.py:28
  186.2 0.0 collective-permute-done.16.refs_1_
  186.2 2.3 %collective-permute-done.17.refs_2_ = bf16[64,768]{1,0:T(8,128)(2,1)S(1)} collective-permute-done((bf16[64,768]{1,0:T(8,128)(2,1)S(1)}, bf16[64,768]{1,0:T(8,128)(2,1)S(1)}, u32[]{:S(2)}, u32[]{:S(2)}) %collective-permute-start.17) | collective-permute-done | bytes 98336 | tf_op jit(solution)/shard_map/ppermute | solution.py:28
  188.5 0.0 collective-permute-done.18.refs_3_
  188.5 1.3 assemble.1
  (12 shorter events, 0.1 us)
Async XLA Ops:
  0.0 41.7 %copy-start.1 = (s32[16]{0:T(128)S(1)}, s32[16]{0:T(128)}, u32[]{:S(2)}) copy-start(s32[16]{0:T(128)} %lengths) | copy-start | bytes 196
  0.0 41.7 %copy-start = (s32[16,16]{1,0:T(8,128)S(1)}, s32[16,16]{1,0:T(8,128)}, u32[]{:S(2)}) copy-start(s32[16,16]{1,0:T(8,128)} %allowed) | copy-start | bytes 3076
  0.0 47.6 %copy-start.2 = (s32[16]{0:T(128)S(1)}, s32[16]{0:T(128)}, u32[]{:S(2)}) copy-start(s32[16]{0:T(128)} %param.12) | copy-start | bytes 196
  0.0 42.8 %copy-start.3 = (bf16[16,768]{1,0:T(8,128)(2,1)S(1)}, bf16[16,768]{1,0:T(8,128)(2,1)}, u32[]{:S(2)}) copy-start(bf16[16,768]{1,0:T(8,128)(2,1)} %param.13) | copy-start | bytes 73732
  2.7 17.3 %collective-permute-start.1 = (bf16[128,128]{1,0:T(8,128)(2,1)S(1)}, bf16[128,128]{1,0:T(8,128)(2,1)S(1)}, u32[]{:S(2)}, u32[]{:S(2)}) collective-permute-start(bf16[128,128]{1,0:T(8,128)(2,1)S(1)} %pad_maximum_fusion.2), channel_id=1, source_target_pairs={{0,64},{2,66},{64,128},{66,130},{128,192},{130,194},{192,0},{194,2... | collective-permute-start | bytes 98312 | tf_op jit(solution)/shard_map/ppermute | solution.py:48
  6.1 15.9 %collective-permute-start.2 = (bf16[128,128]{1,0:T(8,128)(2,1)S(1)}, bf16[128,128]{1,0:T(8,128)(2,1)S(1)}, u32[]{:S(2)}, u32[]{:S(2)}) collective-permute-start(bf16[128,128]{1,0:T(8,128)(2,1)S(1)} %pad_maximum_fusion.2), channel_id=1, source_target_pairs={{0,66},{2,64},{64,130},{66,128},{128,194},{130,192},{192,2},{194,0... | collective-permute-start | bytes 98312 | tf_op jit(solution)/shard_map/ppermute | solution.py:48
  11.0 11.0 %collective-permute-start.3 = (bf16[128,128]{1,0:T(8,128)(2,1)S(1)}, bf16[128,128]{1,0:T(8,128)(2,1)S(1)}, u32[]{:S(2)}, u32[]{:S(2)}) collective-permute-start(bf16[128,128]{1,0:T(8,128)(2,1)S(1)} %pad_maximum_fusion.3), channel_id=1, source_target_pairs={{0,128},{2,130},{64,192},{66,194},{128,0},{130,2},{192,64},{194,66... | collective-permute-start | bytes 98312 | tf_op jit(solution)/shard_map/ppermute | solution.py:48
  12.0 10.0 %collective-permute-start.4 = (bf16[128,128]{1,0:T(8,128)(2,1)S(1)}, bf16[128,128]{1,0:T(8,128)(2,1)S(1)}, u32[]{:S(2)}, u32[]{:S(2)}) collective-permute-start(bf16[128,128]{1,0:T(8,128)(2,1)S(1)} %pad_maximum_fusion.3), channel_id=1, source_target_pairs={{0,130},{2,128},{64,194},{66,192},{128,2},{130,0},{192,66},{194,64... | collective-permute-start | bytes 98312 | tf_op jit(solution)/shard_map/ppermute | solution.py:48
  15.6 4.2 %collective-permute-start = (bf16[128,128]{1,0:T(8,128)(2,1)S(1)}, bf16[128,128]{1,0:T(8,128)(2,1)S(1)}, u32[]{:S(2)}, u32[]{:S(2)}) collective-permute-start(bf16[128,128]{1,0:T(8,128)(2,1)S(1)} %pad_maximum_fusion.1), channel_id=1, source_target_pairs={{0,2},{2,0},{64,66},{66,64},{128,130},{130,128},{192,194},{194,192... | collective-permute-start | bytes 98312 | tf_op jit(solution)/shard_map/ppermute | solution.py:48
  19.8 4.8 %collective-permute-start.5 = (bf16[128,128]{1,0:T(8,128)(2,1)S(1)}, bf16[128,128]{1,0:T(8,128)(2,1)S(1)}, u32[]{:S(2)}, u32[]{:S(2)}) collective-permute-start(bf16[128,128]{1,0:T(8,128)(2,1)S(1)} %pad_maximum_fusion.4), channel_id=1, source_target_pairs={{0,192},{2,194},{64,0},{66,2},{128,64},{130,66},{192,128},{194,130... | collective-permute-start | bytes 98312 | tf_op jit(solution)/shard_map/ppermute | solution.py:48
  20.0 6.7 %collective-permute-start.6 = (bf16[128,128]{1,0:T(8,128)(2,1)S(1)}, bf16[128,128]{1,0:T(8,128)(2,1)S(1)}, u32[]{:S(2)}, u32[]{:S(2)}) collective-permute-start(bf16[128,128]{1,0:T(8,128)(2,1)S(1)} %pad_maximum_fusion.4), channel_id=1, source_target_pairs={{0,194},{2,192},{64,2},{66,0},{128,66},{130,64},{192,130},{194,128... | collective-permute-start | bytes 98312 | tf_op jit(solution)/shard_map/ppermute | solution.py:48
  26.7 8.7 %collective-permute-start.7 = (bf16[8,128,128]{2,1,0:T(8,128)(2,1)S(1)}, bf16[8,128,128]{2,1,0:T(8,128)(2,1)S(1)}, u32[]{:S(2)}, u32[]{:S(2)}) collective-permute-start(bf16[8,128,128]{2,1,0:T(8,128)(2,1)S(1)} %bitcast_dynamic-update-slice_fusion), channel_id=1, source_target_pairs={{0,16},{1,5},{4,20},{5,9},{8,24},{9,13},{12,28},{13,1},{16,32},{17... | collective-permute-start | bytes 786440 | tf_op jit(solution)/shard_map/ppermute | solution.py:43
  27.2 10.4 %collective-permute-start.8 = (bf16[8,128,128]{2,1,0:T(8,128)(2,1)S(1)}, bf16[8,128,128]{2,1,0:T(8,128)(2,1)S(1)}, u32[]{:S(2)}, u32[]{:S(2)}) collective-permute-start(bf16[8,128,128]{2,1,0:T(8,128)(2,1)S(1)} %bitcast_dynamic-update-slice_fusion), channel_id=1, source_target_pairs={{0,48},{1,13},{4,52},{5,1},{8,56},{9,5},{12,60},{13,9},{16,0},{17,... | collective-permute-start | bytes 786440 | tf_op jit(solution)/shard_map/ppermute | solution.py:43
  28.8 8.8 %collective-permute-start.9 = (bf16[8,128,128]{2,1,0:T(8,128)(2,1)S(1)}, bf16[8,128,128]{2,1,0:T(8,128)(2,1)S(1)}, u32[]{:S(2)}, u32[]{:S(2)}) collective-permute-start(bf16[8,128,128]{2,1,0:T(8,128)(2,1)S(1)} %bitcast_dynamic-update-slice_fusion), channel_id=1, source_target_pairs={{0,32},{1,9},{4,36},{5,13},{8,40},{9,1},{12,44},{13,5},{16,48},{17... | collective-permute-start | bytes 786440 | tf_op jit(solution)/shard_map/ppermute | solution.py:43
  30.2 15.9 %all-to-all-start = ((bf16[4,64,768]{2,1,0:T(8,128)(2,1)}), bf16[4,64,768]{2,1,0:T(8,128)(2,1)S(1)}, u32[]{:S(2)}, u32[]{:S(2)}) async-start(bf16[4,64,768]{2,1,0:T(8,128)(2,1)} %bitcast.33), calls=%async_computation | async-start | bytes 786432 | tf_op jit(solution)/shard_map/all_to_all | solution.py:446
  37.7 19.4 %collective-permute-start.10 = (bf16[16,2,128,128]{3,2,1,0:T(8,128)(2,1)S(1)}, bf16[16,2,128,128]{3,2,1,0:T(8,128)(2,1)S(1)}, u32[]{:S(2)}, u32[]{:S(2)}) collective-permute-start(bf16[16,2,128,128]{3,2,1,0:T(8,128)(2,1)S(1)} %bitcast.34), channel_id=1, source_target_pairs={{0,4},{1,17},{4,8},{5,21},{8,12},{9,25},{12,0},{13,29},{16,20},{17... | collective-permute-start | bytes 3145736 | tf_op jit(solution)/shard_map/ppermute | solution.py:43
  39.4 17.8 %collective-permute-start.11 = (bf16[16,2,128,128]{3,2,1,0:T(8,128)(2,1)S(1)}, bf16[16,2,128,128]{3,2,1,0:T(8,128)(2,1)}, u32[]{:S(2)}, u32[]{:S(2)}) collective-permute-start(bf16[16,2,128,128]{3,2,1,0:T(8,128)(2,1)S(1)} %bitcast.35), channel_id=1, source_target_pairs={{0,12},{1,49},{4,0},{5,53},{8,4},{9,57},{12,8},{13,61},{16,28},{17... | collective-permute-start | bytes 3145736 | tf_op jit(solution)/shard_map/ppermute | solution.py:43
  42.8 5.0 %collective-permute-start.13 = (bf16[16,768]{1,0:T(8,128)(2,1)S(1)}, bf16[16,768]{1,0:T(8,128)(2,1)S(1)}, u32[]{:S(2)}, u32[]{:S(2)}) collective-permute-start(bf16[16,768]{1,0:T(8,128)(2,1)S(1)} %copy-done.3), channel_id=1, source_target_pairs={{0,0},{1,64},{2,128},{3,192},{64,1},{65,65},{66,129},{67,193},{128... | collective-permute-start | bytes 73736 | tf_op jit(solution)/shard_map/ppermute | solution.py:474
  46.0 3.0 %collective-permute-start.12 = (bf16[4,64,768]{2,1,0:T(8,128)(2,1)S(1)}, bf16[4,64,768]{2,1,0:T(8,128)(2,1)S(1)}, u32[]{:S(2)}, u32[]{:S(2)}) collective-permute-start(bf16[4,64,768]{2,1,0:T(8,128)(2,1)S(1)} %all-to-all-done.refs_5_), channel_id=1, source_target_pairs={{0,1},{1,0},{2,3},{3,2},{4,5},{5,4},{6,7},{7,6},{8,9},{9,8},{10,11... | collective-permute-start | bytes 1179656 | tf_op jit(solution)/shard_map/ppermute | solution.py:32
  57.2 18.4 %collective-permute-start.14 = (bf16[16,2,128,128]{3,2,1,0:T(8,128)(2,1)S(1)}, bf16[16,2,128,128]{3,2,1,0:T(8,128)(2,1)S(1)}, u32[]{:S(2)}, u32[]{:S(2)}) collective-permute-start(bf16[16,2,128,128]{3,2,1,0:T(8,128)(2,1)S(1)} %bitcast.37), channel_id=1, source_target_pairs={{0,8},{1,33},{4,12},{5,37},{8,0},{9,41},{12,4},{13,45},{16,24},{17... | collective-permute-start | bytes 3145736 | tf_op jit(solution)/shard_map/ppermute | solution.py:43
  173.0 2.1 %collective-permute-start.15 = (bf16[4,576,128]{2,1,0:T(8,128)(2,1)S(1)}, bf16[4,576,128]{2,1,0:T(8,128)(2,1)S(1)}, u32[]{:S(2)}, u32[]{:S(2)}) collective-permute-start(bf16[4,576,128]{2,1,0:T(8,128)(2,1)S(1)} %get-tuple-element.50), channel_id=1, source_target_pairs={{0,1},{1,0},{2,3},{3,2},{4,5},{5,4},{6,7},{7,6},{8,9},{9,8},{10,11... | collective-permute-start | bytes 1769480 | tf_op jit(solution)/shard_map/ppermute | solution.py:32
  176.8 9.4 %collective-permute-start.16 = (bf16[64,768]{1,0:T(8,128)(2,1)S(1)}, bf16[64,768]{1,0:T(8,128)(2,1)S(1)}, u32[]{:S(2)}, u32[]{:S(2)}) collective-permute-start(bf16[64,768]{1,0:T(8,128)(2,1)S(1)} %get-tuple-element.52), channel_id=1, source_target_pairs={{0,64},{64,128},{128,192},{192,0},{1,65},{65,129},{129,193},{193,1... | collective-permute-start | bytes 294920 | tf_op jit(solution)/shard_map/ppermute | solution.py:28
  179.7 8.9 %collective-permute-start.17 = (bf16[64,768]{1,0:T(8,128)(2,1)S(1)}, bf16[64,768]{1,0:T(8,128)(2,1)S(1)}, u32[]{:S(2)}, u32[]{:S(2)}) collective-permute-start(bf16[64,768]{1,0:T(8,128)(2,1)S(1)} %get-tuple-element.53), channel_id=1, source_target_pairs={{0,128},{64,192},{128,0},{192,64},{1,129},{65,193},{129,1},{193,65... | collective-permute-start | bytes 294920 | tf_op jit(solution)/shard_map/ppermute | solution.py:28
  182.2 6.4 %collective-permute-start.18 = (bf16[64,768]{1,0:T(8,128)(2,1)S(1)}, bf16[64,768]{1,0:T(8,128)(2,1)S(1)}, u32[]{:S(2)}, u32[]{:S(2)}) collective-permute-start(bf16[64,768]{1,0:T(8,128)(2,1)S(1)} %get-tuple-element.54), channel_id=1, source_target_pairs={{0,192},{64,0},{128,64},{192,128},{1,193},{65,1},{129,65},{193,129... | collective-permute-start | bytes 294920 | tf_op jit(solution)/shard_map/ppermute | solution.py:28

commit v3 on v2

--- a/solution.py
+++ b/solution.py
@@ -19,7 +19,8 @@
 TILE = 128
 TILES = 64
 LONG, SHORT = 8, 4
-STAGES = ((0, 16), (16, 32), (48, 16))
+HALF = 8
+STAGES = ((0, HALF), (HALF, 48 - HALF), (48, 16))
 LAST = len(STAGES) - 1
 AWAY = (0, 3, 1, 2)
 
@@ -54,23 +55,25 @@
 
 
 def attend(stage, *refs):
-    last = stage == LAST
+    first, last = stage == 0, stage == LAST
     base, count = STAGES[stage]
-    parts_count = (1, 2, 4)[stage]
-    fast_parts = (1, 2, 1)[stage]
-    slots, tiles, place, bounds_ref, hidden_ref, own_ref, other_ref = refs[:7]
-    refs = refs[7:]
-    if stage > 0:
-        state_ref, refs = refs[0], refs[1:]
+    parts_count = (1, 3, 4)[stage]
+    slots, tiles, marks, row_marks = refs[:4]
+    refs = refs[4:]
+    if first:
+        own_ref, other_ref, refs = refs[0], refs[1], refs[2:]
+    else:
+        rows, state_ref, refs = refs[0], refs[1], refs[2:]
     parts, refs = refs[:parts_count], refs[parts_count:]
+    if first:
+        rows, refs = refs[0], refs[1:]
     if last:
         kept_ref, kept_sums_ref, sent_ref, refs = *refs[:3], refs[3:]
     else:
         result_ref, refs = refs[0], refs[1:]
-    keys, values, marks, ones, rows, total, arrived = refs[:7]
+    keys, values, ones, arrived = refs[:4]
     if last:
-        peak, faults = refs[7:]
-    x, y, zl, core, zh = place[0], place[1], place[2], place[3], place[4]
+        total, peak, faults = refs[4:]
     blank_tile = TILES if last else count
 
     def bring(some, at):
@@ -90,43 +93,34 @@
             copy.start()
         return copies
 
-    def mark_keys(first, start, number):
-        row = lax.broadcasted_iota(jnp.int32, (TILE, 128), 0)
-        inner = ((row // 64) ^ zl) * 128 + core * 64 + row % 64
-
-        def mark(n, _):
-            position = tile_from(place, start + n) + inner
-            at = first + n
-            marks[at] = one_hot_rows(position, bounds_ref)
-            return 0
-
-        lax.fori_loop(0, number, mark, 0)
-
-    copies = bring(parts[:fast_parts], 0)
-    mark_keys(0, base, count)
-    blank = (lax.broadcasted_iota(jnp.int32, (TILE, 128), 1) == 127).astype(jnp.float32)
-    marks[blank_tile] = blank.astype(jnp.bfloat16)
+    if first:
+        wanted = [parts[0].at[pl.ds(0, HALF)]]
+    elif last:
+        wanted = parts[:1]
+    else:
+        wanted = [parts[0].at[pl.ds(HALF, 16 - HALF)]] + list(parts[1:])
+    copies = bring(wanted, 0)
     keys[blank_tile] = jnp.zeros((2, 64, 128), jnp.bfloat16)
     values[blank_tile] = jnp.zeros((2, 64, 128), jnp.bfloat16)
     ones[...] = jnp.ones_like(ones)
     if last:
         faults[...] = jnp.zeros_like(faults)
+    if first:
+        for t in range(4):
+            for half, ref in enumerate((own_ref, other_ref)):
+                mark = row_marks[t, half]
+                for g in range(GROUP):
+                    at = pl.ds(half * 384 + g * 64, 64)
+                    rows[t, at, 0:128] = ref[t, :, g * 128 : (g + 1) * 128]
+                    rows[t, at, 128:256] = mark
     for copy in copies:
         copy.wait()
 
-    def prepare(t):
-        row = lax.broadcasted_iota(jnp.int32, (64, 128), 0)
-        for half, (ref, side) in enumerate(((own_ref, core), (other_ref, 1 - core))):
-            position = rows_from(place, t) + side * 64 + row
-            mark = jnp.dot(
-                one_hot_rows(position, bounds_ref),
-                hidden_ref[...],
-                preferred_element_type=jnp.float32,
-            ).astype(jnp.bfloat16)
-            for g in range(GROUP):
-                at = pl.ds(half * 384 + g * 64, 64)
-                rows[at, 0:128] = ref[t, :, g * 128 : (g + 1) * 128]
-                rows[at, 128:256] = mark
+    def mark_of(n):
+        if last:
+            n = jnp.where(n < count, n + base, jnp.where(n < TILES, n - count, TILES))
+            return marks[n]
+        return marks[jnp.where(n < count, n + base, TILES)]
 
     def load(ref, beside, numbers):
         wide = [
@@ -135,14 +129,14 @@
         return jnp.concatenate(wide, axis=0)
 
     def load_keys(numbers):
-        return load(keys, lambda n: marks[n], numbers)
+        return load(keys, mark_of, numbers)
 
     def load_values(numbers):
         return load(values, lambda n: ones[...], numbers)
 
-    def score(numbers):
+    def score(t, numbers):
         return lax.dot_general(
-            rows[...],
+            rows[t],
             load_keys(numbers),
             (((1,), (1,)), ((), ())),
             preferred_element_type=jnp.float32,
@@ -168,23 +162,29 @@
                     both = both - piece.astype(jnp.float32)
 
     def quick(t, _):
-        prepare(t)
-        total[...] = jnp.zeros_like(total) if stage == 0 else state_ref[t]
+        if last:
+            total[...] = state_ref[t]
+            sum_ref = total
+        elif first:
+            result_ref[t] = jnp.zeros((768, 256), jnp.float32)
+            sum_ref = result_ref.at[t]
+        else:
+            sum_ref = result_ref.at[t]
         begin, end = slots[t, base], slots[t, base + count]
         seen = end - begin
 
-        def numbers(first, width):
+        def numbers(from_slot, width):
             picked = []
             for j in range(width):
-                inside = first + j < end
-                at = jnp.where(inside, first + j, 0)
+                inside = from_slot + j < end
+                at = jnp.where(inside, from_slot + j, 0)
                 picked.append(jnp.where(inside, tiles[t, at] - base, blank_tile))
             return picked
 
-        def add(first, width):
-            picked = numbers(first, width)
-            weights = jnp.exp2(score(picked) * UNIT).astype(jnp.bfloat16)
-            total[...] += jnp.dot(
+        def add(from_slot, width):
+            picked = numbers(from_slot, width)
+            weights = jnp.exp2(score(t, picked) * UNIT).astype(jnp.bfloat16)
+            sum_ref[...] += jnp.dot(
                 weights, load_values(picked), preferred_element_type=jnp.float32
             )
 
@@ -205,8 +205,6 @@
             bad = jnp.where(good, 0.0, 1.0)
             faults[...] = jnp.maximum(faults[...], jnp.max(bad.reshape(96, 8, 128), axis=0))
             finish(t, False)
-        else:
-            result_ref[t] = total[...]
         return 0
 
     lax.fori_loop(0, 4, quick, 0)
@@ -215,19 +213,17 @@
 
         @pl.when(jnp.max(faults[...]) > 0.0)
         def _():
-            others = bring(parts[fast_parts:], count)
-            mark_keys(count, 0, base)
+            others = bring(parts[1:], count)
             for copy in others:
                 copy.wait()
 
             def careful(t, _):
-                prepare(t)
                 total[...] = jnp.zeros_like(total)
                 peak[...] = jnp.full_like(peak, -3e38)
 
                 def step(i, _):
                     picked = [i * LONG + j for j in range(LONG)]
-                    scores = score(picked) * UNIT
+                    scores = score(t, picked) * UNIT
                     before = peak[...]
                     top = jnp.maximum(before, jnp.max(scores, axis=1, keepdims=True))
                     weights = jnp.exp2(scores - top[:, 0:1]).astype(jnp.bfloat16)
@@ -247,8 +243,8 @@
             lax.fori_loop(0, 4, careful, 0)
 
 
-def attend_call(stage, scalars, tables, asked, state, parts):
-    last = stage == LAST
+def attend_call(stage, lists, tables, asked, state, parts):
+    first, last = stage == 0, stage == LAST
     smem = pl.BlockSpec(memory_space=pltpu.SMEM)
     vmem = pl.BlockSpec(memory_space=pltpu.VMEM)
     anywhere = pl.BlockSpec(memory_space=pl.ANY)
@@ -256,22 +252,28 @@
     scratch = [
         pltpu.VMEM((held, 2, 64, 128), jnp.bfloat16),
         pltpu.VMEM((held, 2, 64, 128), jnp.bfloat16),
-        pltpu.VMEM((held, TILE, 128), jnp.bfloat16),
         pltpu.VMEM((TILE, 128), jnp.bfloat16),
-        pltpu.VMEM((768, 256), jnp.bfloat16),
-        pltpu.VMEM((768, 256), jnp.float32),
         pltpu.SemaphoreType.DMA,
     ]
+    state_shape = jax.ShapeDtypeStruct((4, 768, 256), jnp.float32)
+    aliases = {}
     if last:
-        scratch += [pltpu.VMEM((768, 128), jnp.float32), pltpu.VMEM((8, 128), jnp.float32)]
+        scratch += [
+            pltpu.VMEM((768, 256), jnp.float32),
+            pltpu.VMEM((768, 128), jnp.float32),
+            pltpu.VMEM((8, 128), jnp.float32),
+        ]
         out_shape = (
             jax.ShapeDtypeStruct((4, 384, 128), jnp.float32),
             jax.ShapeDtypeStruct((4, 64, 128), jnp.float32),
             jax.ShapeDtypeStruct((4, 576, 128), jnp.bfloat16),
         )
+    elif first:
+        out_shape = (jax.ShapeDtypeStruct((4, 768, 256), jnp.bfloat16), state_shape)
     else:
-        out_shape = jax.ShapeDtypeStruct((4, 768, 256), jnp.float32)
-    states = [] if state is None else [state]
+        out_shape = (state_shape,)
+        aliases = {5: 0}
+    inputs = (*lists, *tables, *(asked if first else state))
 
     def body(*refs):
         attend(stage, *refs)
@@ -280,15 +282,16 @@
     return pl.pallas_call(
         body,
         out_shape=out_shape,
-        in_specs=[smem] * 3 + [vmem] * (4 + len(states)) + [anywhere] * len(parts),
-        out_specs=(vmem,) * 3 if last else vmem,
+        in_specs=[smem] * 2 + [vmem] * 4 + [anywhere] * len(parts),
+        out_specs=(vmem,) * len(out_shape),
         scratch_shapes=scratch,
+        input_output_aliases=aliases,
         compiler_params=pltpu.CompilerParams(vmem_limit_bytes=24 * 1024 * 1024),
         cost_estimate=pl.CostEstimate(
             flops=int(1.2e10 * share), bytes_accessed=8 << 20, transcendentals=0
         ),
         name=f"attend{stage}",
-    )(*scalars, *tables, *asked, *states, *parts)
+    )(*inputs, *parts)
 
 
 def ring_step(v):
@@ -309,7 +312,7 @@
     return t * 4096 + (x * 4 + y) * 256 + zl * 128
 
 
-def plan(place, lengths, allowed, slots_ref, tiles_ref, bounds_ref, hidden_ref, pad):
+def plan(place, lengths, allowed, slots_ref, tiles_ref, bounds_ref, marks_ref, row_marks_ref, pad):
     lane = lax.broadcasted_iota(jnp.int32, (8, 128), 1)
     line = lax.broadcasted_iota(jnp.int32, (8, 128), 0)
     bounds = jnp.zeros((8, 128), jnp.int32)
@@ -328,7 +331,7 @@
     column = lax.broadcasted_iota(jnp.int32, (128, 128), 1)
     inner = (row < SEGMENTS) & (column < SEGMENTS)
     hides = (inner & (open_pairs < 0.5)) | (column == 127)
-    hidden_ref[...] = jnp.where(hides, HIDDEN, 0.0).astype(jnp.bfloat16)
+    hidden = jnp.where(hides, HIDDEN, 0.0).astype(jnp.bfloat16)
 
     starts, ends = bounds[0:1, :], bounds[1:2, :]
 
@@ -356,6 +359,22 @@
         result = jnp.where(line == t, dot(number, chosen, True), result)
     tiles_ref[...] = result.astype(jnp.int32)
 
+    zl, core = place[2], place[3]
+    inner = ((row // 64) ^ zl) * 128 + core * 64 + row % 64
+
+    def mark(n, _):
+        marks_ref[n] = one_hot_rows(tile_from(place, n) + inner, bounds)
+        return 0
+
+    lax.fori_loop(0, TILES, mark, 0)
+    marks_ref[TILES] = flags(column == 127)
+    row = lax.broadcasted_iota(jnp.int32, (64, 128), 0)
+    for t in range(4):
+        for half, side in enumerate((core, 1 - core)):
+            position = rows_from(place, t) + side * 64 + row
+            mark_row = dot(one_hot_rows(position, bounds), hidden, False)
+            row_marks_ref[t, half] = mark_row.astype(jnp.bfloat16)
+
 
 def plan_call(place, lengths, allowed):
     smem = pl.BlockSpec(memory_space=pltpu.SMEM)
@@ -366,10 +385,11 @@
             jax.ShapeDtypeStruct((8, 128), jnp.int32),
             jax.ShapeDtypeStruct((8, 128), jnp.int32),
             jax.ShapeDtypeStruct((8, 128), jnp.int32),
-            jax.ShapeDtypeStruct((128, 128), jnp.bfloat16),
+            jax.ShapeDtypeStruct((TILES + 1, TILE, 128), jnp.bfloat16),
+            jax.ShapeDtypeStruct((4, 2, 64, 128), jnp.bfloat16),
         ),
         in_specs=[smem, smem, vmem],
-        out_specs=(vmem,) * 4,
+        out_specs=(vmem,) * 5,
         scratch_shapes=[pltpu.VMEM((128, 128), jnp.float32)],
         compiler_params=pltpu.CompilerParams(vmem_limit_bytes=4 * 1024 * 1024),
         name="plan",
@@ -439,13 +459,6 @@
     zh, x, y, zl, core = (lax.axis_index(name) for name in AXES)
     place = jnp.stack([x, y, zl, core, zh]).astype(jnp.int32)
 
-    asked = jnp.transpose(queries.reshape(64, 4, 768), (1, 0, 2))
-    asked, key_vectors, value_vectors = lax.optimization_barrier(
-        (asked, key_vectors, value_vectors)
-    )
-    own = lax.all_to_all(asked, "zh", split_axis=0, concat_axis=0, tiled=True)
-    other = swap(own, "core")
-
     column = []
     for d in range(4):
         at = (zh + d) % 4 * HEAD_DIM
@@ -457,9 +470,19 @@
             axis=0,
         )
         column.append(pair if d == 0 else shift_column(pair, d, 0))
-        column.append(shift_column(pair, d, 1))
+        if d > 0:
+            column.append(shift_column(pair, d, 1))
+        else:
+            both = jnp.concatenate([pair, gate_table.reshape(96, 128)], axis=0)
+            both = shift_column(both, 0, 1)
+            column.append(both[:128])
+            gates = jnp.stack([gate_table, both[128:].reshape(16, 768)])
 
     own_column = jnp.stack(column)
+
+    asked = jnp.transpose(queries.reshape(64, 4, 768), (1, 0, 2))
+    own_column, asked = lax.optimization_barrier((own_column, asked))
+    own = lax.all_to_all(asked, "zh", split_axis=0, concat_axis=0, tiled=True)
 
 
     own_column, segment_lengths, segment_allowed = lax.optimization_barrier(
@@ -467,23 +490,30 @@
     )
     line = jnp.stack([own_column] + [shift_cross(own_column, True, by) for by in (1, -1, 2)])
     line = line.reshape(16, 2, 128, 128)
-    slots, tiles, bounds, hidden = plan_call(place, segment_lengths, segment_allowed)
-    line, noise_level, gate_table = lax.optimization_barrier((line, noise_level, gate_table))
+    slots, tiles, bounds, marks, row_marks = plan_call(place, segment_lengths, segment_allowed)
     near = [shift_cross(line, False, by) for by in (1, -1)]
 
-    gate = lax.ppermute(
-        gate_table, ("zh", "zl", "core"), [(b * 4 + h, h * 4 + b) for b in range(4) for h in range(4)]
+    own, slots, tiles, bounds, marks, row_marks = lax.optimization_barrier(
+        (own, slots, tiles, bounds, marks, row_marks)
     )
+    other = swap(own, "core")
+    own, noise_level, gates = lax.optimization_barrier((own, noise_level, gates))
+
+    swapped = swap(gates, "core")
+    which = ((zh // 2) ^ zl) + 2 * ((zh % 2) ^ core)
+    gate = lax.dynamic_index_in_dim(jnp.concatenate([gates, swapped]), which, 0, keepdims=False)
     levels = noise_level[:, None] == jnp.arange(gate.shape[0], dtype=jnp.int32)[None, :]
     levels = jnp.pad(levels.astype(jnp.bfloat16), ((0, 128 - SEGMENTS), (0, 0)))
     gate = jnp.dot(levels, gate, preferred_element_type=jnp.float32).astype(jnp.bfloat16)
 
-    scalars, tables, asked = (slots, tiles, place), (bounds, hidden), (own, other)
-    state = attend_call(0, scalars, tables, asked, None, [line])
+    lists, tables = (slots, tiles), (marks, row_marks)
+    rows, state = attend_call(0, lists, tables, (own, other), None, [line])
     after, near, state, gate = lax.optimization_barrier((line, near, state, gate))
     far = shift_cross(after, False, 2)
-    state = attend_call(1, scalars, tables, asked, state, near)
-    kept, kept_sums, sent = attend_call(2, scalars, tables, asked, state, [far, line] + near)
+    (state,) = attend_call(1, lists, tables, None, (rows, state), [line] + near)
+    kept, kept_sums, sent = attend_call(
+        2, lists, tables, None, (rows, state), [far, line] + near
+    )
     got = swap(sent, "core")
     merged = merge_call(place, bounds, gate, kept, kept_sums, got)
     pieces = [merged[0]] + [shift(merged[d], "zh", d) for d in (1, 2, 3)]

time: 190 us -> 185 us (0.974)
  starting transfers between devices: 46.3 us -> 42.8 us
  waiting for transfers between devices: 17.1 us -> 13.9 us
    pallas_call x3, Pallas kernels: 119 us -> 115 us  [attend_call(): pl.pallas_call(body, out_shape=out_shape, in_specs=[smem] * 2 + [vmem] *...]
    pallas_call x1, Pallas kernels: 1.09 us -> 3.99 us  [plan_call(): pl.pallas_call(plan, out_shape=(jax.ShapeDtypeStruct((8, 128), jnp.int32)...]
  transfers between devices with their start and end apart: 20 -> 20, of which waited for: 8 -> 8; matrix products, arithmetic and copies ran while one was open for 0% -> 2% of each run, Pallas kernels for 12% -> 13%
where the time goes in v3:
time: 185 us; the launch traced here: 183 us
  Pallas kernels  122 us (66%)
  starting transfers between devices  42.8 us (23%)
  waiting for transfers between devices  13.9 us (8%)
  local copies, waits for them, and re-layouts  3.63 us (2%)
    pallas_call x3, Pallas kernels, attend_call(): pl.pallas_call(body, out_shape=out_shape, in_specs=[smem] * 2 + [vmem] *...  115 us
    ppermute x7, starting transfers between devices, shift_column(): return lax.ppermute(x, COLUMN, pairs)  17 us
    ppermute x6, starting transfers between devices, shift_cross(): return lax.ppermute(x, ('x', 'y', 'core'), pairs)  11.1 us
    ppermute x3, starting transfers between devices, shift(): return lax.ppermute(x, axis, [(i, (i + by) % 4) for i in range(4)])  8.75 us
    ppermute x7, waiting for transfers between devices, shift_column(): return lax.ppermute(x, COLUMN, pairs)  5.52 us
    all_to_all x1, starting transfers between devices, per_device(): own = lax.all_to_all(asked, 'zh', split_axis=0, concat_axis=0, tiled=True)  5.15 us
    pallas_call x1, Pallas kernels, plan_call(): pl.pallas_call(plan, out_shape=(jax.ShapeDtypeStruct((8, 128), jnp.int32)...  3.99 us
  transfers between devices with their start and end apart: 20, of which 8 were waited for; matrix products, arithmetic and copies ran while one was open for 2% of the time, Pallas kernels for 13%

profile of v3, /device:TPU:6, one launch (start us, length us, event | category | flops | bytes accessed | tf_op | source)
XLA Modules:
  0.0 183.4 jit_solution(12903789526674272981)
XLA Ops:
  0.0 0.0 copy-start.2
  0.0 0.0 copy-start.1
  0.0 0.0 copy-start
  0.0 0.0 copy-start.3
  0.1 0.9 constant_dynamic-slice_fusion
  1.0 3.3 %collective-permute-start.1 = (bf16[128,128]{1,0:T(8,128)(2,1)S(1)}, bf16[128,128]{1,0:T(8,128)(2,1)S(1)}, u32[]{:S(2)}, u32[]{:S(2)}) collective-permute-start(bf16[128,128]{1,0:T(8,128)(2,1)S(1)} %pad_maximum_fusion.3), channel_id=1, source_target_pairs={{0,64},{2,66},{64,128},{66,130},{128,192},{130,194},{192,0},{194,2... | collective-permute-start | bytes 98312 | tf_op jit(solution)/shard_map/ppermute | solution.py:49
  4.3 4.9 %collective-permute-start.2 = (bf16[128,128]{1,0:T(8,128)(2,1)S(1)}, bf16[128,128]{1,0:T(8,128)(2,1)S(1)}, u32[]{:S(2)}, u32[]{:S(2)}) collective-permute-start(bf16[128,128]{1,0:T(8,128)(2,1)S(1)} %pad_maximum_fusion.3), channel_id=1, source_target_pairs={{0,66},{2,64},{64,130},{66,128},{128,194},{130,192},{192,2},{194,0... | collective-permute-start | bytes 98312 | tf_op jit(solution)/shard_map/ppermute | solution.py:49
  9.2 1.0 collective-permute-start.3
  10.2 3.6 %collective-permute-start.4 = (bf16[128,128]{1,0:T(8,128)(2,1)S(1)}, bf16[128,128]{1,0:T(8,128)(2,1)S(1)}, u32[]{:S(2)}, u32[]{:S(2)}) collective-permute-start(bf16[128,128]{1,0:T(8,128)(2,1)S(1)} %pad_maximum_fusion.4), channel_id=1, source_target_pairs={{0,130},{2,128},{64,194},{66,192},{128,2},{130,0},{192,66},{194,64... | collective-permute-start | bytes 98312 | tf_op jit(solution)/shard_map/ppermute | solution.py:49
  13.8 0.8 reshape.10
  14.6 2.0 %collective-permute-start = (bf16[224,128]{1,0:T(8,128)(2,1)S(1)}, bf16[224,128]{1,0:T(8,128)(2,1)S(1)}, u32[]{:S(2)}, u32[]{:S(2)}) collective-permute-start(bf16[224,128]{1,0:T(8,128)(2,1)S(1)} %pad_maximum_fusion.1), channel_id=1, source_target_pairs={{0,2},{2,0},{64,66},{66,64},{128,130},{130,128},{192,194},{194,192... | collective-permute-start | bytes 172040 | tf_op jit(solution)/shard_map/ppermute | solution.py:49
  16.6 1.8 copy.12
  18.4 0.5 collective-permute-done
  18.9 0.5 collective-permute-start.5
  19.4 0.0 collective-permute-done.1
  19.4 1.6 collective-permute-start.6
  21.0 0.0 collective-permute-done.2
  21.0 0.0 collective-permute-done.3
  21.0 0.0 collective-permute-done.4
  21.1 2.6 %collective-permute-done.5 = bf16[128,128]{1,0:T(8,128)(2,1)S(1)} collective-permute-done((bf16[128,128]{1,0:T(8,128)(2,1)S(1)}, bf16[128,128]{1,0:T(8,128)(2,1)S(1)}, u32[]{:S(2)}, u32[]{:S(2)}) %collective-permute-start.5) | collective-permute-done | bytes 32800 | tf_op jit(solution)/shard_map/ppermute | solution.py:49
  23.7 2.4 %collective-permute-done.6 = bf16[128,128]{1,0:T(8,128)(2,1)S(1)} collective-permute-done((bf16[128,128]{1,0:T(8,128)(2,1)S(1)}, bf16[128,128]{1,0:T(8,128)(2,1)S(1)}, u32[]{:S(2)}, u32[]{:S(2)}) %collective-permute-start.6) | collective-permute-done | bytes 32800 | tf_op jit(solution)/shard_map/ppermute | solution.py:49
  26.1 1.4 collective-permute-start.9
  27.5 0.0 collective-permute-start.8
  27.5 3.2 %collective-permute-start.7 = (bf16[8,128,128]{2,1,0:T(8,128)(2,1)S(1)}, bf16[8,128,128]{2,1,0:T(8,128)(2,1)S(1)}, u32[]{:S(2)}, u32[]{:S(2)}) collective-permute-start(bf16[8,128,128]{2,1,0:T(8,128)(2,1)S(1)} %bitcast_dynamic-update-slice_fusion), channel_id=1, source_target_pairs={{0,16},{1,5},{4,20},{5,9},{8,24},{9,13},{12,28},{13,1},{16,32},{17... | collective-permute-start | bytes 786440 | tf_op jit(solution)/shard_map/ppermute | solution.py:44
  30.8 5.1 %all-to-all-start = ((bf16[4,64,768]{2,1,0:T(8,128)(2,1)}), bf16[4,64,768]{2,1,0:T(8,128)(2,1)}, u32[]{:S(2)}, u32[]{:S(2)}) async-start(bf16[4,64,768]{2,1,0:T(8,128)(2,1)} %bitcast.40), calls=%async_computation | async-start | bytes 786432 | tf_op jit(solution)/shard_map/all_to_all | solution.py:485
  35.9 0.0 collective-permute-done.9
  35.9 0.9 collective-permute-done.8
  36.8 0.0 collective-permute-done.7
  36.8 0.1 pad_maximum_fusion
  36.9 2.0 %collective-permute-start.10 = (bf16[16,2,128,128]{3,2,1,0:T(8,128)(2,1)S(1)}, bf16[16,2,128,128]{3,2,1,0:T(8,128)(2,1)}, u32[]{:S(2)}, u32[]{:S(2)}) collective-permute-start(bf16[16,2,128,128]{3,2,1,0:T(8,128)(2,1)S(1)} %bitcast.41), channel_id=1, source_target_pairs={{0,4},{1,17},{4,8},{5,21},{8,12},{9,25},{12,0},{13,29},{16,20},{17... | collective-permute-start | bytes 3145736 | tf_op jit(solution)/shard_map/ppermute | solution.py:44
  39.0 1.7 collective-permute-start.11
  40.6 0.1 stack.71.place
  40.8 0.0 copy-done.1
  40.8 0.0 copy-done
  40.8 4.0 %plan.1 = (s32[8,128]{1,0:T(8,128)S(1)}, s32[8,128]{1,0:T(8,128)S(1)}, s32[8,128]{1,0:T(8,128)S(1)}, bf16[65,128,128]{2,1,0:T(8,128)(2,1)S(1)}, bf16[4,2,64,128]{3,2,1,0:T(8,128)(2,1)S(1)}) custom-call(s32[5]{0:T(128)S(1)} %stack.71.place, s32[16]{0:T(128)S(1)} %copy-done.1, s32[16,16]{1,0:T(8,128)S(1)} %copy-done), custom_call_target="tpu_custom_call" | custom-call | tf_op jit(solution)/shard_map/plan/pallas_call | solution.py:382
  44.8 2.1 %all-to-all-done.refs_4_ = bf16[4,64,768]{2,1,0:T(8,128)(2,1)} async-done(((bf16[4,64,768]{2,1,0:T(8,128)(2,1)}), bf16[4,64,768]{2,1,0:T(8,128)(2,1)}, u32[]{:S(2)}, u32[]{:S(2)}) %all-to-all-start) | async-done | bytes 393248 | tf_op jit(solution)/shard_map/all_to_all | solution.py:485
  46.8 0.0 collective-permute-start.12
  46.9 0.0 copy-done.2
  46.9 0.8 collective-permute-start.13
  47.6 0.0 copy-done.3
  47.6 0.1 iota_compare_fusion
  47.7 0.9 collective-permute-done.13
  48.6 0.2 convolution_convert_fusion.gate_ref
  48.8 0.0 collective-permute-done.12.refs_5_
  48.9 5.3 %attend0.1 = (bf16[4,768,256]{2,1,0:T(8,128)(2,1)S(1)}, f32[4,768,256]{2,1,0:T(8,128)S(1)}) custom-call(s32[8,128]{1,0:T(8,128)S(1)} %get-tuple-element.49.refs_0_, s32[8,128]{1,0:T(8,128)S(1)} %get-tuple-element.50.refs_1_, bf16[65,128,128]{2,1,0:T(8,128)(2,1)S(1)} %get-tuple-element.51.refs_2_, bf16[4,2,64,128]{3,2,1,0:T(8,128)(2,1)S(1)} %get-tuple-element.52.refs_3_, ...), custom_call_target="tpu_custom_call" | custom-call | flops 1500000000 | bytes 8388608 | tf_op jit(solution)/shard_map/attend0/pallas_call | solution.py:282
  54.1 0.0 collective-permute-done.10.refs_7_.refs_8_
  54.1 0.0 collective-permute-done.11.refs_8_.refs_9_
  54.1 2.8 %collective-permute-start.14 = (bf16[16,2,128,128]{3,2,1,0:T(8,128)(2,1)S(1)}, bf16[16,2,128,128]{3,2,1,0:T(8,128)(2,1)S(1)}, u32[]{:S(2)}, u32[]{:S(2)}) collective-permute-start(bf16[16,2,128,128]{3,2,1,0:T(8,128)(2,1)S(1)} %bitcast.44), channel_id=1, source_target_pairs={{0,8},{1,33},{4,12},{5,37},{8,0},{9,41},{12,4},{13,45},{16,24},{17... | collective-permute-start | bytes 3145736 | tf_op jit(solution)/shard_map/ppermute | solution.py:44
  56.9 15.2 %attend1.1.refs_5_ = f32[4,768,256]{2,1,0:T(8,128)S(1)} custom-call(s32[8,128]{1,0:T(8,128)S(1)} %get-tuple-element.49.refs_0_, s32[8,128]{1,0:T(8,128)S(1)} %get-tuple-element.50.refs_1_, bf16[65,128,128]{2,1,0:T(8,128)(2,1)S(1)} %get-tuple-element.51.refs_2_, ...), custom_call_target="tpu_custom_call", output_to_operand_aliasing={{}: (5, {})} | custom-call | flops 7500000256 | bytes 8388608 | tf_op jit(solution)/shard_map/attend1/pallas_call | solution.py:282
  72.1 0.0 collective-permute-done.14.refs_6_
  72.1 94.9 %attend2.1 = (f32[4,384,128]{2,1,0:T(8,128)S(1)}, f32[4,64,128]{2,1,0:T(8,128)S(1)}, bf16[4,576,128]{2,1,0:T(8,128)(2,1)S(1)}) custom-call(s32[8,128]{1,0:T(8,128)S(1)} %get-tuple-element.49.refs_0_, s32[8,128]{1,0:T(8,128)S(1)} %get-tuple-element.50.refs_1_, bf16[65,128,128]{2,1,0:T(8,128)(2,1)S(1)} %get-tuple-element.51.refs_2_, ...), custom_call_target="tpu_custom_call" | custom-call | flops 3000000000 | bytes 8388608 | tf_op jit(solution)/shard_map/attend2/pallas_call | solution.py:282
  167.0 0.1 collective-permute-start.15
  167.1 2.0 %collective-permute-done.15.got = bf16[4,576,128]{2,1,0:T(8,128)(2,1)S(1)} collective-permute-done((bf16[4,576,128]{2,1,0:T(8,128)(2,1)S(1)}, bf16[4,576,128]{2,1,0:T(8,128)(2,1)S(1)}, u32[]{:S(2)}, u32[]{:S(2)}) %collective-permute-start.15) | collective-permute-done | bytes 589856 | tf_op jit(solution)/shard_map/ppermute | solution.py:33
  169.1 1.7 merge.1
  170.8 2.3 %collective-permute-start.16 = (bf16[64,768]{1,0:T(8,128)(2,1)S(1)}, bf16[64,768]{1,0:T(8,128)(2,1)S(1)}, u32[]{:S(2)}, u32[]{:S(2)}) collective-permute-start(bf16[64,768]{1,0:T(8,128)(2,1)S(1)} %get-tuple-element.68), channel_id=1, source_target_pairs={{0,64},{64,128},{128,192},{192,0},{1,65},{65,129},{129,193},{193,1... | collective-permute-start | bytes 294920 | tf_op jit(solution)/shard_map/ppermute | solution.py:29
  173.1 2.9 %collective-permute-start.17 = (bf16[64,768]{1,0:T(8,128)(2,1)S(1)}, bf16[64,768]{1,0:T(8,128)(2,1)S(1)}, u32[]{:S(2)}, u32[]{:S(2)}) collective-permute-start(bf16[64,768]{1,0:T(8,128)(2,1)S(1)} %get-tuple-element.69), channel_id=1, source_target_pairs={{0,128},{64,192},{128,0},{192,64},{1,129},{65,193},{129,1},{193,65... | collective-permute-start | bytes 294920 | tf_op jit(solution)/shard_map/ppermute | solution.py:29
  176.0 3.6 %collective-permute-start.18 = (bf16[64,768]{1,0:T(8,128)(2,1)S(1)}, bf16[64,768]{1,0:T(8,128)(2,1)S(1)}, u32[]{:S(2)}, u32[]{:S(2)}) collective-permute-start(bf16[64,768]{1,0:T(8,128)(2,1)S(1)} %get-tuple-element.70), channel_id=1, source_target_pairs={{0,192},{64,0},{128,64},{192,128},{1,193},{65,1},{129,65},{193,129... | collective-permute-start | bytes 294920 | tf_op jit(solution)/shard_map/ppermute | solution.py:29
  179.5 0.0 collective-permute-done.16.refs_1_
  179.5 2.5 %collective-permute-done.17.refs_2_ = bf16[64,768]{1,0:T(8,128)(2,1)S(1)} collective-permute-done((bf16[64,768]{1,0:T(8,128)(2,1)S(1)}, bf16[64,768]{1,0:T(8,128)(2,1)S(1)}, u32[]{:S(2)}, u32[]{:S(2)}) %collective-permute-start.17) | collective-permute-done | bytes 98336 | tf_op jit(solution)/shard_map/ppermute | solution.py:29
  182.1 0.0 collective-permute-done.18.refs_3_
  182.1 1.3 assemble.1
  (15 shorter events, 0.1 us)
Async XLA Ops:
  0.0 46.9 %copy-start.2 = (bf16[16,768]{1,0:T(8,128)(2,1)S(1)}, bf16[16,768]{1,0:T(8,128)(2,1)}, u32[]{:S(2)}) copy-start(bf16[16,768]{1,0:T(8,128)(2,1)} %param.13) | copy-start | bytes 73732
  0.0 40.8 %copy-start.1 = (s32[16]{0:T(128)S(1)}, s32[16]{0:T(128)}, u32[]{:S(2)}) copy-start(s32[16]{0:T(128)} %lengths) | copy-start | bytes 196
  0.0 40.8 %copy-start = (s32[16,16]{1,0:T(8,128)S(1)}, s32[16,16]{1,0:T(8,128)}, u32[]{:S(2)}) copy-start(s32[16,16]{1,0:T(8,128)} %allowed) | copy-start | bytes 3076
  0.0 47.6 %copy-start.3 = (s32[16]{0:T(128)S(1)}, s32[16]{0:T(128)}, u32[]{:S(2)}) copy-start(s32[16]{0:T(128)} %param.12) | copy-start | bytes 196
  1.0 18.4 %collective-permute-start.1 = (bf16[128,128]{1,0:T(8,128)(2,1)S(1)}, bf16[128,128]{1,0:T(8,128)(2,1)S(1)}, u32[]{:S(2)}, u32[]{:S(2)}) collective-permute-start(bf16[128,128]{1,0:T(8,128)(2,1)S(1)} %pad_maximum_fusion.3), channel_id=1, source_target_pairs={{0,64},{2,66},{64,128},{66,130},{128,192},{130,194},{192,0},{194,2... | collective-permute-start | bytes 98312 | tf_op jit(solution)/shard_map/ppermute | solution.py:49
  4.3 16.7 %collective-permute-start.2 = (bf16[128,128]{1,0:T(8,128)(2,1)S(1)}, bf16[128,128]{1,0:T(8,128)(2,1)S(1)}, u32[]{:S(2)}, u32[]{:S(2)}) collective-permute-start(bf16[128,128]{1,0:T(8,128)(2,1)S(1)} %pad_maximum_fusion.3), channel_id=1, source_target_pairs={{0,66},{2,64},{64,130},{66,128},{128,194},{130,192},{192,2},{194,0... | collective-permute-start | bytes 98312 | tf_op jit(solution)/shard_map/ppermute | solution.py:49
  9.2 11.8 %collective-permute-start.3 = (bf16[128,128]{1,0:T(8,128)(2,1)S(1)}, bf16[128,128]{1,0:T(8,128)(2,1)S(1)}, u32[]{:S(2)}, u32[]{:S(2)}) collective-permute-start(bf16[128,128]{1,0:T(8,128)(2,1)S(1)} %pad_maximum_fusion.4), channel_id=1, source_target_pairs={{0,128},{2,130},{64,192},{66,194},{128,0},{130,2},{192,64},{194,66... | collective-permute-start | bytes 98312 | tf_op jit(solution)/shard_map/ppermute | solution.py:49
  10.2 10.8 %collective-permute-start.4 = (bf16[128,128]{1,0:T(8,128)(2,1)S(1)}, bf16[128,128]{1,0:T(8,128)(2,1)S(1)}, u32[]{:S(2)}, u32[]{:S(2)}) collective-permute-start(bf16[128,128]{1,0:T(8,128)(2,1)S(1)} %pad_maximum_fusion.4), channel_id=1, source_target_pairs={{0,130},{2,128},{64,194},{66,192},{128,2},{130,0},{192,66},{194,64... | collective-permute-start | bytes 98312 | tf_op jit(solution)/shard_map/ppermute | solution.py:49
  14.6 4.3 %collective-permute-start = (bf16[224,128]{1,0:T(8,128)(2,1)S(1)}, bf16[224,128]{1,0:T(8,128)(2,1)S(1)}, u32[]{:S(2)}, u32[]{:S(2)}) collective-permute-start(bf16[224,128]{1,0:T(8,128)(2,1)S(1)} %pad_maximum_fusion.1), channel_id=1, source_target_pairs={{0,2},{2,0},{64,66},{66,64},{128,130},{130,128},{192,194},{194,192... | collective-permute-start | bytes 172040 | tf_op jit(solution)/shard_map/ppermute | solution.py:49
  18.9 4.8 %collective-permute-start.5 = (bf16[128,128]{1,0:T(8,128)(2,1)S(1)}, bf16[128,128]{1,0:T(8,128)(2,1)S(1)}, u32[]{:S(2)}, u32[]{:S(2)}) collective-permute-start(bf16[128,128]{1,0:T(8,128)(2,1)S(1)} %pad_maximum_fusion.5), channel_id=1, source_target_pairs={{0,192},{2,194},{64,0},{66,2},{128,64},{130,66},{192,128},{194,130... | collective-permute-start | bytes 98312 | tf_op jit(solution)/shard_map/ppermute | solution.py:49
  19.4 6.7 %collective-permute-start.6 = (bf16[128,128]{1,0:T(8,128)(2,1)S(1)}, bf16[128,128]{1,0:T(8,128)(2,1)S(1)}, u32[]{:S(2)}, u32[]{:S(2)}) collective-permute-start(bf16[128,128]{1,0:T(8,128)(2,1)S(1)} %pad_maximum_fusion.5), channel_id=1, source_target_pairs={{0,194},{2,192},{64,2},{66,0},{128,66},{130,64},{192,130},{194,128... | collective-permute-start | bytes 98312 | tf_op jit(solution)/shard_map/ppermute | solution.py:49
  26.1 9.8 %collective-permute-start.9 = (bf16[8,128,128]{2,1,0:T(8,128)(2,1)S(1)}, bf16[8,128,128]{2,1,0:T(8,128)(2,1)S(1)}, u32[]{:S(2)}, u32[]{:S(2)}) collective-permute-start(bf16[8,128,128]{2,1,0:T(8,128)(2,1)S(1)} %bitcast_dynamic-update-slice_fusion), channel_id=1, source_target_pairs={{0,32},{1,9},{4,36},{5,13},{8,40},{9,1},{12,44},{13,5},{16,48},{17... | collective-permute-start | bytes 786440 | tf_op jit(solution)/shard_map/ppermute | solution.py:44
  27.5 9.3 %collective-permute-start.8 = (bf16[8,128,128]{2,1,0:T(8,128)(2,1)S(1)}, bf16[8,128,128]{2,1,0:T(8,128)(2,1)S(1)}, u32[]{:S(2)}, u32[]{:S(2)}) collective-permute-start(bf16[8,128,128]{2,1,0:T(8,128)(2,1)S(1)} %bitcast_dynamic-update-slice_fusion), channel_id=1, source_target_pairs={{0,48},{1,13},{4,52},{5,1},{8,56},{9,5},{12,60},{13,9},{16,0},{17,... | collective-permute-start | bytes 786440 | tf_op jit(solution)/shard_map/ppermute | solution.py:44
  27.5 9.3 %collective-permute-start.7 = (bf16[8,128,128]{2,1,0:T(8,128)(2,1)S(1)}, bf16[8,128,128]{2,1,0:T(8,128)(2,1)S(1)}, u32[]{:S(2)}, u32[]{:S(2)}) collective-permute-start(bf16[8,128,128]{2,1,0:T(8,128)(2,1)S(1)} %bitcast_dynamic-update-slice_fusion), channel_id=1, source_target_pairs={{0,16},{1,5},{4,20},{5,9},{8,24},{9,13},{12,28},{13,1},{16,32},{17... | collective-permute-start | bytes 786440 | tf_op jit(solution)/shard_map/ppermute | solution.py:44
  30.8 16.1 %all-to-all-start = ((bf16[4,64,768]{2,1,0:T(8,128)(2,1)}), bf16[4,64,768]{2,1,0:T(8,128)(2,1)}, u32[]{:S(2)}, u32[]{:S(2)}) async-start(bf16[4,64,768]{2,1,0:T(8,128)(2,1)} %bitcast.40), calls=%async_computation | async-start | bytes 786432 | tf_op jit(solution)/shard_map/all_to_all | solution.py:485
  36.9 17.2 %collective-permute-start.10 = (bf16[16,2,128,128]{3,2,1,0:T(8,128)(2,1)S(1)}, bf16[16,2,128,128]{3,2,1,0:T(8,128)(2,1)}, u32[]{:S(2)}, u32[]{:S(2)}) collective-permute-start(bf16[16,2,128,128]{3,2,1,0:T(8,128)(2,1)S(1)} %bitcast.41), channel_id=1, source_target_pairs={{0,4},{1,17},{4,8},{5,21},{8,12},{9,25},{12,0},{13,29},{16,20},{17... | collective-permute-start | bytes 3145736 | tf_op jit(solution)/shard_map/ppermute | solution.py:44
  39.0 15.2 %collective-permute-start.11 = (bf16[16,2,128,128]{3,2,1,0:T(8,128)(2,1)S(1)}, bf16[16,2,128,128]{3,2,1,0:T(8,128)(2,1)}, u32[]{:S(2)}, u32[]{:S(2)}) collective-permute-start(bf16[16,2,128,128]{3,2,1,0:T(8,128)(2,1)S(1)} %bitcast.42), channel_id=1, source_target_pairs={{0,12},{1,49},{4,0},{5,53},{8,4},{9,57},{12,8},{13,61},{16,28},{17... | collective-permute-start | bytes 3145736 | tf_op jit(solution)/shard_map/ppermute | solution.py:44
  46.8 2.0 %collective-permute-start.12 = (bf16[4,64,768]{2,1,0:T(8,128)(2,1)}, bf16[4,64,768]{2,1,0:T(8,128)(2,1)S(1)}, u32[]{:S(2)}, u32[]{:S(2)}) collective-permute-start(bf16[4,64,768]{2,1,0:T(8,128)(2,1)} %all-to-all-done.refs_4_), channel_id=1, source_target_pairs={{0,1},{1,0},{2,3},{3,2},{4,5},{5,4},{6,7},{7,6},{8,9},{9,8},{10,11... | collective-permute-start | bytes 1179656 | tf_op jit(solution)/shard_map/ppermute | solution.py:33
  46.9 1.8 collective-permute-start.13
  54.1 17.9 %collective-permute-start.14 = (bf16[16,2,128,128]{3,2,1,0:T(8,128)(2,1)S(1)}, bf16[16,2,128,128]{3,2,1,0:T(8,128)(2,1)S(1)}, u32[]{:S(2)}, u32[]{:S(2)}) collective-permute-start(bf16[16,2,128,128]{3,2,1,0:T(8,128)(2,1)S(1)} %bitcast.44), channel_id=1, source_target_pairs={{0,8},{1,33},{4,12},{5,37},{8,0},{9,41},{12,4},{13,45},{16,24},{17... | collective-permute-start | bytes 3145736 | tf_op jit(solution)/shard_map/ppermute | solution.py:44
  167.0 2.1 %collective-permute-start.15 = (bf16[4,576,128]{2,1,0:T(8,128)(2,1)S(1)}, bf16[4,576,128]{2,1,0:T(8,128)(2,1)S(1)}, u32[]{:S(2)}, u32[]{:S(2)}) collective-permute-start(bf16[4,576,128]{2,1,0:T(8,128)(2,1)S(1)} %get-tuple-element.66), channel_id=1, source_target_pairs={{0,1},{1,0},{2,3},{3,2},{4,5},{5,4},{6,7},{7,6},{8,9},{9,8},{10,11... | collective-permute-start | bytes 1769480 | tf_op jit(solution)/shard_map/ppermute | solution.py:33
  170.8 8.8 %collective-permute-start.16 = (bf16[64,768]{1,0:T(8,128)(2,1)S(1)}, bf16[64,768]{1,0:T(8,128)(2,1)S(1)}, u32[]{:S(2)}, u32[]{:S(2)}) collective-permute-start(bf16[64,768]{1,0:T(8,128)(2,1)S(1)} %get-tuple-element.68), channel_id=1, source_target_pairs={{0,64},{64,128},{128,192},{192,0},{1,65},{65,129},{129,193},{193,1... | collective-permute-start | bytes 294920 | tf_op jit(solution)/shard_map/ppermute | solution.py:29
  173.1 9.0 %collective-permute-start.17 = (bf16[64,768]{1,0:T(8,128)(2,1)S(1)}, bf16[64,768]{1,0:T(8,128)(2,1)S(1)}, u32[]{:S(2)}, u32[]{:S(2)}) collective-permute-start(bf16[64,768]{1,0:T(8,128)(2,1)S(1)} %get-tuple-element.69), channel_id=1, source_target_pairs={{0,128},{64,192},{128,0},{192,64},{1,129},{65,193},{129,1},{193,65... | collective-permute-start | bytes 294920 | tf_op jit(solution)/shard_map/ppermute | solution.py:29
  176.0 6.1 %collective-permute-start.18 = (bf16[64,768]{1,0:T(8,128)(2,1)S(1)}, bf16[64,768]{1,0:T(8,128)(2,1)S(1)}, u32[]{:S(2)}, u32[]{:S(2)}) collective-permute-start(bf16[64,768]{1,0:T(8,128)(2,1)S(1)} %get-tuple-element.70), channel_id=1, source_target_pairs={{0,192},{64,0},{128,64},{192,128},{1,193},{65,1},{129,65},{193,129... | collective-permute-start | bytes 294920 | tf_op jit(solution)/shard_map/ppermute | solution.py:29

commit v4 on v3

--- a/solution.py
+++ b/solution.py
@@ -11,14 +11,13 @@
 GROUP = 6
 SEGMENTS = 16
 AXES = ("zh", "x", "y", "zl", "core")
-COLUMN = ("zh", "zl")
 UNIT = math.log2(math.e) / math.sqrt(HEAD_DIM)
 HIDDEN = -1e30
 LEAST = 2.0**-60
 MOST_SUM = 2.0**100
 TILE = 128
 TILES = 64
-LONG, SHORT = 8, 4
+LONGEST, LONG, SHORT = 16, 8, 4
 HALF = 8
 STAGES = ((0, HALF), (HALF, 48 - HALF), (48, 16))
 LAST = len(STAGES) - 1
@@ -42,11 +41,6 @@
                 to = ((i + by) % 4 * 4 + j) if along_x else (i * 4 + (j + by) % 4)
                 pairs.append(((i * 4 + j) * 2 + core, to * 2 + core))
     return lax.ppermute(x, ("x", "y", "core"), pairs)
-
-
-def shift_column(x, by, flip):
-    pairs = [(i, (i // 2 + by) % 4 * 2 + (i % 2 ^ flip)) for i in range(8)]
-    return lax.ppermute(x, COLUMN, pairs)
 
 
 def one_hot_rows(position, bounds_ref):
@@ -188,14 +182,23 @@
                 weights, load_values(picked), preferred_element_type=jnp.float32
             )
 
+        def longest_step(i, _):
+            add(begin + i * LONGEST, LONGEST)
+            return 0
+
+        longest = seen // LONGEST
+        lax.fori_loop(0, longest, longest_step, 0)
+        left = seen - longest * LONGEST
+        begin = begin + longest * LONGEST
+
         def step(i, _):
             add(begin + i * LONG, LONG)
             return 0
 
-        whole = (seen + LONG - SHORT - 1) // LONG
+        whole = (left + LONG - SHORT - 1) // LONG
         lax.fori_loop(0, whole, step, 0)
 
-        @pl.when(seen > whole * LONG)
+        @pl.when(left > whole * LONG)
         def _():
             add(begin + whole * LONG, SHORT)
 
@@ -469,16 +472,12 @@
             ],
             axis=0,
         )
-        column.append(pair if d == 0 else shift_column(pair, d, 0))
-        if d > 0:
-            column.append(shift_column(pair, d, 1))
-        else:
-            both = jnp.concatenate([pair, gate_table.reshape(96, 128)], axis=0)
-            both = shift_column(both, 0, 1)
-            column.append(both[:128])
-            gates = jnp.stack([gate_table, both[128:].reshape(16, 768)])
-
-    own_column = jnp.stack(column)
+        column.append(pair if d == 0 else shift(pair, "zh", d))
+    both = jnp.concatenate(column + [gate_table.reshape(96, 128)], axis=0)
+    beside = swap(both, "zl")
+    own_column = jnp.stack([both[:512].reshape(4, 128, 128), beside[:512].reshape(4, 128, 128)], 1)
+    own_column = own_column.reshape(8, 128, 128)
+    gates = jnp.stack([gate_table, beside[512:].reshape(16, 768)])
 
     asked = jnp.transpose(queries.reshape(64, 4, 768), (1, 0, 2))
     own_column, asked = lax.optimization_barrier((own_column, asked))

time: 185 us -> 179 us (0.968)
  starting transfers between devices: 42.8 us -> 38.6 us
    ppermute x7 -> x0, starting transfers between devices: 17 us -> none  [shift_column(): return lax.ppermute(x, COLUMN, pairs)]
    ppermute x3 -> x6, starting transfers between devices: 8.75 us -> 20.4 us  [shift(): return lax.ppermute(x, axis, [(i, (i + by) % 4) for i in range(4)])]
    ppermute x7 -> x0, waiting for transfers between devices: 5.52 us -> none  [shift_column(): return lax.ppermute(x, COLUMN, pairs)]
    ppermute x3 -> x4, waiting for transfers between devices: 2.92 us -> 5.37 us  [swap(): return lax.ppermute(x, axis, [(0, 1), (1, 0)])]
    ppermute x3 -> x6, waiting for transfers between devices: 2.53 us -> 3.96 us  [shift(): return lax.ppermute(x, axis, [(i, (i + by) % 4) for i in range(4)])]
  transfers between devices with their start and end apart: 20 -> 17, of which waited for: 8 -> 7; matrix products, arithmetic and copies ran while one was open for 2% -> 2% of each run, Pallas kernels for 13% -> 13%
where the time goes in v4:
time: 179 us; the launch traced here: 178 us
  Pallas kernels  122 us (68%)
  starting transfers between devices  38.6 us (22%)
  waiting for transfers between devices  12.1 us (7%)
  local copies, waits for them, and re-layouts  4.37 us (2%)
    pallas_call x3, Pallas kernels, attend_call(): pl.pallas_call(body, out_shape=out_shape, in_specs=[smem] * 2 + [vmem] *...  115 us
    ppermute x6, starting transfers between devices, shift(): return lax.ppermute(x, axis, [(i, (i + by) % 4) for i in range(4)])  20.4 us
    ppermute x6, starting transfers between devices, shift_cross(): return lax.ppermute(x, ('x', 'y', 'core'), pairs)  11 us
    ppermute x4, waiting for transfers between devices, swap(): return lax.ppermute(x, axis, [(0, 1), (1, 0)])  5.37 us
    all_to_all x1, starting transfers between devices, per_device(): own = lax.all_to_all(asked, 'zh', split_axis=0, concat_axis=0, tiled=True)  5.14 us
    pallas_call x1, Pallas kernels, plan_call(): pl.pallas_call(plan, out_shape=(jax.ShapeDtypeStruct((8, 128), jnp.int32)...  3.98 us
    ppermute x6, waiting for transfers between devices, shift(): return lax.ppermute(x, axis, [(i, (i + by) % 4) for i in range(4)])  3.96 us
  transfers between devices with their start and end apart: 17, of which 7 were waited for; matrix products, arithmetic and copies ran while one was open for 2% of the time, Pallas kernels for 13%

profile of v4, /device:TPU:6, one launch (start us, length us, event | category | flops | bytes accessed | tf_op | source)
XLA Modules:
  0.0 178.0 jit_solution(10642961533332076569)
XLA Ops:
  0.0 0.0 copy-start.2
  0.0 0.0 copy-start.1
  0.0 0.0 copy-start
  0.0 0.0 copy-start.3
  0.1 0.8 constant_dynamic-update-slice_fusion.4
  0.9 0.8 constant_dynamic-update-slice_fusion.3
  1.7 3.3 %collective-permute-start = (bf16[128,128]{1,0:T(8,128)(2,1)S(1)}, bf16[128,128]{1,0:T(8,128)(2,1)S(1)}, u32[]{:S(2)}, u32[]{:S(2)}) collective-permute-start(bf16[128,128]{1,0:T(8,128)(2,1)S(1)} %pad_maximum_fusion.3), channel_id=1, source_target_pairs={{0,64},{64,128},{128,192},{192,0},{1,65},{65,129},{129,193},{193,1... | collective-permute-start | bytes 98312 | tf_op jit(solution)/shard_map/ppermute | solution.py:28
  5.0 5.4 %collective-permute-start.1 = (bf16[128,128]{1,0:T(8,128)(2,1)S(1)}, bf16[128,128]{1,0:T(8,128)(2,1)S(1)}, u32[]{:S(2)}, u32[]{:S(2)}) collective-permute-start(bf16[128,128]{1,0:T(8,128)(2,1)S(1)} %pad_maximum_fusion.4), channel_id=1, source_target_pairs={{0,128},{64,192},{128,0},{192,64},{1,129},{65,193},{129,1},{193,65... | collective-permute-start | bytes 98312 | tf_op jit(solution)/shard_map/ppermute | solution.py:28
  10.4 2.7 %collective-permute-start.2 = (bf16[128,128]{1,0:T(8,128)(2,1)S(1)}, bf16[128,128]{1,0:T(8,128)(2,1)S(1)}, u32[]{:S(2)}, u32[]{:S(2)}) collective-permute-start(bf16[128,128]{1,0:T(8,128)(2,1)S(1)} %pad_maximum_fusion.5), channel_id=1, source_target_pairs={{0,192},{64,0},{128,64},{192,128},{1,193},{65,1},{129,65},{193,129... | collective-permute-start | bytes 98312 | tf_op jit(solution)/shard_map/ppermute | solution.py:28
  13.1 0.8 reshape.13
  13.9 0.0 collective-permute-done
  13.9 0.0 collective-permute-done.1
  13.9 1.3 collective-permute-done.2
  15.3 1.1 collective-permute-start.3
  16.4 1.8 copy.14
  18.2 2.4 %collective-permute-done.3 = bf16[608,128]{1,0:T(8,128)(2,1)S(1)} collective-permute-done((bf16[608,128]{1,0:T(8,128)(2,1)S(1)}, bf16[608,128]{1,0:T(8,128)(2,1)S(1)}, u32[]{:S(2)}, u32[]{:S(2)}) %collective-permute-start.3) | collective-permute-done | bytes 155680 | tf_op jit(solution)/shard_map/ppermute | solution.py:32
  20.7 1.5 collective-permute-start.6
  22.2 0.0 collective-permute-start.5
  22.2 3.2 %collective-permute-start.4 = (bf16[8,128,128]{2,1,0:T(8,128)(2,1)S(1)}, bf16[8,128,128]{2,1,0:T(8,128)(2,1)S(1)}, u32[]{:S(2)}, u32[]{:S(2)}) collective-permute-start(bf16[8,128,128]{2,1,0:T(8,128)(2,1)S(1)} %bitcast.32), channel_id=1, source_target_pairs={{0,16},{1,5},{4,20},{5,9},{8,24},{9,13},{12,28},{13,1},{16,32},{17... | collective-permute-start | bytes 786440 | tf_op jit(solution)/shard_map/ppermute | solution.py:43
  25.4 5.1 %all-to-all-start = ((bf16[4,64,768]{2,1,0:T(8,128)(2,1)}), bf16[4,64,768]{2,1,0:T(8,128)(2,1)}, u32[]{:S(2)}, u32[]{:S(2)}) async-start(bf16[4,64,768]{2,1,0:T(8,128)(2,1)} %bitcast.23), calls=%async_computation | async-start | bytes 786432 | tf_op jit(solution)/shard_map/all_to_all | solution.py:484
  30.5 0.0 collective-permute-done.6
  30.5 0.9 collective-permute-done.5
  31.4 0.0 collective-permute-done.4
  31.4 0.1 pad_maximum_fusion
  31.6 1.7 collective-permute-start.7
  33.2 1.7 collective-permute-start.8
  34.9 0.1 stack.47.place
  35.0 0.0 copy-done.1
  35.0 0.0 copy-done
  35.1 4.0 %plan.1 = (s32[8,128]{1,0:T(8,128)S(1)}, s32[8,128]{1,0:T(8,128)S(1)}, s32[8,128]{1,0:T(8,128)S(1)}, bf16[65,128,128]{2,1,0:T(8,128)(2,1)S(1)}, bf16[4,2,64,128]{3,2,1,0:T(8,128)(2,1)S(1)}) custom-call(s32[5]{0:T(128)S(1)} %stack.47.place, s32[16]{0:T(128)S(1)} %copy-done.1, s32[16,16]{1,0:T(8,128)S(1)} %copy-done), custom_call_target="tpu_custom_call" | custom-call | tf_op jit(solution)/shard_map/plan/pallas_call | solution.py:385
  39.0 1.9 %all-to-all-done.refs_4_ = bf16[4,64,768]{2,1,0:T(8,128)(2,1)} async-done(((bf16[4,64,768]{2,1,0:T(8,128)(2,1)}), bf16[4,64,768]{2,1,0:T(8,128)(2,1)}, u32[]{:S(2)}, u32[]{:S(2)}) %all-to-all-start) | async-done | bytes 393248 | tf_op jit(solution)/shard_map/all_to_all | solution.py:484
  41.0 0.0 collective-permute-start.9
  41.0 0.0 copy-done.2
  41.0 0.8 collective-permute-start.10
  41.8 0.0 copy-done.3
  41.8 0.1 iota_compare_fusion
  41.8 0.9 collective-permute-done.10
  42.8 0.2 convolution_convert_fusion.gate_ref
  43.0 0.0 collective-permute-done.9.refs_5_
  43.0 5.3 %attend0.1 = (bf16[4,768,256]{2,1,0:T(8,128)(2,1)S(1)}, f32[4,768,256]{2,1,0:T(8,128)S(1)}) custom-call(s32[8,128]{1,0:T(8,128)S(1)} %get-tuple-element.49.refs_0_, s32[8,128]{1,0:T(8,128)S(1)} %get-tuple-element.50.refs_1_, bf16[65,128,128]{2,1,0:T(8,128)(2,1)S(1)} %get-tuple-element.51.refs_2_, bf16[4,2,64,128]{3,2,1,0:T(8,128)(2,1)S(1)} %get-tuple-element.52.refs_3_, ...), custom_call_target="tpu_custom_call" | custom-call | flops 1500000000 | bytes 8388608 | tf_op jit(solution)/shard_map/attend0/pallas_call | solution.py:285
  48.3 0.0 collective-permute-done.7.refs_7_.refs_8_
  48.3 0.0 collective-permute-done.8.refs_8_.refs_9_
  48.3 3.0 %collective-permute-start.11 = (bf16[16,2,128,128]{3,2,1,0:T(8,128)(2,1)S(1)}, bf16[16,2,128,128]{3,2,1,0:T(8,128)(2,1)S(1)}, u32[]{:S(2)}, u32[]{:S(2)}) collective-permute-start(bf16[16,2,128,128]{3,2,1,0:T(8,128)(2,1)S(1)} %bitcast.27), channel_id=1, source_target_pairs={{0,8},{1,33},{4,12},{5,37},{8,0},{9,41},{12,4},{13,45},{16,24},{17... | collective-permute-start | bytes 3145736 | tf_op jit(solution)/shard_map/ppermute | solution.py:43
  51.3 14.2 %attend1.1.refs_5_ = f32[4,768,256]{2,1,0:T(8,128)S(1)} custom-call(s32[8,128]{1,0:T(8,128)S(1)} %get-tuple-element.49.refs_0_, s32[8,128]{1,0:T(8,128)S(1)} %get-tuple-element.50.refs_1_, bf16[65,128,128]{2,1,0:T(8,128)(2,1)S(1)} %get-tuple-element.51.refs_2_, ...), custom_call_target="tpu_custom_call", output_to_operand_aliasing={{}: (5, {})} | custom-call | flops 7500000256 | bytes 8388608 | tf_op jit(solution)/shard_map/attend1/pallas_call | solution.py:285
  65.5 0.0 collective-permute-done.11.refs_6_
  65.5 95.7 %attend2.1 = (f32[4,384,128]{2,1,0:T(8,128)S(1)}, f32[4,64,128]{2,1,0:T(8,128)S(1)}, bf16[4,576,128]{2,1,0:T(8,128)(2,1)S(1)}) custom-call(s32[8,128]{1,0:T(8,128)S(1)} %get-tuple-element.49.refs_0_, s32[8,128]{1,0:T(8,128)S(1)} %get-tuple-element.50.refs_1_, bf16[65,128,128]{2,1,0:T(8,128)(2,1)S(1)} %get-tuple-element.51.refs_2_, ...), custom_call_target="tpu_custom_call" | custom-call | flops 3000000000 | bytes 8388608 | tf_op jit(solution)/shard_map/attend2/pallas_call | solution.py:285
  161.2 0.1 collective-permute-start.12
  161.3 2.0 %collective-permute-done.12.got = bf16[4,576,128]{2,1,0:T(8,128)(2,1)S(1)} collective-permute-done((bf16[4,576,128]{2,1,0:T(8,128)(2,1)S(1)}, bf16[4,576,128]{2,1,0:T(8,128)(2,1)S(1)}, u32[]{:S(2)}, u32[]{:S(2)}) %collective-permute-start.12) | collective-permute-done | bytes 589856 | tf_op jit(solution)/shard_map/ppermute | solution.py:32
  163.3 1.7 merge.1
  165.0 2.6 %collective-permute-start.13 = (bf16[64,768]{1,0:T(8,128)(2,1)S(1)}, bf16[64,768]{1,0:T(8,128)(2,1)S(1)}, u32[]{:S(2)}, u32[]{:S(2)}) collective-permute-start(bf16[64,768]{1,0:T(8,128)(2,1)S(1)} %get-tuple-element.68), channel_id=1, source_target_pairs={{0,64},{64,128},{128,192},{192,0},{1,65},{65,129},{129,193},{193,1... | collective-permute-start | bytes 294920 | tf_op jit(solution)/shard_map/ppermute | solution.py:28
  167.6 3.5 %collective-permute-start.14 = (bf16[64,768]{1,0:T(8,128)(2,1)S(1)}, bf16[64,768]{1,0:T(8,128)(2,1)S(1)}, u32[]{:S(2)}, u32[]{:S(2)}) collective-permute-start(bf16[64,768]{1,0:T(8,128)(2,1)S(1)} %get-tuple-element.69), channel_id=1, source_target_pairs={{0,128},{64,192},{128,0},{192,64},{1,129},{65,193},{129,1},{193,65... | collective-permute-start | bytes 294920 | tf_op jit(solution)/shard_map/ppermute | solution.py:28
  171.1 3.0 %collective-permute-start.15 = (bf16[64,768]{1,0:T(8,128)(2,1)S(1)}, bf16[64,768]{1,0:T(8,128)(2,1)S(1)}, u32[]{:S(2)}, u32[]{:S(2)}) collective-permute-start(bf16[64,768]{1,0:T(8,128)(2,1)S(1)} %get-tuple-element.70), channel_id=1, source_target_pairs={{0,192},{64,0},{128,64},{192,128},{1,193},{65,1},{129,65},{193,129... | collective-permute-start | bytes 294920 | tf_op jit(solution)/shard_map/ppermute | solution.py:28
  174.0 0.0 collective-permute-done.13.refs_1_
  174.0 2.6 %collective-permute-done.14.refs_2_ = bf16[64,768]{1,0:T(8,128)(2,1)S(1)} collective-permute-done((bf16[64,768]{1,0:T(8,128)(2,1)S(1)}, bf16[64,768]{1,0:T(8,128)(2,1)S(1)}, u32[]{:S(2)}, u32[]{:S(2)}) %collective-permute-start.14) | collective-permute-done | bytes 98336 | tf_op jit(solution)/shard_map/ppermute | solution.py:28
  176.7 0.0 collective-permute-done.15.refs_3_
  176.7 1.3 assemble.1
  (13 shorter events, 0.2 us)
Async XLA Ops:
  0.0 41.0 %copy-start.2 = (bf16[16,768]{1,0:T(8,128)(2,1)S(1)}, bf16[16,768]{1,0:T(8,128)(2,1)}, u32[]{:S(2)}) copy-start(bf16[16,768]{1,0:T(8,128)(2,1)} %param.13) | copy-start | bytes 73732
  0.0 35.0 %copy-start.1 = (s32[16]{0:T(128)S(1)}, s32[16]{0:T(128)}, u32[]{:S(2)}) copy-start(s32[16]{0:T(128)} %lengths) | copy-start | bytes 196
  0.0 35.0 %copy-start = (s32[16,16]{1,0:T(8,128)S(1)}, s32[16,16]{1,0:T(8,128)}, u32[]{:S(2)}) copy-start(s32[16,16]{1,0:T(8,128)} %allowed) | copy-start | bytes 3076
  0.0 41.7 %copy-start.3 = (s32[16]{0:T(128)S(1)}, s32[16]{0:T(128)}, u32[]{:S(2)}) copy-start(s32[16]{0:T(128)} %param.12) | copy-start | bytes 196
  1.7 12.2 %collective-permute-start = (bf16[128,128]{1,0:T(8,128)(2,1)S(1)}, bf16[128,128]{1,0:T(8,128)(2,1)S(1)}, u32[]{:S(2)}, u32[]{:S(2)}) collective-permute-start(bf16[128,128]{1,0:T(8,128)(2,1)S(1)} %pad_maximum_fusion.3), channel_id=1, source_target_pairs={{0,64},{64,128},{128,192},{192,0},{1,65},{65,129},{129,193},{193,1... | collective-permute-start | bytes 98312 | tf_op jit(solution)/shard_map/ppermute | solution.py:28
  5.0 8.9 %collective-permute-start.1 = (bf16[128,128]{1,0:T(8,128)(2,1)S(1)}, bf16[128,128]{1,0:T(8,128)(2,1)S(1)}, u32[]{:S(2)}, u32[]{:S(2)}) collective-permute-start(bf16[128,128]{1,0:T(8,128)(2,1)S(1)} %pad_maximum_fusion.4), channel_id=1, source_target_pairs={{0,128},{64,192},{128,0},{192,64},{1,129},{65,193},{129,1},{193,65... | collective-permute-start | bytes 98312 | tf_op jit(solution)/shard_map/ppermute | solution.py:28
  10.4 4.8 %collective-permute-start.2 = (bf16[128,128]{1,0:T(8,128)(2,1)S(1)}, bf16[128,128]{1,0:T(8,128)(2,1)S(1)}, u32[]{:S(2)}, u32[]{:S(2)}) collective-permute-start(bf16[128,128]{1,0:T(8,128)(2,1)S(1)} %pad_maximum_fusion.5), channel_id=1, source_target_pairs={{0,192},{64,0},{128,64},{192,128},{1,193},{65,1},{129,65},{193,129... | collective-permute-start | bytes 98312 | tf_op jit(solution)/shard_map/ppermute | solution.py:28
  15.3 5.3 %collective-permute-start.3 = (bf16[608,128]{1,0:T(8,128)(2,1)S(1)}, bf16[608,128]{1,0:T(8,128)(2,1)S(1)}, u32[]{:S(2)}, u32[]{:S(2)}) collective-permute-start(bf16[608,128]{1,0:T(8,128)(2,1)S(1)} %constant_dynamic-update-slice_fusion.5), channel_id=1, source_target_pairs={{0,2},{2,0},{1,3},{3,1},{4,6},{6,4},{5,7},{7,5},{8,10},{10,8},{9,1... | collective-permute-start | bytes 466952 | tf_op jit(solution)/shard_map/ppermute | solution.py:32
  20.7 9.9 %collective-permute-start.6 = (bf16[8,128,128]{2,1,0:T(8,128)(2,1)S(1)}, bf16[8,128,128]{2,1,0:T(8,128)(2,1)S(1)}, u32[]{:S(2)}, u32[]{:S(2)}) collective-permute-start(bf16[8,128,128]{2,1,0:T(8,128)(2,1)S(1)} %bitcast.30), channel_id=1, source_target_pairs={{0,32},{1,9},{4,36},{5,13},{8,40},{9,1},{12,44},{13,5},{16,48},{17... | collective-permute-start | bytes 786440 | tf_op jit(solution)/shard_map/ppermute | solution.py:43
  22.2 9.3 %collective-permute-start.5 = (bf16[8,128,128]{2,1,0:T(8,128)(2,1)S(1)}, bf16[8,128,128]{2,1,0:T(8,128)(2,1)S(1)}, u32[]{:S(2)}, u32[]{:S(2)}) collective-permute-start(bf16[8,128,128]{2,1,0:T(8,128)(2,1)S(1)} %bitcast.31), channel_id=1, source_target_pairs={{0,48},{1,13},{4,52},{5,1},{8,56},{9,5},{12,60},{13,9},{16,0},{17,... | collective-permute-start | bytes 786440 | tf_op jit(solution)/shard_map/ppermute | solution.py:43
  22.2 9.3 %collective-permute-start.4 = (bf16[8,128,128]{2,1,0:T(8,128)(2,1)S(1)}, bf16[8,128,128]{2,1,0:T(8,128)(2,1)S(1)}, u32[]{:S(2)}, u32[]{:S(2)}) collective-permute-start(bf16[8,128,128]{2,1,0:T(8,128)(2,1)S(1)} %bitcast.32), channel_id=1, source_target_pairs={{0,16},{1,5},{4,20},{5,9},{8,24},{9,13},{12,28},{13,1},{16,32},{17... | collective-permute-start | bytes 786440 | tf_op jit(solution)/shard_map/ppermute | solution.py:43
  25.4 15.6 %all-to-all-start = ((bf16[4,64,768]{2,1,0:T(8,128)(2,1)}), bf16[4,64,768]{2,1,0:T(8,128)(2,1)}, u32[]{:S(2)}, u32[]{:S(2)}) async-start(bf16[4,64,768]{2,1,0:T(8,128)(2,1)} %bitcast.23), calls=%async_computation | async-start | bytes 786432 | tf_op jit(solution)/shard_map/all_to_all | solution.py:484
  31.6 16.7 %collective-permute-start.7 = (bf16[16,2,128,128]{3,2,1,0:T(8,128)(2,1)S(1)}, bf16[16,2,128,128]{3,2,1,0:T(8,128)(2,1)}, u32[]{:S(2)}, u32[]{:S(2)}) collective-permute-start(bf16[16,2,128,128]{3,2,1,0:T(8,128)(2,1)S(1)} %bitcast.24), channel_id=1, source_target_pairs={{0,4},{1,17},{4,8},{5,21},{8,12},{9,25},{12,0},{13,29},{16,20},{17... | collective-permute-start | bytes 3145736 | tf_op jit(solution)/shard_map/ppermute | solution.py:43
  33.2 15.1 %collective-permute-start.8 = (bf16[16,2,128,128]{3,2,1,0:T(8,128)(2,1)S(1)}, bf16[16,2,128,128]{3,2,1,0:T(8,128)(2,1)}, u32[]{:S(2)}, u32[]{:S(2)}) collective-permute-start(bf16[16,2,128,128]{3,2,1,0:T(8,128)(2,1)S(1)} %bitcast.25), channel_id=1, source_target_pairs={{0,12},{1,49},{4,0},{5,53},{8,4},{9,57},{12,8},{13,61},{16,28},{17... | collective-permute-start | bytes 3145736 | tf_op jit(solution)/shard_map/ppermute | solution.py:43
  41.0 2.0 %collective-permute-start.9 = (bf16[4,64,768]{2,1,0:T(8,128)(2,1)}, bf16[4,64,768]{2,1,0:T(8,128)(2,1)S(1)}, u32[]{:S(2)}, u32[]{:S(2)}) collective-permute-start(bf16[4,64,768]{2,1,0:T(8,128)(2,1)} %all-to-all-done.refs_4_), channel_id=1, source_target_pairs={{0,1},{1,0},{2,3},{3,2},{4,5},{5,4},{6,7},{7,6},{8,9},{9,8},{10,11... | collective-permute-start | bytes 1179656 | tf_op jit(solution)/shard_map/ppermute | solution.py:32
  41.0 1.8 collective-permute-start.10
  48.3 17.2 %collective-permute-start.11 = (bf16[16,2,128,128]{3,2,1,0:T(8,128)(2,1)S(1)}, bf16[16,2,128,128]{3,2,1,0:T(8,128)(2,1)S(1)}, u32[]{:S(2)}, u32[]{:S(2)}) collective-permute-start(bf16[16,2,128,128]{3,2,1,0:T(8,128)(2,1)S(1)} %bitcast.27), channel_id=1, source_target_pairs={{0,8},{1,33},{4,12},{5,37},{8,0},{9,41},{12,4},{13,45},{16,24},{17... | collective-permute-start | bytes 3145736 | tf_op jit(solution)/shard_map/ppermute | solution.py:43
  161.2 2.1 %collective-permute-start.12 = (bf16[4,576,128]{2,1,0:T(8,128)(2,1)S(1)}, bf16[4,576,128]{2,1,0:T(8,128)(2,1)S(1)}, u32[]{:S(2)}, u32[]{:S(2)}) collective-permute-start(bf16[4,576,128]{2,1,0:T(8,128)(2,1)S(1)} %get-tuple-element.66), channel_id=1, source_target_pairs={{0,1},{1,0},{2,3},{3,2},{4,5},{5,4},{6,7},{7,6},{8,9},{9,8},{10,11... | collective-permute-start | bytes 1769480 | tf_op jit(solution)/shard_map/ppermute | solution.py:32
  165.0 9.0 %collective-permute-start.13 = (bf16[64,768]{1,0:T(8,128)(2,1)S(1)}, bf16[64,768]{1,0:T(8,128)(2,1)S(1)}, u32[]{:S(2)}, u32[]{:S(2)}) collective-permute-start(bf16[64,768]{1,0:T(8,128)(2,1)S(1)} %get-tuple-element.68), channel_id=1, source_target_pairs={{0,64},{64,128},{128,192},{192,0},{1,65},{65,129},{129,193},{193,1... | collective-permute-start | bytes 294920 | tf_op jit(solution)/shard_map/ppermute | solution.py:28
  167.6 9.1 %collective-permute-start.14 = (bf16[64,768]{1,0:T(8,128)(2,1)S(1)}, bf16[64,768]{1,0:T(8,128)(2,1)S(1)}, u32[]{:S(2)}, u32[]{:S(2)}) collective-permute-start(bf16[64,768]{1,0:T(8,128)(2,1)S(1)} %get-tuple-element.69), channel_id=1, source_target_pairs={{0,128},{64,192},{128,0},{192,64},{1,129},{65,193},{129,1},{193,65... | collective-permute-start | bytes 294920 | tf_op jit(solution)/shard_map/ppermute | solution.py:28
  171.1 5.6 %collective-permute-start.15 = (bf16[64,768]{1,0:T(8,128)(2,1)S(1)}, bf16[64,768]{1,0:T(8,128)(2,1)S(1)}, u32[]{:S(2)}, u32[]{:S(2)}) collective-permute-start(bf16[64,768]{1,0:T(8,128)(2,1)S(1)} %get-tuple-element.70), channel_id=1, source_target_pairs={{0,192},{64,0},{128,64},{192,128},{1,193},{65,1},{129,65},{193,129... | collective-permute-start | bytes 294920 | tf_op jit(solution)/shard_map/ppermute | solution.py:28

commit v5 on v4

--- a/solution.py
+++ b/solution.py
@@ -473,6 +473,7 @@
             axis=0,
         )
         column.append(pair if d == 0 else shift(pair, "zh", d))
+    gate_table, _ = lax.optimization_barrier((gate_table, column[1]))
     both = jnp.concatenate(column + [gate_table.reshape(96, 128)], axis=0)
     beside = swap(both, "zl")
     own_column = jnp.stack([both[:512].reshape(4, 128, 128), beside[:512].reshape(4, 128, 128)], 1)

time: 179 us -> 179 us (level); the launches traced: 178 us -> 176 us
  Pallas kernels: 122 us -> 118 us
  waiting for transfers between devices: 12.1 us -> 14.5 us
    pallas_call x3, Pallas kernels: 115 us -> 111 us  [attend_call(): pl.pallas_call(body, out_shape=out_shape, in_specs=[smem] * 2 + [vmem] *...]
  transfers between devices with their start and end apart: 17 -> 17, of which waited for: 7 -> 9; matrix products, arithmetic and copies ran while one was open for 2% -> 2% of each run, Pallas kernels for 13% -> 12%
where the time goes in v5:
time: 179 us; the launch traced here: 176 us
  Pallas kernels  118 us (66%)
  starting transfers between devices  37.7 us (21%)
  waiting for transfers between devices  14.5 us (8%)
  local copies, waits for them, and re-layouts  4.37 us (2%)
    pallas_call x3, Pallas kernels, attend_call(): pl.pallas_call(body, out_shape=out_shape, in_specs=[smem] * 2 + [vmem] *...  111 us
    ppermute x6, starting transfers between devices, shift(): return lax.ppermute(x, axis, [(i, (i + by) % 4) for i in range(4)])  20 us
    ppermute x6, starting transfers between devices, shift_cross(): return lax.ppermute(x, ('x', 'y', 'core'), pairs)  10.6 us
    ppermute x4, waiting for transfers between devices, swap(): return lax.ppermute(x, axis, [(0, 1), (1, 0)])  5.37 us
    all_to_all x1, starting transfers between devices, per_device(): own = lax.all_to_all(asked, 'zh', split_axis=0, concat_axis=0, tiled=True)  5.14 us
    ppermute x6, waiting for transfers between devices, shift(): return lax.ppermute(x, axis, [(i, (i + by) % 4) for i in range(4)])  4.35 us
    pallas_call x1, Pallas kernels, plan_call(): pl.pallas_call(plan, out_shape=(jax.ShapeDtypeStruct((8, 128), jnp.int32)...  3.98 us
  transfers between devices with their start and end apart: 17, of which 9 were waited for; matrix products, arithmetic and copies ran while one was open for 2% of the time, Pallas kernels for 12%

profile of v5, /device:TPU:6, one launch (start us, length us, event | category | flops | bytes accessed | tf_op | source)
XLA Modules:
  0.0 175.6 jit_solution(16695130802522386749)
XLA Ops:
  0.0 0.0 copy-start.2
  0.0 0.0 copy-start.1
  0.0 0.0 copy-start
  0.0 0.0 copy-start.3
  0.1 0.8 constant_dynamic-update-slice_fusion.4
  0.9 0.8 constant_dynamic-update-slice_fusion.3
  1.7 3.3 %collective-permute-start = (bf16[128,128]{1,0:T(8,128)(2,1)S(1)}, bf16[128,128]{1,0:T(8,128)(2,1)S(1)}, u32[]{:S(2)}, u32[]{:S(2)}) collective-permute-start(bf16[128,128]{1,0:T(8,128)(2,1)S(1)} %pad_maximum_fusion.3), channel_id=1, source_target_pairs={{0,64},{64,128},{128,192},{192,0},{1,65},{65,129},{129,193},{193,1... | collective-permute-start | bytes 98312 | tf_op jit(solution)/shard_map/ppermute | solution.py:28
  5.0 5.4 %collective-permute-start.1 = (bf16[128,128]{1,0:T(8,128)(2,1)S(1)}, bf16[128,128]{1,0:T(8,128)(2,1)S(1)}, u32[]{:S(2)}, u32[]{:S(2)}) collective-permute-start(bf16[128,128]{1,0:T(8,128)(2,1)S(1)} %pad_maximum_fusion.4), channel_id=1, source_target_pairs={{0,128},{64,192},{128,0},{192,64},{1,129},{65,193},{129,1},{193,65... | collective-permute-start | bytes 98312 | tf_op jit(solution)/shard_map/ppermute | solution.py:28
  10.4 2.7 %collective-permute-start.2 = (bf16[128,128]{1,0:T(8,128)(2,1)S(1)}, bf16[128,128]{1,0:T(8,128)(2,1)S(1)}, u32[]{:S(2)}, u32[]{:S(2)}) collective-permute-start(bf16[128,128]{1,0:T(8,128)(2,1)S(1)} %pad_maximum_fusion.5), channel_id=1, source_target_pairs={{0,192},{64,0},{128,64},{192,128},{1,193},{65,1},{129,65},{193,129... | collective-permute-start | bytes 98312 | tf_op jit(solution)/shard_map/ppermute | solution.py:28
  13.1 0.0 collective-permute-done
  13.1 0.1 collective-permute-done.1
  13.2 0.8 reshape.13
  14.0 1.3 collective-permute-done.2
  15.3 1.1 collective-permute-start.3
  16.4 1.8 %copy.14 = bf16[8,4,8,768]{3,2,0,1:T(8,128)(2,1)} copy(bf16[8,4,8,768]{3,2,1,0:T(8,128)(2,1)} %bitcast.35) | data formatting | bytes 786432 | tf_op jit(solution)/shard_map/reshape | solution.py:483
  18.2 2.4 %collective-permute-done.3 = bf16[608,128]{1,0:T(8,128)(2,1)S(1)} collective-permute-done((bf16[608,128]{1,0:T(8,128)(2,1)S(1)}, bf16[608,128]{1,0:T(8,128)(2,1)S(1)}, u32[]{:S(2)}, u32[]{:S(2)}) %collective-permute-start.3) | collective-permute-done | bytes 155680 | tf_op jit(solution)/shard_map/ppermute | solution.py:32
  20.7 1.5 collective-permute-start.6
  22.2 0.0 collective-permute-start.5
  22.2 3.2 %collective-permute-start.4 = (bf16[8,128,128]{2,1,0:T(8,128)(2,1)S(1)}, bf16[8,128,128]{2,1,0:T(8,128)(2,1)S(1)}, u32[]{:S(2)}, u32[]{:S(2)}) collective-permute-start(bf16[8,128,128]{2,1,0:T(8,128)(2,1)S(1)} %bitcast.32), channel_id=1, source_target_pairs={{0,16},{1,5},{4,20},{5,9},{8,24},{9,13},{12,28},{13,1},{16,32},{17... | collective-permute-start | bytes 786440 | tf_op jit(solution)/shard_map/ppermute | solution.py:43
  25.4 5.1 %all-to-all-start = ((bf16[4,64,768]{2,1,0:T(8,128)(2,1)}), bf16[4,64,768]{2,1,0:T(8,128)(2,1)}, u32[]{:S(2)}, u32[]{:S(2)}) async-start(bf16[4,64,768]{2,1,0:T(8,128)(2,1)} %bitcast.23), calls=%async_computation | async-start | bytes 786432 | tf_op jit(solution)/shard_map/all_to_all | solution.py:485
  30.5 0.0 collective-permute-done.6
  30.5 0.9 collective-permute-done.5
  31.4 0.0 collective-permute-done.4
  31.4 0.1 pad_maximum_fusion
  31.6 1.7 collective-permute-start.7
  33.2 1.7 collective-permute-start.8
  34.9 0.1 stack.47.place
  35.0 0.0 copy-done.1
  35.0 0.0 copy-done
  35.1 4.0 %plan.1 = (s32[8,128]{1,0:T(8,128)S(1)}, s32[8,128]{1,0:T(8,128)S(1)}, s32[8,128]{1,0:T(8,128)S(1)}, bf16[65,128,128]{2,1,0:T(8,128)(2,1)S(1)}, bf16[4,2,64,128]{3,2,1,0:T(8,128)(2,1)S(1)}) custom-call(s32[5]{0:T(128)S(1)} %stack.47.place, s32[16]{0:T(128)S(1)} %copy-done.1, s32[16,16]{1,0:T(8,128)S(1)} %copy-done), custom_call_target="tpu_custom_call" | custom-call | tf_op jit(solution)/shard_map/plan/pallas_call | solution.py:385
  39.0 2.4 %all-to-all-done.refs_4_ = bf16[4,64,768]{2,1,0:T(8,128)(2,1)} async-done(((bf16[4,64,768]{2,1,0:T(8,128)(2,1)}), bf16[4,64,768]{2,1,0:T(8,128)(2,1)}, u32[]{:S(2)}, u32[]{:S(2)}) %all-to-all-start) | async-done | bytes 393248 | tf_op jit(solution)/shard_map/all_to_all | solution.py:485
  41.4 0.0 collective-permute-start.9
  41.4 0.0 copy-done.2
  41.4 0.8 collective-permute-start.10
  42.2 0.0 copy-done.3
  42.2 0.1 iota_compare_fusion
  42.3 0.9 collective-permute-done.10
  43.2 0.2 convolution_convert_fusion.gate_ref
  43.4 0.0 collective-permute-done.9.refs_5_
  43.4 5.3 %attend0.1 = (bf16[4,768,256]{2,1,0:T(8,128)(2,1)S(1)}, f32[4,768,256]{2,1,0:T(8,128)S(1)}) custom-call(s32[8,128]{1,0:T(8,128)S(1)} %get-tuple-element.51.refs_0_, s32[8,128]{1,0:T(8,128)S(1)} %get-tuple-element.52.refs_1_, bf16[65,128,128]{2,1,0:T(8,128)(2,1)S(1)} %get-tuple-element.53.refs_2_, bf16[4,2,64,128]{3,2,1,0:T(8,128)(2,1)S(1)} %get-tuple-element.54.refs_3_, ...), custom_call_target="tpu_custom_call" | custom-call | flops 1500000000 | bytes 8388608 | tf_op jit(solution)/shard_map/attend0/pallas_call | solution.py:285
  48.7 0.0 collective-permute-done.7.refs_7_.refs_8_
  48.7 0.0 collective-permute-done.8.refs_8_.refs_9_
  48.7 2.5 %collective-permute-start.11 = (bf16[16,2,128,128]{3,2,1,0:T(8,128)(2,1)S(1)}, bf16[16,2,128,128]{3,2,1,0:T(8,128)(2,1)S(1)}, u32[]{:S(2)}, u32[]{:S(2)}) collective-permute-start(bf16[16,2,128,128]{3,2,1,0:T(8,128)(2,1)S(1)} %bitcast.27), channel_id=1, source_target_pairs={{0,8},{1,33},{4,12},{5,37},{8,0},{9,41},{12,4},{13,45},{16,24},{17... | collective-permute-start | bytes 3145736 | tf_op jit(solution)/shard_map/ppermute | solution.py:43
  51.3 12.3 %attend1.1.refs_5_ = f32[4,768,256]{2,1,0:T(8,128)S(1)} custom-call(s32[8,128]{1,0:T(8,128)S(1)} %get-tuple-element.51.refs_0_, s32[8,128]{1,0:T(8,128)S(1)} %get-tuple-element.52.refs_1_, bf16[65,128,128]{2,1,0:T(8,128)(2,1)S(1)} %get-tuple-element.53.refs_2_, ...), custom_call_target="tpu_custom_call", output_to_operand_aliasing={{}: (5, {})} | custom-call | flops 7500000256 | bytes 8388608 | tf_op jit(solution)/shard_map/attend1/pallas_call | solution.py:285
  63.6 1.5 collective-permute-done.11.refs_6_
  65.1 93.8 %attend2.1 = (f32[4,384,128]{2,1,0:T(8,128)S(1)}, f32[4,64,128]{2,1,0:T(8,128)S(1)}, bf16[4,576,128]{2,1,0:T(8,128)(2,1)S(1)}) custom-call(s32[8,128]{1,0:T(8,128)S(1)} %get-tuple-element.51.refs_0_, s32[8,128]{1,0:T(8,128)S(1)} %get-tuple-element.52.refs_1_, bf16[65,128,128]{2,1,0:T(8,128)(2,1)S(1)} %get-tuple-element.53.refs_2_, ...), custom_call_target="tpu_custom_call" | custom-call | flops 3000000000 | bytes 8388608 | tf_op jit(solution)/shard_map/attend2/pallas_call | solution.py:285
  158.9 0.1 collective-permute-start.12
  159.0 2.0 %collective-permute-done.12.got = bf16[4,576,128]{2,1,0:T(8,128)(2,1)S(1)} collective-permute-done((bf16[4,576,128]{2,1,0:T(8,128)(2,1)S(1)}, bf16[4,576,128]{2,1,0:T(8,128)(2,1)S(1)}, u32[]{:S(2)}, u32[]{:S(2)}) %collective-permute-start.12) | collective-permute-done | bytes 589856 | tf_op jit(solution)/shard_map/ppermute | solution.py:32
  161.0 1.7 merge.1
  162.7 2.3 %collective-permute-start.13 = (bf16[64,768]{1,0:T(8,128)(2,1)S(1)}, bf16[64,768]{1,0:T(8,128)(2,1)S(1)}, u32[]{:S(2)}, u32[]{:S(2)}) collective-permute-start(bf16[64,768]{1,0:T(8,128)(2,1)S(1)} %get-tuple-element.70), channel_id=1, source_target_pairs={{0,64},{64,128},{128,192},{192,0},{1,65},{65,129},{129,193},{193,1... | collective-permute-start | bytes 294920 | tf_op jit(solution)/shard_map/ppermute | solution.py:28
  165.0 3.3 %collective-permute-start.14 = (bf16[64,768]{1,0:T(8,128)(2,1)S(1)}, bf16[64,768]{1,0:T(8,128)(2,1)S(1)}, u32[]{:S(2)}, u32[]{:S(2)}) collective-permute-start(bf16[64,768]{1,0:T(8,128)(2,1)S(1)} %get-tuple-element.71), channel_id=1, source_target_pairs={{0,128},{64,192},{128,0},{192,64},{1,129},{65,193},{129,1},{193,65... | collective-permute-start | bytes 294920 | tf_op jit(solution)/shard_map/ppermute | solution.py:28
  168.4 2.9 %collective-permute-start.15 = (bf16[64,768]{1,0:T(8,128)(2,1)S(1)}, bf16[64,768]{1,0:T(8,128)(2,1)S(1)}, u32[]{:S(2)}, u32[]{:S(2)}) collective-permute-start(bf16[64,768]{1,0:T(8,128)(2,1)S(1)} %get-tuple-element.72), channel_id=1, source_target_pairs={{0,192},{64,0},{128,64},{192,128},{1,193},{65,1},{129,65},{193,129... | collective-permute-start | bytes 294920 | tf_op jit(solution)/shard_map/ppermute | solution.py:28
  171.3 0.0 collective-permute-done.13.refs_1_
  171.3 3.0 %collective-permute-done.14.refs_2_ = bf16[64,768]{1,0:T(8,128)(2,1)S(1)} collective-permute-done((bf16[64,768]{1,0:T(8,128)(2,1)S(1)}, bf16[64,768]{1,0:T(8,128)(2,1)S(1)}, u32[]{:S(2)}, u32[]{:S(2)}) %collective-permute-start.14) | collective-permute-done | bytes 98336 | tf_op jit(solution)/shard_map/ppermute | solution.py:28
  174.3 0.0 collective-permute-done.15.refs_3_
  174.3 1.3 assemble.1
  (13 shorter events, 0.2 us)
Async XLA Ops:
  0.0 41.4 %copy-start.2 = (bf16[16,768]{1,0:T(8,128)(2,1)S(1)}, bf16[16,768]{1,0:T(8,128)(2,1)}, u32[]{:S(2)}) copy-start(bf16[16,768]{1,0:T(8,128)(2,1)} %param.13) | copy-start | bytes 73732
  0.0 35.0 %copy-start.1 = (s32[16]{0:T(128)S(1)}, s32[16]{0:T(128)}, u32[]{:S(2)}) copy-start(s32[16]{0:T(128)} %lengths) | copy-start | bytes 196
  0.0 35.0 %copy-start = (s32[16,16]{1,0:T(8,128)S(1)}, s32[16,16]{1,0:T(8,128)}, u32[]{:S(2)}) copy-start(s32[16,16]{1,0:T(8,128)} %allowed) | copy-start | bytes 3076
  0.0 42.2 %copy-start.3 = (s32[16]{0:T(128)S(1)}, s32[16]{0:T(128)}, u32[]{:S(2)}) copy-start(s32[16]{0:T(128)} %param.12) | copy-start | bytes 196
  1.7 11.4 %collective-permute-start = (bf16[128,128]{1,0:T(8,128)(2,1)S(1)}, bf16[128,128]{1,0:T(8,128)(2,1)S(1)}, u32[]{:S(2)}, u32[]{:S(2)}) collective-permute-start(bf16[128,128]{1,0:T(8,128)(2,1)S(1)} %pad_maximum_fusion.3), channel_id=1, source_target_pairs={{0,64},{64,128},{128,192},{192,0},{1,65},{65,129},{129,193},{193,1... | collective-permute-start | bytes 98312 | tf_op jit(solution)/shard_map/ppermute | solution.py:28
  5.0 8.1 %collective-permute-start.1 = (bf16[128,128]{1,0:T(8,128)(2,1)S(1)}, bf16[128,128]{1,0:T(8,128)(2,1)S(1)}, u32[]{:S(2)}, u32[]{:S(2)}) collective-permute-start(bf16[128,128]{1,0:T(8,128)(2,1)S(1)} %pad_maximum_fusion.4), channel_id=1, source_target_pairs={{0,128},{64,192},{128,0},{192,64},{1,129},{65,193},{129,1},{193,65... | collective-permute-start | bytes 98312 | tf_op jit(solution)/shard_map/ppermute | solution.py:28
  10.4 4.8 %collective-permute-start.2 = (bf16[128,128]{1,0:T(8,128)(2,1)S(1)}, bf16[128,128]{1,0:T(8,128)(2,1)S(1)}, u32[]{:S(2)}, u32[]{:S(2)}) collective-permute-start(bf16[128,128]{1,0:T(8,128)(2,1)S(1)} %pad_maximum_fusion.5), channel_id=1, source_target_pairs={{0,192},{64,0},{128,64},{192,128},{1,193},{65,1},{129,65},{193,129... | collective-permute-start | bytes 98312 | tf_op jit(solution)/shard_map/ppermute | solution.py:28
  15.3 5.3 %collective-permute-start.3 = (bf16[608,128]{1,0:T(8,128)(2,1)S(1)}, bf16[608,128]{1,0:T(8,128)(2,1)S(1)}, u32[]{:S(2)}, u32[]{:S(2)}) collective-permute-start(bf16[608,128]{1,0:T(8,128)(2,1)S(1)} %constant_dynamic-update-slice_fusion.5), channel_id=1, source_target_pairs={{0,2},{2,0},{1,3},{3,1},{4,6},{6,4},{5,7},{7,5},{8,10},{10,8},{9,1... | collective-permute-start | bytes 466952 | tf_op jit(solution)/shard_map/ppermute | solution.py:32
  20.7 9.9 %collective-permute-start.6 = (bf16[8,128,128]{2,1,0:T(8,128)(2,1)S(1)}, bf16[8,128,128]{2,1,0:T(8,128)(2,1)S(1)}, u32[]{:S(2)}, u32[]{:S(2)}) collective-permute-start(bf16[8,128,128]{2,1,0:T(8,128)(2,1)S(1)} %bitcast.30), channel_id=1, source_target_pairs={{0,32},{1,9},{4,36},{5,13},{8,40},{9,1},{12,44},{13,5},{16,48},{17... | collective-permute-start | bytes 786440 | tf_op jit(solution)/shard_map/ppermute | solution.py:43
  22.2 9.3 %collective-permute-start.5 = (bf16[8,128,128]{2,1,0:T(8,128)(2,1)S(1)}, bf16[8,128,128]{2,1,0:T(8,128)(2,1)S(1)}, u32[]{:S(2)}, u32[]{:S(2)}) collective-permute-start(bf16[8,128,128]{2,1,0:T(8,128)(2,1)S(1)} %bitcast.31), channel_id=1, source_target_pairs={{0,48},{1,13},{4,52},{5,1},{8,56},{9,5},{12,60},{13,9},{16,0},{17,... | collective-permute-start | bytes 786440 | tf_op jit(solution)/shard_map/ppermute | solution.py:43
  22.2 9.3 %collective-permute-start.4 = (bf16[8,128,128]{2,1,0:T(8,128)(2,1)S(1)}, bf16[8,128,128]{2,1,0:T(8,128)(2,1)S(1)}, u32[]{:S(2)}, u32[]{:S(2)}) collective-permute-start(bf16[8,128,128]{2,1,0:T(8,128)(2,1)S(1)} %bitcast.32), channel_id=1, source_target_pairs={{0,16},{1,5},{4,20},{5,9},{8,24},{9,13},{12,28},{13,1},{16,32},{17... | collective-permute-start | bytes 786440 | tf_op jit(solution)/shard_map/ppermute | solution.py:43
  25.4 16.0 %all-to-all-start = ((bf16[4,64,768]{2,1,0:T(8,128)(2,1)}), bf16[4,64,768]{2,1,0:T(8,128)(2,1)}, u32[]{:S(2)}, u32[]{:S(2)}) async-start(bf16[4,64,768]{2,1,0:T(8,128)(2,1)} %bitcast.23), calls=%async_computation | async-start | bytes 786432 | tf_op jit(solution)/shard_map/all_to_all | solution.py:485
  31.6 17.1 %collective-permute-start.7 = (bf16[16,2,128,128]{3,2,1,0:T(8,128)(2,1)S(1)}, bf16[16,2,128,128]{3,2,1,0:T(8,128)(2,1)}, u32[]{:S(2)}, u32[]{:S(2)}) collective-permute-start(bf16[16,2,128,128]{3,2,1,0:T(8,128)(2,1)S(1)} %bitcast.24), channel_id=1, source_target_pairs={{0,4},{1,17},{4,8},{5,21},{8,12},{9,25},{12,0},{13,29},{16,20},{17... | collective-permute-start | bytes 3145736 | tf_op jit(solution)/shard_map/ppermute | solution.py:43
  33.2 15.5 %collective-permute-start.8 = (bf16[16,2,128,128]{3,2,1,0:T(8,128)(2,1)S(1)}, bf16[16,2,128,128]{3,2,1,0:T(8,128)(2,1)}, u32[]{:S(2)}, u32[]{:S(2)}) collective-permute-start(bf16[16,2,128,128]{3,2,1,0:T(8,128)(2,1)S(1)} %bitcast.25), channel_id=1, source_target_pairs={{0,12},{1,49},{4,0},{5,53},{8,4},{9,57},{12,8},{13,61},{16,28},{17... | collective-permute-start | bytes 3145736 | tf_op jit(solution)/shard_map/ppermute | solution.py:43
  41.4 2.0 %collective-permute-start.9 = (bf16[4,64,768]{2,1,0:T(8,128)(2,1)}, bf16[4,64,768]{2,1,0:T(8,128)(2,1)S(1)}, u32[]{:S(2)}, u32[]{:S(2)}) collective-permute-start(bf16[4,64,768]{2,1,0:T(8,128)(2,1)} %all-to-all-done.refs_4_), channel_id=1, source_target_pairs={{0,1},{1,0},{2,3},{3,2},{4,5},{5,4},{6,7},{7,6},{8,9},{9,8},{10,11... | collective-permute-start | bytes 1179656 | tf_op jit(solution)/shard_map/ppermute | solution.py:32
  41.4 1.8 %collective-permute-start.10 = (bf16[2,16,768]{2,1,0:T(8,128)(2,1)S(1)}, bf16[2,16,768]{2,1,0:T(8,128)(2,1)S(1)}, u32[]{:S(2)}, u32[]{:S(2)}) collective-permute-start(bf16[2,16,768]{2,1,0:T(8,128)(2,1)S(1)} %pad_maximum_fusion.2), channel_id=1, source_target_pairs={{0,1},{1,0},{2,3},{3,2},{4,5},{5,4},{6,7},{7,6},{8,9},{9,8},{10,11... | collective-permute-start | bytes 147464 | tf_op jit(solution)/shard_map/ppermute | solution.py:32
  48.7 16.4 %collective-permute-start.11 = (bf16[16,2,128,128]{3,2,1,0:T(8,128)(2,1)S(1)}, bf16[16,2,128,128]{3,2,1,0:T(8,128)(2,1)S(1)}, u32[]{:S(2)}, u32[]{:S(2)}) collective-permute-start(bf16[16,2,128,128]{3,2,1,0:T(8,128)(2,1)S(1)} %bitcast.27), channel_id=1, source_target_pairs={{0,8},{1,33},{4,12},{5,37},{8,0},{9,41},{12,4},{13,45},{16,24},{17... | collective-permute-start | bytes 3145736 | tf_op jit(solution)/shard_map/ppermute | solution.py:43
  158.9 2.1 %collective-permute-start.12 = (bf16[4,576,128]{2,1,0:T(8,128)(2,1)S(1)}, bf16[4,576,128]{2,1,0:T(8,128)(2,1)S(1)}, u32[]{:S(2)}, u32[]{:S(2)}) collective-permute-start(bf16[4,576,128]{2,1,0:T(8,128)(2,1)S(1)} %get-tuple-element.68), channel_id=1, source_target_pairs={{0,1},{1,0},{2,3},{3,2},{4,5},{5,4},{6,7},{7,6},{8,9},{9,8},{10,11... | collective-permute-start | bytes 1769480 | tf_op jit(solution)/shard_map/ppermute | solution.py:32
  162.7 8.6 %collective-permute-start.13 = (bf16[64,768]{1,0:T(8,128)(2,1)S(1)}, bf16[64,768]{1,0:T(8,128)(2,1)S(1)}, u32[]{:S(2)}, u32[]{:S(2)}) collective-permute-start(bf16[64,768]{1,0:T(8,128)(2,1)S(1)} %get-tuple-element.70), channel_id=1, source_target_pairs={{0,64},{64,128},{128,192},{192,0},{1,65},{65,129},{129,193},{193,1... | collective-permute-start | bytes 294920 | tf_op jit(solution)/shard_map/ppermute | solution.py:28
  165.0 9.3 %collective-permute-start.14 = (bf16[64,768]{1,0:T(8,128)(2,1)S(1)}, bf16[64,768]{1,0:T(8,128)(2,1)S(1)}, u32[]{:S(2)}, u32[]{:S(2)}) collective-permute-start(bf16[64,768]{1,0:T(8,128)(2,1)S(1)} %get-tuple-element.71), channel_id=1, source_target_pairs={{0,128},{64,192},{128,0},{192,64},{1,129},{65,193},{129,1},{193,65... | collective-permute-start | bytes 294920 | tf_op jit(solution)/shard_map/ppermute | solution.py:28
  168.4 6.0 %collective-permute-start.15 = (bf16[64,768]{1,0:T(8,128)(2,1)S(1)}, bf16[64,768]{1,0:T(8,128)(2,1)S(1)}, u32[]{:S(2)}, u32[]{:S(2)}) collective-permute-start(bf16[64,768]{1,0:T(8,128)(2,1)S(1)} %get-tuple-element.72), channel_id=1, source_target_pairs={{0,192},{64,0},{128,64},{192,128},{1,193},{65,1},{129,65},{193,129... | collective-permute-start | bytes 294920 | tf_op jit(solution)/shard_map/ppermute | solution.py:28
